TPU v7x, 32 devices: a whole 2x2x4 slice. The times are simulated.
32 devices in a mesh: basis: 16 (over z, y, x), angle: 1, pol: 2 (over core).
Axes of the slice: x: 2, y: 2, z: 4, core: 2. Of those that a mesh axis runs over, the one named last changes fastest.
Arguments:
- adjoint: float32 [2, 16, 128, 2, 128], P('pol', 'angle', 'basis'), may hold values from -6 to 6
- currents: float32 [2, 16, 128, 2, 128], P('pol', 'angle', 'basis'), may hold values from -6 to 6
- radiation: float32 [2, 16, 128, 2, 128], P('pol', 'angle', 'basis'), may hold values from -6 to 6
- near_blocks: bfloat16 [128, 6, 2, 128, 128], P('basis'), may hold values from -0.15625 to 0.15625
- inverse_blocks: bfloat16 [128, 2, 128, 128], P('basis'), may hold values from -0.375 to 0.375
- col_device: int32 [128, 6], P('basis'), may hold values from 0 to 15, all different within a row; in each aligned block of 8 rows (0 to 7, 8 to 15, ...) at most 6 rows name the same one
- col_offset: int32 [128, 6], P('basis'), may hold values from 0 to 7
- box_of_block: int32 [128], P('basis'), may hold values from 0 to 63
- pair_rate: float32 [128, 6], P('basis'), may hold values from -4 to 4
Outputs:
- updated: float32 [2, 16, 128, 2, 128], P('pol', 'angle', 'basis')
- shape_grad: float32 [64], P('basis')
Inputs may be any that keep to these rules, and one draw needn't show every extreme that they name: `col_device`: each row names 6 different devices; the rows of one basis device name any device at most 6 times, and in some devices' rows one device exactly 6 times.
All inputs are finite; a program needn't handle non-finite values.
Results may differ from a plain program's by a relative error of at most 0.0033.
Values sent between devices are 32-bit elements; how exact they have to be, the bound alone decides.
No kernel may reach another device: no remote copies, remote signals or barrier semaphores. Data moves between devices by JAX's collectives and lax.ppermute only.
A program may use at most 64 MiB of HBM per device.

v0:
```python
import math

import jax
import jax.numpy as jnp
from jax import lax
from jax.sharding import PartitionSpec as P

BOX_DEV = 4


def conjugate_pairs(matrices, vectors):
    products = jnp.einsum(
        "rjcnm,radn->rjcdam", matrices, vectors, preferred_element_type=jnp.float32
    )
    real_part = products[:, :, 0, 0] + products[:, :, 1, 1]
    imag_part = products[:, :, 0, 1] - products[:, :, 1, 0]
    return jnp.stack([real_part, imag_part], axis=3)


def on_device(
    adjoint,
    currents,
    radiation,
    near_blocks,
    inverse_blocks,
    col_device,
    col_offset,
    box_of_block,
    pair_rate,
):
    highest = lax.Precision.HIGHEST
    angles_here = adjoint.shape[1]
    blocks = adjoint.shape[2]
    unknowns = adjoint.shape[4]
    near_count = near_blocks.shape[1]
    pairs = blocks * near_count
    record = angles_here * 2 * unknowns
    basis_count = lax.axis_size("basis")
    angles_all = angles_here * lax.axis_size("angle")
    rad_real = radiation[0, :, :, 0, :]
    rad_imag = radiation[0, :, :, 1, :]
    cur_real = currents[0, :, :, 0, :]
    cur_imag = currents[0, :, :, 1, :]
    part_real = jnp.sum(rad_real * cur_real - rad_imag * cur_imag, axis=(1, 2))
    part_imag = jnp.sum(rad_real * cur_imag + rad_imag * cur_real, axis=(1, 2))
    far_real, far_imag = lax.psum((part_real, part_imag), "basis")
    norm_far = 1.0 / math.sqrt(blocks * basis_count * unknowns)
    far_real = (far_real * norm_far)[:, None, None]
    far_imag = (far_imag * norm_far)[:, None, None]
    source = jnp.stack(
        [far_real * rad_real + far_imag * rad_imag, far_imag * rad_real - far_real * rad_imag],
        axis=2,
    )
    rounded = adjoint[0].astype(jnp.bfloat16)
    vectors = jnp.transpose(rounded, (1, 0, 2, 3))
    terms = conjugate_pairs(near_blocks, vectors)
    flat_terms = terms.reshape(pairs, record)
    target = col_device.reshape(pairs)
    offset_flat = col_offset.reshape(pairs)
    rate_flat = pair_rate.reshape(pairs)
    box_pairs = jnp.repeat(box_of_block, near_count)
    cur_rows = jnp.transpose(currents[0], (1, 0, 2, 3)).reshape(blocks, record)
    box_range = lax.iota(jnp.int32, BOX_DEV * basis_count)
    global_col = target * blocks + offset_flat
    rows_here = lax.iota(jnp.int32, blocks * lax.axis_size("basis"))
    chosen = (rows_here[:, None] == global_col[None, :]).astype(jnp.float32)
    received = lax.psum_scatter(
        jnp.dot(chosen, flat_terms, precision=highest, preferred_element_type=jnp.float32),
        "basis",
        scatter_dimension=0,
        tiled=True,
    )
    every_row = lax.all_gather(cur_rows, "basis", axis=0, tiled=True)
    beside = jnp.take(every_row, global_col, axis=0)
    values = rate_flat * jnp.sum(flat_terms * beside, axis=1)
    box_table = (box_pairs[:, None] == box_range[None, :]).astype(jnp.float32)
    partial_grad = jnp.dot(values, box_table, precision=highest, preferred_element_type=jnp.float32)
    total_grad = lax.psum(partial_grad, ("basis", "angle", "pol"))
    share = lax.dynamic_slice_in_dim(total_grad, lax.axis_index("basis") * BOX_DEV, BOX_DEV)
    shape_grad = share * (-1.0 / math.sqrt(4 * unknowns * angles_all * near_count))
    column_sums = jnp.transpose(received.reshape(blocks, angles_here, 2, unknowns), (1, 0, 2, 3))
    residual = (source - column_sums).astype(jnp.bfloat16)
    res_rows = jnp.transpose(residual, (1, 0, 2, 3))
    update = conjugate_pairs(inverse_blocks[:, None], res_rows)[:, 0]
    updated = adjoint[0] + jnp.transpose(update, (1, 0, 2, 3))
    return (updated[None], shape_grad)


def solution(mesh):
    placed = (
        P("pol", "angle", "basis", None, None),
        P("pol", "angle", "basis", None, None),
        P("pol", "angle", "basis", None, None),
        P("basis", None, None, None, None),
        P("basis", None, None, None),
        P("basis", None),
        P("basis", None),
        P("basis"),
        P("basis", None),
    )
    return jax.shard_map(
        on_device,
        mesh=mesh,
        in_specs=placed,
        out_specs=(P("pol", "angle", "basis", None, None), P("basis")),
        check_vma=False,
    )
```

profile of v0, /device:TPU:0, one launch (start us, length us, event | category | flops | bytes accessed | tf_op | source)
XLA Modules:
  0.0 166.6 jit_solution(2603051303724578474)
XLA Ops:
  7.2 0.0 all-gather.2.cloned.1.call-start
  7.2 1.7 %copy.40 = f32[8,16,2,128]{3,0,2,1:T(8,128)} copy(f32[8,16,2,128]{3,2,0,1:T(2,128)} %bitcast.102) | data formatting | bytes 262144 | tf_op jit(solution)/shard_map/transpose | solution.py:62
  9.0 0.0 reduce-scatter.2.cloned.1.call-start
  9.0 0.7 compare_and_fusion
  9.7 0.1 add.104
  9.8 1.4 fusion.2
  11.3 0.1 fusion.6
  11.4 0.1 pad_maximum_fusion
  11.4 1.5 copy.35
  13.0 2.6 %reshape.232 = f32[48,4096]{1,0:T(8,128)} reshape(f32[8,6,16,2,128]{4,3,2,1,0:T(2,128)} %copy.35) | data formatting | bytes 1572864 | tf_op jit(solution)/shard_map/reshape | solution.py:57
  15.6 3.5 %fusion.19 = f32[128,4096]{1,0:T(8,128)} fusion(f32[48,4096]{1,0:T(8,128)} %reshape.232, s32[48]{0:T(128)S(1)} %add.104), kind=kOutput, calls=%fused_computation.36 | convolution fusion | flops 301996032 | bytes 2883776 | tf_op jit(solution)/shard_map/dot_general | solution.py:68
  19.1 0.1 add.112
  19.2 0.1 reshape.234
  19.3 0.1 broadcast_in_dim.28
  19.3 0.1 eq.31
  19.4 0.1 broadcast_in_dim.25
  19.5 0.1 fusion.23
  19.6 0.1 fusion.24
  19.8 0.2 subtract_reduce_fusion
  20.0 43.9 %all-reduce = (f32[16]{0:T(128)S(1)}, f32[16]{0:T(128)S(1)}) all-reduce(f32[16]{0:T(128)S(1)} %get-tuple-element.7, f32[16]{0:T(128)S(1)} %get-tuple-element.6), channel_id=1, replica_groups=mesh['basis'=16,'angle'=1,'pol'=2] {'basis'}, use_global_device_ids=true, to_apply=%region_3.0 | all-reduce | flops 32 | bytes 256 | tf_op jit(solution)/shard_map/psum | solution.py:46
  63.9 0.1 multiply_add_fusion
  64.0 11.0 %all-gather.2.cloned.1.call-done = f32[128,4096]{1,0:T(8,128)} async-done(((f32[8,4096]{1,0:T(8,128)}), f32[128,4096]{1,0:T(8,128)}) %all-gather.2.cloned.1.call-update) | async-done | bytes 2097168 | tf_op jit(solution)/shard_map/all_gather | solution.py:73
  75.0 3.6 %gather_fusion = f32[48,4096]{1,0:T(8,128)} fusion(f32[128,4096]{1,0:T(8,128)} %all-gather.2.cloned.1.call-done, s32[1024]{0:T(1024)S(1)} %pad_clamp_fusion), kind=kCustom, calls=%fused_computation | custom fusion | bytes 1573056 | tf_op jit(solution)/shard_map/jit(_take)/gather | solution.py:74
  78.6 1.7 multiply_reduce_fusion
  80.2 0.2 convolution_bitcast_fusion.1
  80.4 40.8 %psum.23 = f32[64]{0:T(128)S(1)} all-reduce(f32[64]{0:T(128)S(1)} %convolution_bitcast_fusion.1), channel_id=1, replica_groups=mesh['basis'=16,'angle'=1,'pol'=2] {'basis','angle','pol'}, use_global_device_ids=true, to_apply=%region_6.7 | all-reduce | flops 64 | bytes 512 | tf_op jit(solution)/shard_map/psum | solution.py:78
  121.2 0.6 dynamic-slice_multiply_fusion
  121.8 35.0 %reduce-scatter.2.cloned.1.call-done = f32[8,4096]{1,0:T(8,128)} async-done(((f32[128,4096]{1,0:T(8,128)}), f32[8,4096]{1,0:T(8,128)}) %reduce-scatter.2.cloned.1.call-update) | async-done | bytes 131088 | tf_op jit(solution)/shard_map/reduce_scatter | solution.py:67
  156.8 0.9 fusion.13
  157.7 1.2 convolution_bitcast_fusion
  159.0 0.1 fusion.11
  159.0 0.8 copy.41
  (20 shorter events, 0.1 us)
Async XLA Ops:
  7.2 2.7 %copy-start = (bf16[8,6,2,128,128]{4,3,2,1,0:T(8,128)(2,1)S(1)}, bf16[8,6,2,128,128]{4,3,2,1,0:T(8,128)(2,1)}, u32[]{:S(2)}) copy-start(bf16[8,6,2,128,128]{4,3,2,1,0:T(8,128)(2,1)} %param.12) | copy-start | bytes 9437188
  7.2 67.8 %all-gather.2.cloned.1.call-start = ((), (), s32[]{:S(2)}) async-start(), calls=%async_computation.2 | async-start | bytes 2228224 | tf_op jit(solution)/shard_map/all_gather | solution.py:73
  9.0 147.8 %reduce-scatter.2.cloned.1.call-start = ((), (), s32[]{:S(2)}) async-start(), calls=%async_computation.1 | async-start | bytes 2228224 | tf_op jit(solution)/shard_map/reduce_scatter | solution.py:67
  15.6 3.6 %copy-start.4 = (f32[8,6]{1,0:T(8,128)S(1)}, f32[8,6]{1,0:T(8,128)}, u32[]{:S(2)}) copy-start(f32[8,6]{1,0:T(8,128)} %param.17) | copy-start | bytes 580
  15.6 3.7 %copy-start.5 = (s32[8]{0:T(128)S(1)}, s32[8]{0:T(128)}, u32[]{:S(2)}) copy-start(s32[8]{0:T(128)} %param.16) | copy-start | bytes 100
  15.6 3.9 %copy-start.1 = (f32[1,16,8,2,128]{4,3,2,1,0:T(2,128)S(1)}, f32[1,16,8,2,128]{4,3,2,1,0:T(2,128)}, u32[]{:S(2)}) copy-start(f32[1,16,8,2,128]{4,3,2,1,0:T(2,128)} %param.10) | copy-start | bytes 393220
  15.6 4.0 %copy-start.3 = (f32[1,16,8,2,128]{4,3,2,1,0:T(2,128)S(1)}, f32[1,16,8,2,128]{4,3,2,1,0:T(2,128)}, u32[]{:S(2)}) copy-start(f32[1,16,8,2,128]{4,3,2,1,0:T(2,128)} %param.11) | copy-start | bytes 393220
  78.6 80.4 %copy-start.2 = (f32[1,16,8,2,128]{4,3,2,1,0:T(2,128)S(1)}, f32[1,16,8,2,128]{4,3,2,1,0:T(2,128)}, u32[]{:S(2)}) copy-start(f32[1,16,8,2,128]{4,3,2,1,0:T(2,128)} %param.9) | copy-start | bytes 393220
Sparse Core Ops, SparseCore 0:
  11.4 63.5 all-gather.1
  77.2 79.4 reduce-scatter.1
where the time goes:
time: 167 us
  blocking collectives  84.7 us (51%)
  waiting for transfers between devices  46 us (28%)
  between operations  14.2 us (9%)
  local copies, waits for them, and re-layouts  11 us (7%)
  matrix products  6.34 us (4%)
  other arithmetic  4.44 us (3%)
    psum x1, blocking collectives, on_device(): far_real, far_imag = lax.psum((part_real, part_imag), 'basis')  43.9 us
    psum x1, blocking collectives, on_device(): total_grad = lax.psum(partial_grad, ('basis', 'angle', 'pol'))  40.8 us
    reduce_scatter x1, waiting for transfers between devices, on_device(): lax.psum_scatter(jnp.dot(chosen, flat_terms, precision=highest, preferred...  35 us
    all_gather x1, waiting for transfers between devices, on_device(): every_row = lax.all_gather(cur_rows, 'basis', axis=0, tiled=True)  11 us
    gather x1, local copies, waits for them, and re-layouts, on_device(): beside = jnp.take(every_row, global_col, axis=0)  3.63 us
    dot_general x1, matrix products, on_device(): jnp.dot(chosen, flat_terms, precision=highest, preferred_element_type=jnp...  3.46 us
  transfers between devices with their start and end apart: 2, of which 2 were waited for; matrix products, arithmetic and copies ran while one was open for 10% of the time, Pallas kernels for 0%

commit v1 on v0

v1 whole, which is shorter than its diff:
```python
import functools
import math

import jax
import jax.numpy as jnp
from jax import lax
from jax.experimental import pallas as pl
from jax.experimental.pallas import tpu as pltpu
from jax.sharding import PartitionSpec as P

LOW = 4
LANES = 128
BOX_DEV = 4
VMEM_LIMIT = 48 * 1024 * 1024


def complex_rows(real, imag):
    return jnp.concatenate(
        [jnp.concatenate([real, imag], axis=1), jnp.concatenate([imag, -real], axis=1)], axis=0
    )


def fill_kernel(
    angles,
    slots,
    col_device_ref,
    col_offset_ref,
    box_ref,
    rate_ref,
    adjoint_ref,
    currents_ref,
    radiation_ref,
    near_ref,
    *out_refs,
):
    message_refs, current_rows_ref = out_refs[:LOW], out_refs[LOW]
    blocks, near_count = col_device_ref.shape
    stride = 2 * blocks
    me = lax.axis_index("basis")
    my_low = lax.rem(me, LOW)
    my_high = lax.div(me, LOW)
    for row in range(blocks):
        for part in range(2):
            current_rows_ref[row, pl.ds(part * angles, angles), :] = currents_ref[
                pl.ds(2 * row + part, angles, stride=stride), :
            ]
    count = angles * blocks
    rad_real = radiation_ref[pl.ds(0, count, stride=2), :]
    rad_imag = radiation_ref[pl.ds(1, count, stride=2), :]
    cur_real = currents_ref[pl.ds(0, count, stride=2), :]
    cur_imag = currents_ref[pl.ds(1, count, stride=2), :]
    far_real = jnp.sum((rad_real * cur_real - rad_imag * cur_imag).reshape(angles, blocks, LANES), axis=1)
    far_imag = jnp.sum((rad_real * cur_imag + rad_imag * cur_real).reshape(angles, blocks, LANES), axis=1)
    lane = lax.broadcasted_iota(jnp.int32, (angles, LANES), 1)
    far = jnp.where(lane == 0, jnp.sum(far_real, axis=1, keepdims=True), 0.0) + jnp.where(
        lane == 1, jnp.sum(far_imag, axis=1, keepdims=True), 0.0
    )
    spread = LANES // LOW
    lane8 = lax.broadcasted_iota(jnp.int32, (8, LANES), 1)
    sub8 = lax.broadcasted_iota(jnp.int32, (8, LANES), 0)
    table = jnp.zeros((8, LANES), jnp.float32)
    counts = [jnp.int32(0)] * LOW
    for row in range(blocks):
        real = adjoint_ref[pl.ds(2 * row, angles, stride=stride), :].astype(jnp.bfloat16)
        imag = adjoint_ref[pl.ds(2 * row + 1, angles, stride=stride), :].astype(jnp.bfloat16)
        left = complex_rows(real, imag)
        box = box_ref[row].astype(jnp.float32)
        for k in range(near_count):
            term = jnp.dot(left, near_ref[row * near_count + k], preferred_element_type=jnp.float32)
            device = col_device_ref[row, k]
            low = lax.bitwise_xor(lax.rem(device, LOW), my_low)
            high = lax.bitwise_xor(lax.div(device, LOW), my_high)
            place = high * blocks + col_offset_ref[row, k] + 1
            own_slot = jnp.int32(0)
            for e in range(LOW):
                here = low == e
                slot = jnp.where(here, jnp.minimum(counts[e], slots), slots)
                own_slot = jnp.where(here, counts[e], own_slot)
                counts[e] = counts[e] + here.astype(jnp.int32)
                message_refs[e][slot] = term
            entry = jnp.where(
                sub8 == 0, place.astype(jnp.float32), jnp.where(sub8 == 1, rate_ref[row, k], box)
            )
            table = jnp.where(lane8 == low * spread + own_slot, entry, table)
    for e in range(LOW):
        message_refs[e][slots, pl.ds(0, angles), :] = far
        message_refs[e][slots, pl.ds(angles, 8), :] = jnp.where(lane8 // spread == e, table, 0.0)


def sum_kernel(angles, slots, high_count, *refs):
    message_refs = refs[:LOW]
    current_refs = refs[LOW : LOW + high_count]
    out_refs = refs[LOW + high_count : LOW + 2 * high_count]
    grad_ref, acc_ref, cur_ref, prod_ref, table_ref, place_ref, sem = refs[LOW + 2 * high_count :]
    blocks = current_refs[0].shape[0]
    spread = LANES // LOW
    table = message_refs[0][slots, pl.ds(angles, 8), :]
    far = message_refs[0][slots, pl.ds(0, angles), :]
    for e in range(1, LOW):
        table = table + message_refs[e][slots, pl.ds(angles, 8), :]
        far = far + message_refs[e][slots, pl.ds(0, angles), :]
    table_ref[...] = table.astype(jnp.int32)
    copy = pltpu.make_async_copy(table_ref, place_ref, sem)
    copy.start()
    for d in range(high_count):
        cur_ref[pl.ds(d * blocks, blocks)] = current_refs[d][...]
    acc_ref[...] = jnp.zeros(acc_ref.shape, jnp.float32)
    prod_ref[...] = jnp.zeros(prod_ref.shape, jnp.float32)
    copy.wait()
    for e in range(LOW):
        for s in range(slots):
            place = place_ref[0, e * spread + s]
            used = place > 0
            at = jnp.maximum(place - 1, 0)
            term = jnp.where(used, message_refs[e][s], 0.0)
            acc_ref[at] = acc_ref[at] + term
            both = term * cur_ref[at]
            prod_ref[e * spread + s] = jnp.sum(both.reshape(2 * angles // 8, 8, LANES), axis=0)
    for d in range(high_count):
        for b in range(blocks):
            out_refs[d][pl.ds(b * 2 * angles, 2 * angles), :] = acc_ref[d * blocks + b]
        out_refs[d][pl.ds(blocks * 2 * angles, angles), :] = far
    highest = lax.Precision.HIGHEST
    contract_last = (((1,), (1,)), ((), ()))
    by_slot = jnp.sum(prod_ref[...], axis=1)
    values = lax.dot_general(
        jnp.ones((8, LANES), jnp.float32),
        by_slot,
        contract_last,
        precision=highest,
        preferred_element_type=jnp.float32,
    )
    boxes = grad_ref.shape[1]
    number = lax.broadcasted_iota(jnp.int32, (boxes, LANES), 0).astype(jnp.float32)
    rates = jnp.where(number == table[2:3, :], table[1:2, :], 0.0)
    grad_ref[...] = lax.dot_general(
        values, rates, contract_last, precision=highest, preferred_element_type=jnp.float32
    )


def update_kernel(angles, norm_far, high_count, *refs):
    sum_refs = refs[:high_count]
    adjoint_ref, radiation_ref, inverse_ref, out_ref = refs[high_count:]
    blocks = inverse_ref.shape[0]
    stride = 2 * blocks
    record = 2 * angles
    far = sum_refs[0][pl.ds(blocks * record, angles), :]
    for d in range(1, high_count):
        far = far + sum_refs[d][pl.ds(blocks * record, angles), :]
    far = far * norm_far
    far_real = jnp.broadcast_to(far[:, 0:1], (angles, LANES))
    far_imag = jnp.broadcast_to(far[:, 1:2], (angles, LANES))
    for block in range(blocks):
        rows_real = pl.ds(2 * block, angles, stride=stride)
        rows_imag = pl.ds(2 * block + 1, angles, stride=stride)
        total = sum_refs[0][pl.ds(block * record, record), :]
        for d in range(1, high_count):
            total = total + sum_refs[d][pl.ds(block * record, record), :]
        rad_real, rad_imag = radiation_ref[rows_real, :], radiation_ref[rows_imag, :]
        real = (far_real * rad_real + far_imag * rad_imag - total[:angles]).astype(jnp.bfloat16)
        imag = (far_imag * rad_real - far_real * rad_imag - total[angles:]).astype(jnp.bfloat16)
        step = jnp.dot(complex_rows(real, imag), inverse_ref[block], preferred_element_type=jnp.float32)
        out_ref[rows_real, :] = adjoint_ref[rows_real, :] + step[:angles]
        out_ref[rows_imag, :] = adjoint_ref[rows_imag, :] + step[angles:]


def on_device(
    adjoint,
    currents,
    radiation,
    near_blocks,
    inverse_blocks,
    col_device,
    col_offset,
    box_of_block,
    pair_rate,
):
    angles, blocks, unknowns = adjoint.shape[1], adjoint.shape[2], adjoint.shape[4]
    near_count = near_blocks.shape[1]
    pairs = blocks * near_count
    record = 2 * angles
    basis_count = lax.axis_size("basis")
    high_count = basis_count // LOW
    angles_all = angles * lax.axis_size("angle")
    boxes = BOX_DEV * basis_count
    slots = 2 * pairs // basis_count * high_count
    vmem = pl.BlockSpec(memory_space=pltpu.VMEM)
    smem = pl.BlockSpec(memory_space=pltpu.SMEM)
    params = pltpu.CompilerParams(vmem_limit_bytes=VMEM_LIMIT)

    def moved(value, bits):
        return lax.ppermute(value, "basis", [(i, i ^ bits) for i in range(basis_count)])

    flat = (angles * blocks * 2, unknowns)
    adjoint_rows = adjoint.reshape(flat)
    currents_rows = currents.reshape(flat)
    radiation_rows = radiation.reshape(flat)
    near = near_blocks.reshape(pairs, 2 * unknowns, unknowns)
    inverse = inverse_blocks.reshape(blocks, 2 * unknowns, unknowns)
    message = jax.ShapeDtypeStruct((slots + 1, record, unknowns), jnp.float32)
    current_shape = jax.ShapeDtypeStruct((blocks, record, unknowns), jnp.float32)
    *messages, own_currents = pl.pallas_call(
        functools.partial(fill_kernel, angles, slots),
        out_shape=[message] * LOW + [current_shape],
        in_specs=[smem] * 4 + [vmem] * 4,
        out_specs=[vmem] * (LOW + 1),
        compiler_params=params,
        name="fill",
    )(col_device, col_offset, box_of_block, pair_rate, adjoint_rows, currents_rows, radiation_rows, near)
    arrived = [messages[0]] + [moved(messages[e], e) for e in range(1, LOW)]
    beside = [own_currents] + [moved(own_currents, d * LOW) for d in range(1, high_count)]
    partial = jax.ShapeDtypeStruct((blocks * record + angles, unknowns), jnp.float32)
    box_lanes = -(-boxes // LANES) * LANES
    *sums, grad = pl.pallas_call(
        functools.partial(sum_kernel, angles, slots, high_count),
        out_shape=[partial] * high_count + [jax.ShapeDtypeStruct((8, box_lanes), jnp.float32)],
        in_specs=[vmem] * (LOW + high_count),
        out_specs=[vmem] * (high_count + 1),
        scratch_shapes=[
            pltpu.VMEM((high_count * blocks, record, unknowns), jnp.float32),
            pltpu.VMEM((high_count * blocks, record, unknowns), jnp.float32),
            pltpu.VMEM((LANES, 8, unknowns), jnp.float32),
            pltpu.VMEM((8, LANES), jnp.int32),
            pltpu.SMEM((8, LANES), jnp.int32),
            pltpu.SemaphoreType.DMA,
        ],
        compiler_params=params,
        name="sum",
    )(*arrived, *beside)
    totals = [sums[0]] + [moved(sums[d], d * LOW) for d in range(1, high_count)]
    updated = pl.pallas_call(
        functools.partial(update_kernel, angles, 1.0 / math.sqrt(blocks * basis_count * unknowns), high_count),
        out_shape=jax.ShapeDtypeStruct(flat, jnp.float32),
        in_specs=[vmem] * (high_count + 3),
        out_specs=vmem,
        compiler_params=params,
        name="update",
    )(*totals, adjoint_rows, radiation_rows, inverse)
    for bits in (range(1, LOW), range(LOW, basis_count, LOW)):
        grad = functools.reduce(jnp.add, [moved(grad, b) for b in bits], grad)
    for axis in ("angle", "pol"):
        size = lax.axis_size(axis)
        grad = functools.reduce(
            jnp.add,
            [lax.ppermute(grad, axis, [(i, i ^ b) for i in range(size)]) for b in range(1, size)],
            grad,
        )
    share = lax.dynamic_slice_in_dim(grad[0], lax.axis_index("basis") * BOX_DEV, BOX_DEV)
    shape_grad = share * (-1.0 / math.sqrt(4 * unknowns * angles_all * near_count))
    return (updated.reshape(adjoint.shape), shape_grad)


def solution(mesh):
    placed = (
        P("pol", "angle", "basis", None, None),
        P("pol", "angle", "basis", None, None),
        P("pol", "angle", "basis", None, None),
        P("basis", None, None, None, None),
        P("basis", None, None, None),
        P("basis", None),
        P("basis", None),
        P("basis"),
        P("basis", None),
    )
    return jax.shard_map(
        on_device,
        mesh=mesh,
        in_specs=placed,
        out_specs=(P("pol", "angle", "basis", None, None), P("basis")),
        check_vma=False,
    )
```

time: 167 us -> 58.4 us (0.35)
  blocking collectives: 84.7 us -> 0 us
  waiting for transfers between devices: 46 us -> 19.2 us
  starting transfers between devices: 0.08 us -> 25.6 us
  between operations: 14.2 us -> 0.7 us
  matrix products: 6.34 us -> 0 us
  Pallas kernels: 0 us -> 4.65 us
  other arithmetic: 4.44 us -> 0.6 us
  local copies, waits for them, and re-layouts: 11 us -> 7.32 us
    psum x2 -> x0, blocking collectives: 84.7 us -> none  [the longest x1 43.9 us: on_device(): far_real, far_imag = lax.psum((part_real, part_imag), 'basis')]
    reduce_scatter x1 -> x0, waiting for transfers between devices: 35 us -> none  [on_device(): lax.psum_scatter(jnp.dot(chosen, flat_terms, precision=highest, preferred...]
    ppermute x0 -> x16, starting transfers between devices: none -> 25.6 us  [the longest x15 25.6 us: moved(): lax.ppermute(value, 'basis', [(i, i ^ bits) for i in range(basis_count)])]
    ppermute x0 -> x16, waiting for transfers between devices: none -> 19.2 us  [the longest x15 18.1 us: moved(): lax.ppermute(value, 'basis', [(i, i ^ bits) for i in range(basis_count)])]
    all_gather x1 -> x0, waiting for transfers between devices: 11 us -> none  [on_device(): every_row = lax.all_gather(cur_rows, 'basis', axis=0, tiled=True)]
    unnamed x13 -> x22, local copies, waits for them, and re-layouts: 0.79 us -> 7.32 us
    dot_general x4 -> x0, matrix products: 6.34 us -> none  [the longest x1 3.46 us: on_device(): jnp.dot(chosen, flat_terms, precision=highest, preferred_element_type=jnp...]
    pallas_call x0 -> x3, Pallas kernels: none -> 4.65 us  [the longest x1 1.84 us: on_device(): pl.pallas_call(functools.partial(sum_kernel, angles, slots, high_count),...]
  transfers between devices with their start and end apart: 2 -> 16, of which waited for: 2 -> 9; matrix products, arithmetic and copies ran while one was open for 10% -> 1% of each run, Pallas kernels for 0% -> 0%
where the time goes in v1:
time: 58.4 us; the launch traced here: 58.1 us
  starting transfers between devices  25.6 us (44%)
  waiting for transfers between devices  19.2 us (33%)
  local copies, waits for them, and re-layouts  7.32 us (13%)
  Pallas kernels  4.65 us (8%)
  between operations  0.7 us (1%)
  other arithmetic  0.6 us (1%)
    ppermute x15, starting transfers between devices, moved(): lax.ppermute(value, 'basis', [(i, i ^ bits) for i in range(basis_count)])  25.6 us
    ppermute x15, waiting for transfers between devices, moved(): lax.ppermute(value, 'basis', [(i, i ^ bits) for i in range(basis_count)])  18.1 us
    unnamed x22, local copies, waits for them, and re-layouts  7.32 us
    pallas_call x1, Pallas kernels, on_device(): pl.pallas_call(functools.partial(sum_kernel, angles, slots, high_count),...  1.84 us
    pallas_call x1, Pallas kernels, on_device(): pl.pallas_call(functools.partial(fill_kernel, angles, slots), out_shape=[...  1.84 us
  transfers between devices with their start and end apart: 16, of which 9 were waited for; matrix products, arithmetic and copies ran while one was open for 1% of the time, Pallas kernels for 0%

profile of v1, /device:TPU:0, one launch (start us, length us, event | category | flops | bytes accessed | tf_op | source)
XLA Modules:
  0.0 58.1 jit_solution(371658261918090617)
XLA Ops:
  0.6 1.9 %copy-done = bf16[8,6,2,128,128]{4,3,2,1,0:T(8,128)(2,1)S(1)} copy-done((bf16[8,6,2,128,128]{4,3,2,1,0:T(8,128)(2,1)S(1)}, bf16[8,6,2,128,128]{4,3,2,1,0:T(8,128)(2,1)}, u32[]{:S(2)}) %copy-start) | copy-done | bytes 3145752
  2.5 0.9 %copy-done.2 = f32[1,16,8,2,128]{4,3,2,1,0:T(2,128)S(1)} copy-done((f32[1,16,8,2,128]{4,3,2,1,0:T(2,128)S(1)}, f32[1,16,8,2,128]{4,3,2,1,0:T(2,128)}, u32[]{:S(2)}) %copy-start.2) | copy-done | bytes 131096
  3.4 0.9 %copy-done.4 = f32[1,16,8,2,128]{4,3,2,1,0:T(2,128)S(1)} copy-done((f32[1,16,8,2,128]{4,3,2,1,0:T(2,128)S(1)}, f32[1,16,8,2,128]{4,3,2,1,0:T(2,128)}, u32[]{:S(2)}) %copy-start.4) | copy-done | bytes 131096
  4.3 0.9 %copy-done.6 = f32[1,16,8,2,128]{4,3,2,1,0:T(2,128)S(1)} copy-done((f32[1,16,8,2,128]{4,3,2,1,0:T(2,128)S(1)}, f32[1,16,8,2,128]{4,3,2,1,0:T(2,128)}, u32[]{:S(2)}) %copy-start.6) | copy-done | bytes 131096
  5.2 0.7 %copy-done.7 = s32[8,6]{1,0:T(8,128)S(1)} copy-done((s32[8,6]{1,0:T(8,128)S(1)}, s32[8,6]{1,0:T(8,128)}, u32[]{:S(2)}) %copy-start.7) | copy-done | bytes 216
  5.9 0.7 %copy-done.8 = s32[8,6]{1,0:T(8,128)S(1)} copy-done((s32[8,6]{1,0:T(8,128)S(1)}, s32[8,6]{1,0:T(8,128)}, u32[]{:S(2)}) %copy-start.8) | copy-done | bytes 216
  6.6 0.7 %copy-done.9 = f32[8,6]{1,0:T(8,128)S(1)} copy-done((f32[8,6]{1,0:T(8,128)S(1)}, f32[8,6]{1,0:T(8,128)}, u32[]{:S(2)}) %copy-start.9) | copy-done | bytes 216
  7.3 0.7 %copy-done.10 = s32[8]{0:T(128)S(1)} copy-done((s32[8]{0:T(128)S(1)}, s32[8]{0:T(128)}, u32[]{:S(2)}) %copy-start.10) | copy-done | bytes 56
  8.0 1.8 %fill.1 = (f32[25,32,128]{2,1,0:T(8,128)S(1)}, f32[25,32,128]{2,1,0:T(8,128)S(1)}, f32[25,32,128]{2,1,0:T(8,128)S(1)}, f32[25,32,128]{2,1,0:T(8,128)S(1)}, f32[8,32,128]{2,1,0:T(8,128)S(1)}) custom-call(s32[8,6]{1,0:T(8,128)S(1)} %copy-done.7, s32[8,6]{1,0:T(8,128)S(1)} %copy-done.8, s32[8]{0:T(128)S(1)} %copy-done.10, f32[8,6]{1,0:T(8,128)S(1)} %copy-done.9, ...), custom_call_target="tpu_custom_call" | custom-call | tf_op jit(solution)/shard_map/fill/pallas_call | solution.py:202
  9.8 3.0 %collective-permute-start = (f32[25,32,128]{2,1,0:T(8,128)S(1)}, f32[25,32,128]{2,1,0:T(8,128)S(1)}, u32[]{:S(2)}, u32[]{:S(2)}) collective-permute-start(f32[25,32,128]{2,1,0:T(8,128)S(1)} %get-tuple-element.13), channel_id=1, source_target_pairs={{0,2},{2,0},{4,6},{6,4},{8,10},{10,8},{12,14},{14,12},{16,18},{18,... | collective-permute-start | bytes 1228808 | tf_op jit(solution)/shard_map/ppermute | solution.py:192
  12.8 1.5 %collective-permute-start.1 = (f32[25,32,128]{2,1,0:T(8,128)S(1)}, f32[25,32,128]{2,1,0:T(8,128)S(1)}, u32[]{:S(2)}, u32[]{:S(2)}) collective-permute-start(f32[25,32,128]{2,1,0:T(8,128)S(1)} %get-tuple-element.14), channel_id=1, source_target_pairs={{0,4},{2,6},{4,0},{6,2},{8,12},{10,14},{12,8},{14,10},{16,20},{18,... | collective-permute-start | bytes 1228808 | tf_op jit(solution)/shard_map/ppermute | solution.py:192
  14.4 2.0 %collective-permute-start.3 = (f32[8,32,128]{2,1,0:T(8,128)S(1)}, f32[8,32,128]{2,1,0:T(8,128)S(1)}, u32[]{:S(2)}, u32[]{:S(2)}) collective-permute-start(f32[8,32,128]{2,1,0:T(8,128)S(1)} %get-tuple-element.16.refs_4_), channel_id=1, source_target_pairs={{0,8},{2,10},{4,12},{6,14},{8,0},{10,2},{12,4},{14,6},{16,24},{18,... | collective-permute-start | bytes 393224 | tf_op jit(solution)/shard_map/ppermute | solution.py:192
  16.4 2.6 %collective-permute-start.4 = (f32[8,32,128]{2,1,0:T(8,128)S(1)}, f32[8,32,128]{2,1,0:T(8,128)S(1)}, u32[]{:S(2)}, u32[]{:S(2)}) collective-permute-start(f32[8,32,128]{2,1,0:T(8,128)S(1)} %get-tuple-element.16.refs_4_), channel_id=1, source_target_pairs={{0,16},{2,18},{4,20},{6,22},{8,24},{10,26},{12,28},{14,30},{16,0},... | collective-permute-start | bytes 393224 | tf_op jit(solution)/shard_map/ppermute | solution.py:192
  19.0 1.6 %collective-permute-done.3.refs_5_ = f32[8,32,128]{2,1,0:T(8,128)S(1)} collective-permute-done((f32[8,32,128]{2,1,0:T(8,128)S(1)}, f32[8,32,128]{2,1,0:T(8,128)S(1)}, u32[]{:S(2)}, u32[]{:S(2)}) %collective-permute-start.3) | collective-permute-done | bytes 131104 | tf_op jit(solution)/shard_map/ppermute | solution.py:192
  20.6 4.1 %collective-permute-start.5 = (f32[8,32,128]{2,1,0:T(8,128)S(1)}, f32[8,32,128]{2,1,0:T(8,128)S(1)}, u32[]{:S(2)}, u32[]{:S(2)}) collective-permute-start(f32[8,32,128]{2,1,0:T(8,128)S(1)} %get-tuple-element.16.refs_4_), channel_id=1, source_target_pairs={{0,24},{2,26},{4,28},{6,30},{8,16},{10,18},{12,20},{14,22},{16,8},... | collective-permute-start | bytes 393224 | tf_op jit(solution)/shard_map/ppermute | solution.py:192
  24.7 3.4 %collective-permute-done.4.refs_6_ = f32[8,32,128]{2,1,0:T(8,128)S(1)} collective-permute-done((f32[8,32,128]{2,1,0:T(8,128)S(1)}, f32[8,32,128]{2,1,0:T(8,128)S(1)}, u32[]{:S(2)}, u32[]{:S(2)}) %collective-permute-start.4) | collective-permute-done | bytes 131104 | tf_op jit(solution)/shard_map/ppermute | solution.py:192
  28.1 4.4 %collective-permute-done.1.refs_2_ = f32[25,32,128]{2,1,0:T(8,128)S(1)} collective-permute-done((f32[25,32,128]{2,1,0:T(8,128)S(1)}, f32[25,32,128]{2,1,0:T(8,128)S(1)}, u32[]{:S(2)}, u32[]{:S(2)}) %collective-permute-start.1) | collective-permute-done | bytes 409632 | tf_op jit(solution)/shard_map/ppermute | solution.py:192
  32.5 1.8 %sum.1 = (f32[272,128]{1,0:T(8,128)S(1)}, f32[272,128]{1,0:T(8,128)S(1)}, f32[272,128]{1,0:T(8,128)S(1)}, f32[272,128]{1,0:T(8,128)S(1)}, f32[8,128]{1,0:T(8,128)S(1)}) custom-call(f32[25,32,128]{2,1,0:T(8,128)S(1)} %get-tuple-element.12.refs_0_, f32[25,32,128]{2,1,0:T(8,128)S(1)} %collective-permute-done.refs_1_, ...), custom_call_target="tpu_custom_call" | custom-call | tf_op jit(solution)/shard_map/sum/pallas_call | solution.py:214
  34.4 1.6 %collective-permute-start.10 = (f32[8,128]{1,0:T(8,128)S(1)}, f32[8,128]{1,0:T(8,128)S(1)}, u32[]{:S(2)}, u32[]{:S(2)}) collective-permute-start(f32[8,128]{1,0:T(8,128)S(1)} %get-tuple-element.21), channel_id=1, source_target_pairs={{0,4},{2,6},{4,0},{6,2},{8,12},{10,14},{12,8},{14,10},{16,20},{18,... | collective-permute-start | bytes 12296 | tf_op jit(solution)/shard_map/ppermute | solution.py:192
  36.0 1.1 %collective-permute-start.11 = (f32[8,128]{1,0:T(8,128)S(1)}, f32[8,128]{1,0:T(8,128)S(1)}, u32[]{:S(2)}, u32[]{:S(2)}) collective-permute-start(f32[8,128]{1,0:T(8,128)S(1)} %get-tuple-element.21), channel_id=1, source_target_pairs={{0,6},{2,4},{4,2},{6,0},{8,14},{10,12},{12,10},{14,8},{16,22},{18,... | collective-permute-start | bytes 12296 | tf_op jit(solution)/shard_map/ppermute | solution.py:192
  37.1 0.8 %collective-permute-start.9 = (f32[8,128]{1,0:T(8,128)S(1)}, f32[8,128]{1,0:T(8,128)S(1)}, u32[]{:S(2)}, u32[]{:S(2)}) collective-permute-start(f32[8,128]{1,0:T(8,128)S(1)} %get-tuple-element.21), channel_id=1, source_target_pairs={{0,2},{2,0},{4,6},{6,4},{8,10},{10,8},{12,14},{14,12},{16,18},{18,... | collective-permute-start | bytes 12296 | tf_op jit(solution)/shard_map/ppermute | solution.py:192
  38.1 2.4 %collective-permute-done.11 = f32[8,128]{1,0:T(8,128)S(1)} collective-permute-done((f32[8,128]{1,0:T(8,128)S(1)}, f32[8,128]{1,0:T(8,128)S(1)}, u32[]{:S(2)}, u32[]{:S(2)}) %collective-permute-start.11) | collective-permute-done | bytes 4128 | tf_op jit(solution)/shard_map/ppermute | solution.py:192
  40.5 0.3 collective-permute-done.9
  40.8 1.6 %collective-permute-start.12 = (f32[8,128]{1,0:T(8,128)S(1)}, f32[8,128]{1,0:T(8,128)S(1)}, u32[]{:S(2)}, u32[]{:S(2)}) collective-permute-start(f32[8,128]{1,0:T(8,128)S(1)} %add_add_fusion.1), channel_id=1, source_target_pairs={{0,8},{2,10},{4,12},{6,14},{8,0},{10,2},{12,4},{14,6},{16,24},{18,... | collective-permute-start | bytes 12296 | tf_op jit(solution)/shard_map/ppermute | solution.py:192
  42.3 2.6 %collective-permute-start.13 = (f32[8,128]{1,0:T(8,128)S(1)}, f32[8,128]{1,0:T(8,128)S(1)}, u32[]{:S(2)}, u32[]{:S(2)}) collective-permute-start(f32[8,128]{1,0:T(8,128)S(1)} %add_add_fusion.1), channel_id=1, source_target_pairs={{0,16},{2,18},{4,20},{6,22},{8,24},{10,26},{12,28},{14,30},{16,0},... | collective-permute-start | bytes 12296 | tf_op jit(solution)/shard_map/ppermute | solution.py:192
  45.1 0.7 %collective-permute-start.6 = (f32[272,128]{1,0:T(8,128)S(1)}, f32[272,128]{1,0:T(8,128)S(1)}, u32[]{:S(2)}, u32[]{:S(2)}) collective-permute-start(f32[272,128]{1,0:T(8,128)S(1)} %get-tuple-element.18), channel_id=1, source_target_pairs={{0,8},{2,10},{4,12},{6,14},{8,0},{10,2},{12,4},{14,6},{16,24},{18,... | collective-permute-start | bytes 417800 | tf_op jit(solution)/shard_map/ppermute | solution.py:192
  45.8 3.5 %collective-permute-start.7 = (f32[272,128]{1,0:T(8,128)S(1)}, f32[272,128]{1,0:T(8,128)S(1)}, u32[]{:S(2)}, u32[]{:S(2)}) collective-permute-start(f32[272,128]{1,0:T(8,128)S(1)} %get-tuple-element.19), channel_id=1, source_target_pairs={{0,16},{2,18},{4,20},{6,22},{8,24},{10,26},{12,28},{14,30},{16,0},... | collective-permute-start | bytes 417800 | tf_op jit(solution)/shard_map/ppermute | solution.py:192
  49.5 0.9 %collective-permute-done.14 = f32[8,128]{1,0:T(8,128)S(1)} collective-permute-done((f32[8,128]{1,0:T(8,128)S(1)}, f32[8,128]{1,0:T(8,128)S(1)}, u32[]{:S(2)}, u32[]{:S(2)}) %collective-permute-start.14) | collective-permute-done | bytes 4128 | tf_op jit(solution)/shard_map/ppermute | solution.py:192
  50.4 1.2 %collective-permute-done.15 = f32[8,128]{1,0:T(8,128)S(1)} collective-permute-done((f32[8,128]{1,0:T(8,128)S(1)}, f32[8,128]{1,0:T(8,128)S(1)}, u32[]{:S(2)}, u32[]{:S(2)}) %collective-permute-start.15) | collective-permute-done | bytes 4128 | tf_op jit(solution)/shard_map/ppermute | solution.py:245
  51.6 0.6 %multiply_bitcast_fusion = f32[4]{0:T(128)} fusion(f32[1,128]{1,0:T(1,128)S(1)} %slice.3, s32[]{:T(128)S(6)} %select_n.3), kind=kLoop, calls=%fused_computation.2 | loop fusion | flops 4 | bytes 36 | tf_op jit(solution)/shard_map/mul | solution.py:249
  52.2 4.9 %collective-permute-done.7.refs_2_ = f32[272,128]{1,0:T(8,128)S(1)} collective-permute-done((f32[272,128]{1,0:T(8,128)S(1)}, f32[272,128]{1,0:T(8,128)S(1)}, u32[]{:S(2)}, u32[]{:S(2)}) %collective-permute-start.7) | collective-permute-done | bytes 139296 | tf_op jit(solution)/shard_map/ppermute | solution.py:192
  57.1 1.0 %update.1 = f32[256,128]{1,0:T(8,128)} custom-call(f32[272,128]{1,0:T(8,128)S(1)} %get-tuple-element.17.refs_0_, f32[272,128]{1,0:T(8,128)S(1)} %collective-permute-done.6.refs_1_, f32[272,128]{1,0:T(8,128)S(1)} %collective-permute-done.7.refs_2_, f32[272,128]{1,0:T(8,128)S(1)} %collective-permute-done.8.refs_3_, f32[256,128]{1,0:T(8,128)S(1)} %bitcast.11, ...), custom_call_target="tpu_custom_call" | custom-call | tf_op jit(solution)/shard_map/update/pallas_call | solution.py:231
  (30 shorter events, 0.6 us)
Async XLA Ops:
  0.6 1.9 %copy-start = (bf16[8,6,2,128,128]{4,3,2,1,0:T(8,128)(2,1)S(1)}, bf16[8,6,2,128,128]{4,3,2,1,0:T(8,128)(2,1)}, u32[]{:S(2)}) copy-start(bf16[8,6,2,128,128]{4,3,2,1,0:T(8,128)(2,1)} %param.12) | copy-start | bytes 9437188
  2.5 0.9 %copy-start.2 = (f32[1,16,8,2,128]{4,3,2,1,0:T(2,128)S(1)}, f32[1,16,8,2,128]{4,3,2,1,0:T(2,128)}, u32[]{:S(2)}) copy-start(f32[1,16,8,2,128]{4,3,2,1,0:T(2,128)} %param.9) | copy-start | bytes 393220
  3.4 0.9 %copy-start.4 = (f32[1,16,8,2,128]{4,3,2,1,0:T(2,128)S(1)}, f32[1,16,8,2,128]{4,3,2,1,0:T(2,128)}, u32[]{:S(2)}) copy-start(f32[1,16,8,2,128]{4,3,2,1,0:T(2,128)} %param.11) | copy-start | bytes 393220
  4.3 0.9 %copy-start.6 = (f32[1,16,8,2,128]{4,3,2,1,0:T(2,128)S(1)}, f32[1,16,8,2,128]{4,3,2,1,0:T(2,128)}, u32[]{:S(2)}) copy-start(f32[1,16,8,2,128]{4,3,2,1,0:T(2,128)} %param.10) | copy-start | bytes 393220
  5.2 0.7 %copy-start.7 = (s32[8,6]{1,0:T(8,128)S(1)}, s32[8,6]{1,0:T(8,128)}, u32[]{:S(2)}) copy-start(s32[8,6]{1,0:T(8,128)} %col_device_ref.1) | copy-start | bytes 580
  5.9 0.7 %copy-start.8 = (s32[8,6]{1,0:T(8,128)S(1)}, s32[8,6]{1,0:T(8,128)}, u32[]{:S(2)}) copy-start(s32[8,6]{1,0:T(8,128)} %col_offset_ref.1) | copy-start | bytes 580
  6.6 0.7 %copy-start.9 = (f32[8,6]{1,0:T(8,128)S(1)}, f32[8,6]{1,0:T(8,128)}, u32[]{:S(2)}) copy-start(f32[8,6]{1,0:T(8,128)} %rate_ref.1) | copy-start | bytes 580
  7.3 0.7 %copy-start.10 = (s32[8]{0:T(128)S(1)}, s32[8]{0:T(128)}, u32[]{:S(2)}) copy-start(s32[8]{0:T(128)} %box_ref.1) | copy-start | bytes 100
  8.0 49.1 %copy-start.1 = (bf16[8,2,128,128]{3,2,1,0:T(8,128)(2,1)S(1)}, bf16[8,2,128,128]{3,2,1,0:T(8,128)(2,1)}, u32[]{:S(2)}) copy-start(bf16[8,2,128,128]{3,2,1,0:T(8,128)(2,1)} %param.13) | copy-start | bytes 1572868
  8.0 49.1 %copy-start.3 = (f32[1,16,8,2,128]{4,3,2,1,0:T(2,128)S(1)}, f32[1,16,8,2,128]{4,3,2,1,0:T(2,128)}, u32[]{:S(2)}) copy-start(f32[1,16,8,2,128]{4,3,2,1,0:T(2,128)} %param.9) | copy-start | bytes 393220
  8.0 49.1 %copy-start.5 = (f32[1,16,8,2,128]{4,3,2,1,0:T(2,128)S(1)}, f32[1,16,8,2,128]{4,3,2,1,0:T(2,128)}, u32[]{:S(2)}) copy-start(f32[1,16,8,2,128]{4,3,2,1,0:T(2,128)} %param.11) | copy-start | bytes 393220
  9.8 18.3 %collective-permute-start = (f32[25,32,128]{2,1,0:T(8,128)S(1)}, f32[25,32,128]{2,1,0:T(8,128)S(1)}, u32[]{:S(2)}, u32[]{:S(2)}) collective-permute-start(f32[25,32,128]{2,1,0:T(8,128)S(1)} %get-tuple-element.13), channel_id=1, source_target_pairs={{0,2},{2,0},{4,6},{6,4},{8,10},{10,8},{12,14},{14,12},{16,18},{18,... | collective-permute-start | bytes 1228808 | tf_op jit(solution)/shard_map/ppermute | solution.py:192
  12.8 19.7 %collective-permute-start.1 = (f32[25,32,128]{2,1,0:T(8,128)S(1)}, f32[25,32,128]{2,1,0:T(8,128)S(1)}, u32[]{:S(2)}, u32[]{:S(2)}) collective-permute-start(f32[25,32,128]{2,1,0:T(8,128)S(1)} %get-tuple-element.14), channel_id=1, source_target_pairs={{0,4},{2,6},{4,0},{6,2},{8,12},{10,14},{12,8},{14,10},{16,20},{18,... | collective-permute-start | bytes 1228808 | tf_op jit(solution)/shard_map/ppermute | solution.py:192
  14.3 18.2 %collective-permute-start.2 = (f32[25,32,128]{2,1,0:T(8,128)S(1)}, f32[25,32,128]{2,1,0:T(8,128)S(1)}, u32[]{:S(2)}, u32[]{:S(2)}) collective-permute-start(f32[25,32,128]{2,1,0:T(8,128)S(1)} %get-tuple-element.15), channel_id=1, source_target_pairs={{0,6},{2,4},{4,2},{6,0},{8,14},{10,12},{12,10},{14,8},{16,22},{18,... | collective-permute-start | bytes 1228808 | tf_op jit(solution)/shard_map/ppermute | solution.py:192
  14.4 6.3 %collective-permute-start.3 = (f32[8,32,128]{2,1,0:T(8,128)S(1)}, f32[8,32,128]{2,1,0:T(8,128)S(1)}, u32[]{:S(2)}, u32[]{:S(2)}) collective-permute-start(f32[8,32,128]{2,1,0:T(8,128)S(1)} %get-tuple-element.16.refs_4_), channel_id=1, source_target_pairs={{0,8},{2,10},{4,12},{6,14},{8,0},{10,2},{12,4},{14,6},{16,24},{18,... | collective-permute-start | bytes 393224 | tf_op jit(solution)/shard_map/ppermute | solution.py:192
  16.4 11.7 %collective-permute-start.4 = (f32[8,32,128]{2,1,0:T(8,128)S(1)}, f32[8,32,128]{2,1,0:T(8,128)S(1)}, u32[]{:S(2)}, u32[]{:S(2)}) collective-permute-start(f32[8,32,128]{2,1,0:T(8,128)S(1)} %get-tuple-element.16.refs_4_), channel_id=1, source_target_pairs={{0,16},{2,18},{4,20},{6,22},{8,24},{10,26},{12,28},{14,30},{16,0},... | collective-permute-start | bytes 393224 | tf_op jit(solution)/shard_map/ppermute | solution.py:192
  20.6 7.5 %collective-permute-start.5 = (f32[8,32,128]{2,1,0:T(8,128)S(1)}, f32[8,32,128]{2,1,0:T(8,128)S(1)}, u32[]{:S(2)}, u32[]{:S(2)}) collective-permute-start(f32[8,32,128]{2,1,0:T(8,128)S(1)} %get-tuple-element.16.refs_4_), channel_id=1, source_target_pairs={{0,24},{2,26},{4,28},{6,30},{8,16},{10,18},{12,20},{14,22},{16,8},... | collective-permute-start | bytes 393224 | tf_op jit(solution)/shard_map/ppermute | solution.py:192
  34.4 3.7 %collective-permute-start.10 = (f32[8,128]{1,0:T(8,128)S(1)}, f32[8,128]{1,0:T(8,128)S(1)}, u32[]{:S(2)}, u32[]{:S(2)}) collective-permute-start(f32[8,128]{1,0:T(8,128)S(1)} %get-tuple-element.21), channel_id=1, source_target_pairs={{0,4},{2,6},{4,0},{6,2},{8,12},{10,14},{12,8},{14,10},{16,20},{18,... | collective-permute-start | bytes 12296 | tf_op jit(solution)/shard_map/ppermute | solution.py:192
  36.0 4.5 %collective-permute-start.11 = (f32[8,128]{1,0:T(8,128)S(1)}, f32[8,128]{1,0:T(8,128)S(1)}, u32[]{:S(2)}, u32[]{:S(2)}) collective-permute-start(f32[8,128]{1,0:T(8,128)S(1)} %get-tuple-element.21), channel_id=1, source_target_pairs={{0,6},{2,4},{4,2},{6,0},{8,14},{10,12},{12,10},{14,8},{16,22},{18,... | collective-permute-start | bytes 12296 | tf_op jit(solution)/shard_map/ppermute | solution.py:192
  37.1 3.6 %collective-permute-start.9 = (f32[8,128]{1,0:T(8,128)S(1)}, f32[8,128]{1,0:T(8,128)S(1)}, u32[]{:S(2)}, u32[]{:S(2)}) collective-permute-start(f32[8,128]{1,0:T(8,128)S(1)} %get-tuple-element.21), channel_id=1, source_target_pairs={{0,2},{2,0},{4,6},{6,4},{8,10},{10,8},{12,14},{14,12},{16,18},{18,... | collective-permute-start | bytes 12296 | tf_op jit(solution)/shard_map/ppermute | solution.py:192
  40.8 8.6 %collective-permute-start.12 = (f32[8,128]{1,0:T(8,128)S(1)}, f32[8,128]{1,0:T(8,128)S(1)}, u32[]{:S(2)}, u32[]{:S(2)}) collective-permute-start(f32[8,128]{1,0:T(8,128)S(1)} %add_add_fusion.1), channel_id=1, source_target_pairs={{0,8},{2,10},{4,12},{6,14},{8,0},{10,2},{12,4},{14,6},{16,24},{18,... | collective-permute-start | bytes 12296 | tf_op jit(solution)/shard_map/ppermute | solution.py:192
  42.3 7.2 %collective-permute-start.13 = (f32[8,128]{1,0:T(8,128)S(1)}, f32[8,128]{1,0:T(8,128)S(1)}, u32[]{:S(2)}, u32[]{:S(2)}) collective-permute-start(f32[8,128]{1,0:T(8,128)S(1)} %add_add_fusion.1), channel_id=1, source_target_pairs={{0,16},{2,18},{4,20},{6,22},{8,24},{10,26},{12,28},{14,30},{16,0},... | collective-permute-start | bytes 12296 | tf_op jit(solution)/shard_map/ppermute | solution.py:192
  44.9 5.5 %collective-permute-start.14 = (f32[8,128]{1,0:T(8,128)S(1)}, f32[8,128]{1,0:T(8,128)S(1)}, u32[]{:S(2)}, u32[]{:S(2)}) collective-permute-start(f32[8,128]{1,0:T(8,128)S(1)} %add_add_fusion.1), channel_id=1, source_target_pairs={{0,24},{2,26},{4,28},{6,30},{8,16},{10,18},{12,20},{14,22},{16,8},... | collective-permute-start | bytes 12296 | tf_op jit(solution)/shard_map/ppermute | solution.py:192
  45.1 7.0 %collective-permute-start.6 = (f32[272,128]{1,0:T(8,128)S(1)}, f32[272,128]{1,0:T(8,128)S(1)}, u32[]{:S(2)}, u32[]{:S(2)}) collective-permute-start(f32[272,128]{1,0:T(8,128)S(1)} %get-tuple-element.18), channel_id=1, source_target_pairs={{0,8},{2,10},{4,12},{6,14},{8,0},{10,2},{12,4},{14,6},{16,24},{18,... | collective-permute-start | bytes 417800 | tf_op jit(solution)/shard_map/ppermute | solution.py:192
  45.8 11.2 %collective-permute-start.7 = (f32[272,128]{1,0:T(8,128)S(1)}, f32[272,128]{1,0:T(8,128)S(1)}, u32[]{:S(2)}, u32[]{:S(2)}) collective-permute-start(f32[272,128]{1,0:T(8,128)S(1)} %get-tuple-element.19), channel_id=1, source_target_pairs={{0,16},{2,18},{4,20},{6,22},{8,24},{10,26},{12,28},{14,30},{16,0},... | collective-permute-start | bytes 417800 | tf_op jit(solution)/shard_map/ppermute | solution.py:192
  49.3 7.8 %collective-permute-start.8 = (f32[272,128]{1,0:T(8,128)S(1)}, f32[272,128]{1,0:T(8,128)S(1)}, u32[]{:S(2)}, u32[]{:S(2)}) collective-permute-start(f32[272,128]{1,0:T(8,128)S(1)} %get-tuple-element.20), channel_id=1, source_target_pairs={{0,24},{2,26},{4,28},{6,30},{8,16},{10,18},{12,20},{14,22},{16,8},... | collective-permute-start | bytes 417800 | tf_op jit(solution)/shard_map/ppermute | solution.py:192
  50.4 1.2 %collective-permute-start.15 = (f32[8,128]{1,0:T(8,128)S(1)}, f32[8,128]{1,0:T(8,128)S(1)}, u32[]{:S(2)}, u32[]{:S(2)}) collective-permute-start(f32[8,128]{1,0:T(8,128)S(1)} %add_add_fusion), channel_id=1, source_target_pairs={{0,1},{1,0},{2,3},{3,2},{4,5},{5,4},{6,7},{7,6},{8,9},{9,8},{10,11... | collective-permute-start | bytes 12296 | tf_op jit(solution)/shard_map/ppermute | solution.py:245

commit v2 on v1

v2 whole, which is shorter than its diff:
```python
import functools
import math

import jax
import jax.numpy as jnp
from jax import lax
from jax.experimental import pallas as pl
from jax.experimental.pallas import tpu as pltpu
from jax.sharding import PartitionSpec as P

LOW = 4
LANES = 128
BOX_DEV = 4
VMEM_LIMIT = 48 * 1024 * 1024


def cut(angles):
    sizes = [angles]
    return [(sum(sizes[:c]), size) for c, size in enumerate(sizes)]


def complex_rows(real, imag):
    return jnp.concatenate(
        [jnp.concatenate([real, imag], axis=1), jnp.concatenate([imag, -real], axis=1)], axis=0
    )


def fill_kernel(chunks, slots, *refs):
    whole_refs, refs = refs[:8], refs[8:]
    message_refs = [refs[c * LOW : (c + 1) * LOW] for c in range(len(chunks))]
    current_refs, refs = refs[len(chunks) * LOW : len(chunks) * (LOW + 1)], refs[len(chunks) * (LOW + 1) :]
    held_refs, (sems, near_sems) = refs[:8], refs[8:]
    (
        col_device_ref,
        col_offset_ref,
        box_ref,
        rate_ref,
        adjoint_ref,
        currents_ref,
        radiation_ref,
        near_ref,
    ) = held_refs
    blocks, near_count = col_device_ref.shape
    stride = 2 * blocks
    angles = adjoint_ref.shape[0] // stride
    copies = [
        pltpu.make_async_copy(whole_refs[i], held_refs[i], sems.at[i]) for i in (0, 1, 2, 3, 4, 5, 6)
    ]
    near_copies = [
        pltpu.make_async_copy(
            whole_refs[7].at[pl.ds(row * near_count, near_count)],
            near_ref.at[pl.ds(row * near_count, near_count)],
            near_sems.at[row],
        )
        for row in range(blocks)
    ]
    for copy in copies[:5] + near_copies[:2] + copies[5:] + near_copies[2:]:
        copy.start()
    me = lax.axis_index("basis")
    my_low = lax.rem(me, LOW)
    my_high = lax.div(me, LOW)
    spread = LANES // LOW
    lane8 = lax.broadcasted_iota(jnp.int32, (8, LANES), 1)
    sub8 = lax.broadcasted_iota(jnp.int32, (8, LANES), 0)
    table = jnp.zeros((8, LANES), jnp.float32)
    counts = [jnp.int32(0)] * LOW
    for copy in copies[:5]:
        copy.wait()
    for row in range(blocks):
        real = adjoint_ref[pl.ds(2 * row, angles, stride=stride), :].astype(jnp.bfloat16)
        imag = adjoint_ref[pl.ds(2 * row + 1, angles, stride=stride), :].astype(jnp.bfloat16)
        left = complex_rows(real, imag)
        box = box_ref[row].astype(jnp.float32)
        near_copies[row].wait()
        for k in range(near_count):
            term = jnp.dot(left, near_ref[row * near_count + k], preferred_element_type=jnp.float32)
            device = col_device_ref[row, k]
            low = lax.bitwise_xor(lax.rem(device, LOW), my_low)
            high = lax.bitwise_xor(lax.div(device, LOW), my_high)
            place = high * blocks + col_offset_ref[row, k] + 1
            own_slot = jnp.int32(0)
            for e in range(LOW):
                here = low == e
                slot = jnp.where(here, jnp.minimum(counts[e], slots), slots)
                own_slot = jnp.where(here, counts[e], own_slot)
                counts[e] = counts[e] + here.astype(jnp.int32)
                for c, (first, size) in enumerate(chunks):
                    message_refs[c][e][slot, pl.ds(0, size), :] = term[first : first + size]
                    message_refs[c][e][slot, pl.ds(size, size), :] = term[
                        angles + first : angles + first + size
                    ]
            entry = jnp.where(
                sub8 == 0, place.astype(jnp.float32), jnp.where(sub8 == 1, rate_ref[row, k], box)
            )
            table = jnp.where(lane8 == low * spread + own_slot, entry, table)
    for copy in copies[5:]:
        copy.wait()
    for row in range(blocks):
        for part in range(2):
            rows = currents_ref[pl.ds(2 * row + part, angles, stride=stride), :]
            for c, (first, size) in enumerate(chunks):
                current_refs[c][row, pl.ds(part * size, size), :] = rows[first : first + size]
    count = angles * blocks
    rad_real = radiation_ref[pl.ds(0, count, stride=2), :]
    rad_imag = radiation_ref[pl.ds(1, count, stride=2), :]
    cur_real = currents_ref[pl.ds(0, count, stride=2), :]
    cur_imag = currents_ref[pl.ds(1, count, stride=2), :]
    far_real = jnp.sum((rad_real * cur_real - rad_imag * cur_imag).reshape(angles, blocks, LANES), axis=1)
    far_imag = jnp.sum((rad_real * cur_imag + rad_imag * cur_real).reshape(angles, blocks, LANES), axis=1)
    lane = lax.broadcasted_iota(jnp.int32, (angles, LANES), 1)
    far = jnp.where(lane == 0, jnp.sum(far_real, axis=1, keepdims=True), 0.0) + jnp.where(
        lane == 1, jnp.sum(far_imag, axis=1, keepdims=True), 0.0
    )
    for e in range(LOW):
        mine = jnp.where(lane8 // spread == e, table, 0.0)
        extra = jnp.concatenate([far, mine], axis=0)
        size2 = 2 * chunks[0][1]
        for part in range(-(-extra.shape[0] // size2)):
            rows = extra[part * size2 : (part + 1) * size2]
            message_refs[0][e][slots + part, pl.ds(0, rows.shape[0]), :] = rows


def sum_kernel(angles, size, slots, high_count, first, last, *refs):
    message_refs, refs = refs[:LOW], refs[LOW:]
    current_refs, refs = refs[:high_count], refs[high_count:]
    if not first:
        (earlier_table_ref, earlier_ref), refs = refs[:2], refs[2:]
    out_refs, refs = refs[:high_count], refs[high_count:]
    if last:
        (grad_ref,), refs = refs[:1], refs[1:]
    else:
        (next_table_ref, next_ref), refs = refs[:2], refs[2:]
    acc_ref, cur_ref, prod_ref, table_ref, place_ref, sem = refs
    blocks = current_refs[0].shape[0]
    spread = LANES // LOW
    record = 2 * size
    if first:
        extra = None
        for e in range(LOW):
            parts = [message_refs[e][slots + part] for part in range(message_refs[e].shape[0] - slots)]
            own = jnp.concatenate(parts, axis=0) if len(parts) > 1 else parts[0]
            extra = own if extra is None else extra + own
        far, table = extra[:angles], extra[angles : angles + 8]
    else:
        table = earlier_table_ref[...]
    table_ref[...] = table.astype(jnp.int32)
    copy = pltpu.make_async_copy(table_ref, place_ref, sem)
    copy.start()
    for d in range(high_count):
        cur_ref[pl.ds(d * blocks, blocks)] = current_refs[d][...]
    acc_ref[...] = jnp.zeros(acc_ref.shape, jnp.float32)
    prod_ref[...] = jnp.zeros(prod_ref.shape, jnp.float32)
    copy.wait()
    for e in range(LOW):
        for s in range(slots):
            place = place_ref[0, e * spread + s]
            used = place > 0
            at = jnp.maximum(place - 1, 0)
            term = jnp.where(used, message_refs[e][s], 0.0)
            acc_ref[at] = acc_ref[at] + term
            both = term * cur_ref[at]
            prod_ref[e * spread + s] = jnp.sum(both.reshape(record // 8, 8, LANES), axis=0)
    for d in range(high_count):
        for b in range(blocks):
            out_refs[d][pl.ds(b * record, record), :] = acc_ref[d * blocks + b]
        if first:
            out_refs[d][pl.ds(blocks * record, angles), :] = far
    by_slot = jnp.sum(prod_ref[...], axis=1)
    if not first:
        by_slot = by_slot + earlier_ref[...]
    if not last:
        next_table_ref[...] = table
        next_ref[...] = by_slot
        return
    highest = lax.Precision.HIGHEST
    contract_last = (((1,), (1,)), ((), ()))
    values = lax.dot_general(
        jnp.ones((8, LANES), jnp.float32),
        by_slot,
        contract_last,
        precision=highest,
        preferred_element_type=jnp.float32,
    )
    boxes = grad_ref.shape[1]
    number = lax.broadcasted_iota(jnp.int32, (boxes, LANES), 0).astype(jnp.float32)
    rates = jnp.where(number == table[2:3, :], table[1:2, :], 0.0)
    grad_ref[...] = lax.dot_general(
        values, rates, contract_last, precision=highest, preferred_element_type=jnp.float32
    )


def update_kernel(chunks, angles, norm_far, high_count, *refs):
    sum_refs = [refs[c * high_count : (c + 1) * high_count] for c in range(len(chunks))]
    adjoint_ref, radiation_ref, inverse_ref, out_ref = refs[len(chunks) * high_count :]
    blocks = inverse_ref.shape[0]
    stride = 2 * blocks

    def total(c, start, rows):
        parts = [ref[pl.ds(start, rows), :] for ref in sum_refs[c]]
        return functools.reduce(jnp.add, parts)

    far = total(0, blocks * 2 * chunks[0][1], angles) * norm_far
    far_real = jnp.broadcast_to(far[:, 0:1], (angles, LANES))
    far_imag = jnp.broadcast_to(far[:, 1:2], (angles, LANES))
    for block in range(blocks):
        rows_real = pl.ds(2 * block, angles, stride=stride)
        rows_imag = pl.ds(2 * block + 1, angles, stride=stride)
        near_real = [total(c, block * 2 * size, size) for c, (_, size) in enumerate(chunks)]
        near_imag = [total(c, block * 2 * size + size, size) for c, (_, size) in enumerate(chunks)]
        near_real = jnp.concatenate(near_real, axis=0)
        near_imag = jnp.concatenate(near_imag, axis=0)
        rad_real, rad_imag = radiation_ref[rows_real, :], radiation_ref[rows_imag, :]
        real = (far_real * rad_real + far_imag * rad_imag - near_real).astype(jnp.bfloat16)
        imag = (far_imag * rad_real - far_real * rad_imag - near_imag).astype(jnp.bfloat16)
        step = jnp.dot(complex_rows(real, imag), inverse_ref[block], preferred_element_type=jnp.float32)
        out_ref[rows_real, :] = adjoint_ref[rows_real, :] + step[:angles]
        out_ref[rows_imag, :] = adjoint_ref[rows_imag, :] + step[angles:]


def on_device(
    adjoint,
    currents,
    radiation,
    near_blocks,
    inverse_blocks,
    col_device,
    col_offset,
    box_of_block,
    pair_rate,
):
    angles, blocks, unknowns = adjoint.shape[1], adjoint.shape[2], adjoint.shape[4]
    near_count = near_blocks.shape[1]
    pairs = blocks * near_count
    basis_count = lax.axis_size("basis")
    high_count = basis_count // LOW
    angles_all = angles * lax.axis_size("angle")
    boxes = BOX_DEV * basis_count
    slots = 2 * pairs // basis_count * high_count
    vmem = pl.BlockSpec(memory_space=pltpu.VMEM)
    smem = pl.BlockSpec(memory_space=pltpu.SMEM)
    params = pltpu.CompilerParams(vmem_limit_bytes=VMEM_LIMIT)

    def moved(value, bits):
        return lax.ppermute(value, "basis", [(i, i ^ bits) for i in range(basis_count)])

    flat = (angles * blocks * 2, unknowns)
    adjoint_rows = adjoint.reshape(flat)
    currents_rows = currents.reshape(flat)
    radiation_rows = radiation.reshape(flat)
    near = near_blocks.reshape(pairs, 2 * unknowns, unknowns)
    inverse = inverse_blocks.reshape(blocks, 2 * unknowns, unknowns)
    f32 = functools.partial(jax.ShapeDtypeStruct, dtype=jnp.float32)
    chunks = cut(angles)
    extra = [-(-(angles + 8) // (2 * chunks[0][1]))] + [1] * (len(chunks) - 1)
    filled = pl.pallas_call(
        functools.partial(fill_kernel, chunks, slots),
        out_shape=[f32((slots + more, 2 * size, unknowns)) for (_, size), more in zip(chunks, extra) for _ in range(LOW)]
        + [f32((blocks, 2 * size, unknowns)) for _, size in chunks],
        in_specs=[pl.BlockSpec(memory_space=pltpu.HBM)] * 8,
        out_specs=[vmem] * (len(chunks) * (LOW + 1)),
        scratch_shapes=[
            pltpu.SMEM(col_device.shape, jnp.int32),
            pltpu.SMEM(col_offset.shape, jnp.int32),
            pltpu.SMEM(box_of_block.shape, jnp.int32),
            pltpu.SMEM(pair_rate.shape, jnp.float32),
            pltpu.VMEM(flat, jnp.float32),
            pltpu.VMEM(flat, jnp.float32),
            pltpu.VMEM(flat, jnp.float32),
            pltpu.VMEM(near.shape, near.dtype),
            pltpu.SemaphoreType.DMA((7,)),
            pltpu.SemaphoreType.DMA((blocks,)),
        ],
        compiler_params=params,
        name="fill",
    )(
        *[
            pltpu.with_memory_space_constraint(whole, pltpu.HBM)
            for whole in (
                col_device,
                col_offset,
                box_of_block,
                pair_rate,
                adjoint_rows,
                currents_rows,
                radiation_rows,
                near,
            )
        ]
    )
    own_currents = filled[len(chunks) * LOW :]
    box_lanes = -(-boxes // LANES) * LANES
    totals, carried = [], []
    for c, (_, size) in enumerate(chunks):
        messages = filled[c * LOW : (c + 1) * LOW]
        arrived = [messages[0]] + [moved(messages[e], e) for e in range(1, LOW)]
        beside = [own_currents[c]] + [moved(own_currents[c], d * LOW) for d in range(1, high_count)]
        first, last = c == 0, c == len(chunks) - 1
        partial = f32((blocks * 2 * size + (angles if first else 0), unknowns))
        carry_shapes = [f32((8, box_lanes))] if last else [f32((8, LANES)), f32((LANES, unknowns))]
        sums_and_carry = pl.pallas_call(
            functools.partial(sum_kernel, angles, size, slots, high_count, first, last),
            out_shape=[partial] * high_count + carry_shapes,
            in_specs=[vmem] * (LOW + high_count + len(carried)),
            out_specs=[vmem] * (high_count + len(carry_shapes)),
            scratch_shapes=[
                pltpu.VMEM((high_count * blocks, 2 * size, unknowns), jnp.float32),
                pltpu.VMEM((high_count * blocks, 2 * size, unknowns), jnp.float32),
                pltpu.VMEM((LANES, 8, unknowns), jnp.float32),
                pltpu.VMEM((8, LANES), jnp.int32),
                pltpu.SMEM((8, LANES), jnp.int32),
                pltpu.SemaphoreType.DMA,
            ],
            compiler_params=params,
            name="sum",
        )(*arrived, *beside, *carried)
        sums, carried = sums_and_carry[:high_count], sums_and_carry[high_count:]
        totals += [sums[0]] + [moved(sums[d], d * LOW) for d in range(1, high_count)]
    (grad,) = carried
    norm_far = 1.0 / math.sqrt(blocks * basis_count * unknowns)
    updated = pl.pallas_call(
        functools.partial(update_kernel, chunks, angles, norm_far, high_count),
        out_shape=f32(flat),
        in_specs=[vmem] * (len(totals) + 3),
        out_specs=vmem,
        compiler_params=params,
        cost_estimate=pl.CostEstimate(flops=1 << 20, bytes_accessed=1 << 20, transcendentals=0),
        name="update",
    )(*totals, adjoint_rows, radiation_rows, inverse)
    everyone = ("basis", "pol")
    senders = basis_count * lax.axis_size("pol")
    gathered = lax.all_to_all(
        jnp.broadcast_to(grad[:1], (senders, 1, box_lanes)), everyone, split_axis=0, concat_axis=0
    )
    total_grad = jnp.sum(gathered[:, 0], axis=0)
    if lax.axis_size("angle") > 1:
        total_grad = lax.psum(total_grad, "angle")
    share = lax.dynamic_slice_in_dim(total_grad, lax.axis_index("basis") * BOX_DEV, BOX_DEV)
    shape_grad = share * (-1.0 / math.sqrt(4 * unknowns * angles_all * near_count))
    return (updated.reshape(adjoint.shape), shape_grad)


def solution(mesh):
    placed = (
        P("pol", "angle", "basis", None, None),
        P("pol", "angle", "basis", None, None),
        P("pol", "angle", "basis", None, None),
        P("basis", None, None, None, None),
        P("basis", None, None, None),
        P("basis", None),
        P("basis", None),
        P("basis"),
        P("basis", None),
    )
    return jax.shard_map(
        on_device,
        mesh=mesh,
        in_specs=placed,
        out_specs=(P("pol", "angle", "basis", None, None), P("basis")),
        check_vma=False,
    )
```

time: 58.4 us -> 50.8 us (0.87)
  local copies, waits for them, and re-layouts: 7.32 us -> 0.63 us
  starting transfers between devices: 25.6 us -> 22.6 us
  Pallas kernels: 4.65 us -> 6.39 us
    ppermute x15 -> x9, starting transfers between devices: 25.6 us -> 17.7 us  [moved(): lax.ppermute(value, 'basis', [(i, i ^ bits) for i in range(basis_count)])]
    unnamed x22 -> x6, local copies, waits for them, and re-layouts: 7.32 us -> 0.01 us
    all_to_all x0 -> x1, starting transfers between devices: none -> 4.89 us  [on_device(): lax.all_to_all(jnp.broadcast_to(grad[:1], (senders, 1, box_lanes)), every...]
    all_to_all x0 -> x1, waiting for transfers between devices: none -> 2.7 us  [on_device(): lax.all_to_all(jnp.broadcast_to(grad[:1], (senders, 1, box_lanes)), every...]
    pallas_call x3, Pallas kernels: 4.65 us -> 6.39 us  [the longest x1 3.58 us: on_device(): pl.pallas_call(functools.partial(fill_kernel, chunks, slots), out_shape=[...]
    ppermute x1 -> x0, waiting for transfers between devices: 1.16 us -> none  [on_device(): lax.ppermute(grad, axis, [(i, i ^ b) for i in range(size)])]
    ppermute x15 -> x9, waiting for transfers between devices: 18.1 us -> 17 us  [moved(): lax.ppermute(value, 'basis', [(i, i ^ bits) for i in range(basis_count)])]
    broadcast_in_dim x0 -> x1, local copies, waits for them, and re-layouts: none -> 0.61 us  [on_device(): jnp.broadcast_to(grad[:1], (senders, 1, box_lanes))]
  transfers between devices with their start and end apart: 16 -> 10, of which waited for: 9 -> 6; matrix products, arithmetic and copies ran while one was open for 1% -> 1% of each run, Pallas kernels for 0% -> 0%
where the time goes in v2:
time: 50.8 us; the launch traced here: 50.6 us
  starting transfers between devices  22.6 us (44%)
  waiting for transfers between devices  19.7 us (39%)
  Pallas kernels  6.39 us (13%)
  between operations  0.71 us (1%)
  local copies, waits for them, and re-layouts  0.63 us (1%)
  other arithmetic  0.61 us (1%)
    ppermute x9, starting transfers between devices, moved(): lax.ppermute(value, 'basis', [(i, i ^ bits) for i in range(basis_count)])  17.7 us
    ppermute x9, waiting for transfers between devices, moved(): lax.ppermute(value, 'basis', [(i, i ^ bits) for i in range(basis_count)])  17 us
    all_to_all x1, starting transfers between devices, on_device(): lax.all_to_all(jnp.broadcast_to(grad[:1], (senders, 1, box_lanes)), every...  4.89 us
    pallas_call x1, Pallas kernels, on_device(): pl.pallas_call(functools.partial(fill_kernel, chunks, slots), out_shape=[...  3.58 us
    all_to_all x1, waiting for transfers between devices, on_device(): lax.all_to_all(jnp.broadcast_to(grad[:1], (senders, 1, box_lanes)), every...  2.7 us
    pallas_call x1, Pallas kernels, on_device(): pl.pallas_call(functools.partial(sum_kernel, angles, size, slots, high_co...  1.85 us
  transfers between devices with their start and end apart: 10, of which 6 were waited for; matrix products, arithmetic and copies ran while one was open for 1% of the time, Pallas kernels for 0%

profile of v2, /device:TPU:0, one launch (start us, length us, event | category | flops | bytes accessed | tf_op | source)
XLA Modules:
  0.0 50.6 jit_solution(6334803925472197423)
XLA Ops:
  0.6 0.0 copy-start.1
  0.6 0.0 copy-start.2
  0.7 0.0 copy-start
  0.7 3.6 %fill.1 = (f32[25,32,128]{2,1,0:T(8,128)S(1)}, f32[25,32,128]{2,1,0:T(8,128)S(1)}, f32[25,32,128]{2,1,0:T(8,128)S(1)}, f32[25,32,128]{2,1,0:T(8,128)S(1)}, f32[8,32,128]{2,1,0:T(8,128)S(1)}) custom-call(s32[8,6]{1,0:T(8,128)} %refs_0_.1, s32[8,6]{1,0:T(8,128)} %refs_1_.1, s32[8]{0:T(128)} %refs_2_.1, f32[8,6]{1,0:T(8,128)} %refs_3_.1, f32[256,128]{1,0:T(8,128)} %bitcast.10, ...), custom_call_target="tpu_custom_call" | custom-call | tf_op jit(solution)/shard_map/fill/pallas_call | solution.py:255
  4.2 3.0 %collective-permute-start = (f32[25,32,128]{2,1,0:T(8,128)S(1)}, f32[25,32,128]{2,1,0:T(8,128)S(1)}, u32[]{:S(2)}, u32[]{:S(2)}) collective-permute-start(f32[25,32,128]{2,1,0:T(8,128)S(1)} %get-tuple-element.13), channel_id=1, source_target_pairs={{0,2},{2,0},{4,6},{6,4},{8,10},{10,8},{12,14},{14,12},{16,18},{18,... | collective-permute-start | bytes 1228808 | tf_op jit(solution)/shard_map/ppermute | solution.py:244
  7.2 1.5 %collective-permute-start.1 = (f32[25,32,128]{2,1,0:T(8,128)S(1)}, f32[25,32,128]{2,1,0:T(8,128)S(1)}, u32[]{:S(2)}, u32[]{:S(2)}) collective-permute-start(f32[25,32,128]{2,1,0:T(8,128)S(1)} %get-tuple-element.14), channel_id=1, source_target_pairs={{0,4},{2,6},{4,0},{6,2},{8,12},{10,14},{12,8},{14,10},{16,20},{18,... | collective-permute-start | bytes 1228808 | tf_op jit(solution)/shard_map/ppermute | solution.py:244
  8.8 0.0 collective-permute-start.2
  8.8 2.0 %collective-permute-start.3 = (f32[8,32,128]{2,1,0:T(8,128)S(1)}, f32[8,32,128]{2,1,0:T(8,128)S(1)}, u32[]{:S(2)}, u32[]{:S(2)}) collective-permute-start(f32[8,32,128]{2,1,0:T(8,128)S(1)} %get-tuple-element.16.refs_4_), channel_id=1, source_target_pairs={{0,8},{2,10},{4,12},{6,14},{8,0},{10,2},{12,4},{14,6},{16,24},{18,... | collective-permute-start | bytes 393224 | tf_op jit(solution)/shard_map/ppermute | solution.py:244
  10.8 2.6 %collective-permute-start.4 = (f32[8,32,128]{2,1,0:T(8,128)S(1)}, f32[8,32,128]{2,1,0:T(8,128)S(1)}, u32[]{:S(2)}, u32[]{:S(2)}) collective-permute-start(f32[8,32,128]{2,1,0:T(8,128)S(1)} %get-tuple-element.16.refs_4_), channel_id=1, source_target_pairs={{0,16},{2,18},{4,20},{6,22},{8,24},{10,26},{12,28},{14,30},{16,0},... | collective-permute-start | bytes 393224 | tf_op jit(solution)/shard_map/ppermute | solution.py:244
  13.4 1.6 %collective-permute-done.3.refs_5_ = f32[8,32,128]{2,1,0:T(8,128)S(1)} collective-permute-done((f32[8,32,128]{2,1,0:T(8,128)S(1)}, f32[8,32,128]{2,1,0:T(8,128)S(1)}, u32[]{:S(2)}, u32[]{:S(2)}) %collective-permute-start.3) | collective-permute-done | bytes 131104 | tf_op jit(solution)/shard_map/ppermute | solution.py:244
  15.1 4.1 %collective-permute-start.5 = (f32[8,32,128]{2,1,0:T(8,128)S(1)}, f32[8,32,128]{2,1,0:T(8,128)S(1)}, u32[]{:S(2)}, u32[]{:S(2)}) collective-permute-start(f32[8,32,128]{2,1,0:T(8,128)S(1)} %get-tuple-element.16.refs_4_), channel_id=1, source_target_pairs={{0,24},{2,26},{4,28},{6,30},{8,16},{10,18},{12,20},{14,22},{16,8},... | collective-permute-start | bytes 393224 | tf_op jit(solution)/shard_map/ppermute | solution.py:244
  19.1 3.4 %collective-permute-done.4.refs_6_ = f32[8,32,128]{2,1,0:T(8,128)S(1)} collective-permute-done((f32[8,32,128]{2,1,0:T(8,128)S(1)}, f32[8,32,128]{2,1,0:T(8,128)S(1)}, u32[]{:S(2)}, u32[]{:S(2)}) %collective-permute-start.4) | collective-permute-done | bytes 131104 | tf_op jit(solution)/shard_map/ppermute | solution.py:244
  22.6 0.0 collective-permute-done.5.refs_7_
  22.6 0.0 collective-permute-done.refs_1_
  22.6 4.4 %collective-permute-done.1.refs_2_ = f32[25,32,128]{2,1,0:T(8,128)S(1)} collective-permute-done((f32[25,32,128]{2,1,0:T(8,128)S(1)}, f32[25,32,128]{2,1,0:T(8,128)S(1)}, u32[]{:S(2)}, u32[]{:S(2)}) %collective-permute-start.1) | collective-permute-done | bytes 409632 | tf_op jit(solution)/shard_map/ppermute | solution.py:244
  27.0 0.0 collective-permute-done.2.refs_3_
  27.0 1.9 %sum.1 = (f32[272,128]{1,0:T(8,128)S(1)}, f32[272,128]{1,0:T(8,128)S(1)}, f32[272,128]{1,0:T(8,128)S(1)}, f32[272,128]{1,0:T(8,128)S(1)}, f32[8,128]{1,0:T(8,128)S(1)}) custom-call(f32[25,32,128]{2,1,0:T(8,128)S(1)} %get-tuple-element.12.refs_0_, f32[25,32,128]{2,1,0:T(8,128)S(1)} %collective-permute-done.refs_1_, ...), custom_call_target="tpu_custom_call" | custom-call | tf_op jit(solution)/shard_map/sum/pallas_call | solution.py:300
  28.8 0.6 %broadcast_in_dim.3 = f32[32,1,128]{2,1,0:T(1,128)} broadcast(f32[128]{0:T(128)S(1)} %slice_bitcast_fusion), dimensions={2} | broadcast | bytes 16896 | tf_op jit(solution)/shard_map/broadcast_in_dim | solution.py:332
  29.4 4.9 %all-to-all-start = ((f32[32,1,128]{2,1,0:T(1,128)}), f32[32,1,128]{2,1,0:T(1,128)S(1)}, u32[]{:S(2)}, u32[]{:S(2)}) async-start(f32[32,1,128]{2,1,0:T(1,128)} %broadcast_in_dim.3), calls=%async_computation | async-start | bytes 32768 | tf_op jit(solution)/shard_map/all_to_all | solution.py:331
  34.3 1.8 %collective-permute-start.6 = (f32[272,128]{1,0:T(8,128)S(1)}, f32[272,128]{1,0:T(8,128)S(1)}, u32[]{:S(2)}, u32[]{:S(2)}) collective-permute-start(f32[272,128]{1,0:T(8,128)S(1)} %get-tuple-element.18), channel_id=1, source_target_pairs={{0,8},{2,10},{4,12},{6,14},{8,0},{10,2},{12,4},{14,6},{16,24},{18,... | collective-permute-start | bytes 417800 | tf_op jit(solution)/shard_map/ppermute | solution.py:244
  36.2 2.4 %collective-permute-start.7 = (f32[272,128]{1,0:T(8,128)S(1)}, f32[272,128]{1,0:T(8,128)S(1)}, u32[]{:S(2)}, u32[]{:S(2)}) collective-permute-start(f32[272,128]{1,0:T(8,128)S(1)} %get-tuple-element.19), channel_id=1, source_target_pairs={{0,16},{2,18},{4,20},{6,22},{8,24},{10,26},{12,28},{14,30},{16,0},... | collective-permute-start | bytes 417800 | tf_op jit(solution)/shard_map/ppermute | solution.py:244
  38.6 0.2 collective-permute-start.8
  38.8 2.7 %all-to-all-done = f32[32,1,128]{2,1,0:T(1,128)S(1)} async-done(((f32[32,1,128]{2,1,0:T(1,128)}), f32[32,1,128]{2,1,0:T(1,128)S(1)}, u32[]{:S(2)}, u32[]{:S(2)}) %all-to-all-start) | async-done | bytes 16416 | tf_op jit(solution)/shard_map/all_to_all | solution.py:331
  41.5 0.6 %dynamic-slice_multiply_fusion = f32[4]{0:T(128)} fusion(f32[128]{0:T(128)S(1)} %reduce_sum.9, s32[]{:T(128)S(6)} %select_n.3), kind=kLoop, calls=%fused_computation | loop fusion | flops 4 | bytes 36 | tf_op jit(solution)/shard_map/mul | solution.py:338
  42.1 0.6 %collective-permute-done.6.refs_1_ = f32[272,128]{1,0:T(8,128)S(1)} collective-permute-done((f32[272,128]{1,0:T(8,128)S(1)}, f32[272,128]{1,0:T(8,128)S(1)}, u32[]{:S(2)}, u32[]{:S(2)}) %collective-permute-start.6) | collective-permute-done | bytes 139296 | tf_op jit(solution)/shard_map/ppermute | solution.py:244
  42.7 6.9 %collective-permute-done.7.refs_2_ = f32[272,128]{1,0:T(8,128)S(1)} collective-permute-done((f32[272,128]{1,0:T(8,128)S(1)}, f32[272,128]{1,0:T(8,128)S(1)}, u32[]{:S(2)}, u32[]{:S(2)}) %collective-permute-start.7) | collective-permute-done | bytes 139296 | tf_op jit(solution)/shard_map/ppermute | solution.py:244
  49.6 0.0 collective-permute-done.8.refs_3_
  49.6 0.0 copy-done.1
  49.6 0.0 copy-done.2
  49.6 0.0 copy-done
  49.6 1.0 %update.1 = f32[256,128]{1,0:T(8,128)} custom-call(f32[272,128]{1,0:T(8,128)S(1)} %get-tuple-element.17.refs_0_, f32[272,128]{1,0:T(8,128)S(1)} %collective-permute-done.6.refs_1_, f32[272,128]{1,0:T(8,128)S(1)} %collective-permute-done.7.refs_2_, f32[272,128]{1,0:T(8,128)S(1)} %collective-permute-done.8.refs_3_, f32[256,128]{1,0:T(8,128)S(1)} %bitcast.11, ...), custom_call_target="tpu_custom_call" | custom-call | flops 1048576 | bytes 1048576 | tf_op jit(solution)/shard_map/update/pallas_call | solution.py:320
  (2 shorter events, 0.0 us)
Async XLA Ops:
  0.6 49.0 %copy-start.1 = (f32[1,16,8,2,128]{4,3,2,1,0:T(2,128)S(1)}, f32[1,16,8,2,128]{4,3,2,1,0:T(2,128)}, u32[]{:S(2)}) copy-start(f32[1,16,8,2,128]{4,3,2,1,0:T(2,128)} %param.9) | copy-start | bytes 393220
  0.6 49.0 %copy-start.2 = (f32[1,16,8,2,128]{4,3,2,1,0:T(2,128)S(1)}, f32[1,16,8,2,128]{4,3,2,1,0:T(2,128)}, u32[]{:S(2)}) copy-start(f32[1,16,8,2,128]{4,3,2,1,0:T(2,128)} %param.11) | copy-start | bytes 393220
  0.7 49.0 %copy-start = (bf16[8,2,128,128]{3,2,1,0:T(8,128)(2,1)S(1)}, bf16[8,2,128,128]{3,2,1,0:T(8,128)(2,1)}, u32[]{:S(2)}) copy-start(bf16[8,2,128,128]{3,2,1,0:T(8,128)(2,1)} %param.13) | copy-start | bytes 1572868
  4.2 18.3 %collective-permute-start = (f32[25,32,128]{2,1,0:T(8,128)S(1)}, f32[25,32,128]{2,1,0:T(8,128)S(1)}, u32[]{:S(2)}, u32[]{:S(2)}) collective-permute-start(f32[25,32,128]{2,1,0:T(8,128)S(1)} %get-tuple-element.13), channel_id=1, source_target_pairs={{0,2},{2,0},{4,6},{6,4},{8,10},{10,8},{12,14},{14,12},{16,18},{18,... | collective-permute-start | bytes 1228808 | tf_op jit(solution)/shard_map/ppermute | solution.py:244
  7.2 19.7 %collective-permute-start.1 = (f32[25,32,128]{2,1,0:T(8,128)S(1)}, f32[25,32,128]{2,1,0:T(8,128)S(1)}, u32[]{:S(2)}, u32[]{:S(2)}) collective-permute-start(f32[25,32,128]{2,1,0:T(8,128)S(1)} %get-tuple-element.14), channel_id=1, source_target_pairs={{0,4},{2,6},{4,0},{6,2},{8,12},{10,14},{12,8},{14,10},{16,20},{18,... | collective-permute-start | bytes 1228808 | tf_op jit(solution)/shard_map/ppermute | solution.py:244
  8.8 18.2 %collective-permute-start.2 = (f32[25,32,128]{2,1,0:T(8,128)S(1)}, f32[25,32,128]{2,1,0:T(8,128)S(1)}, u32[]{:S(2)}, u32[]{:S(2)}) collective-permute-start(f32[25,32,128]{2,1,0:T(8,128)S(1)} %get-tuple-element.15), channel_id=1, source_target_pairs={{0,6},{2,4},{4,2},{6,0},{8,14},{10,12},{12,10},{14,8},{16,22},{18,... | collective-permute-start | bytes 1228808 | tf_op jit(solution)/shard_map/ppermute | solution.py:244
  8.8 6.3 %collective-permute-start.3 = (f32[8,32,128]{2,1,0:T(8,128)S(1)}, f32[8,32,128]{2,1,0:T(8,128)S(1)}, u32[]{:S(2)}, u32[]{:S(2)}) collective-permute-start(f32[8,32,128]{2,1,0:T(8,128)S(1)} %get-tuple-element.16.refs_4_), channel_id=1, source_target_pairs={{0,8},{2,10},{4,12},{6,14},{8,0},{10,2},{12,4},{14,6},{16,24},{18,... | collective-permute-start | bytes 393224 | tf_op jit(solution)/shard_map/ppermute | solution.py:244
  10.8 11.7 %collective-permute-start.4 = (f32[8,32,128]{2,1,0:T(8,128)S(1)}, f32[8,32,128]{2,1,0:T(8,128)S(1)}, u32[]{:S(2)}, u32[]{:S(2)}) collective-permute-start(f32[8,32,128]{2,1,0:T(8,128)S(1)} %get-tuple-element.16.refs_4_), channel_id=1, source_target_pairs={{0,16},{2,18},{4,20},{6,22},{8,24},{10,26},{12,28},{14,30},{16,0},... | collective-permute-start | bytes 393224 | tf_op jit(solution)/shard_map/ppermute | solution.py:244
  15.1 7.5 %collective-permute-start.5 = (f32[8,32,128]{2,1,0:T(8,128)S(1)}, f32[8,32,128]{2,1,0:T(8,128)S(1)}, u32[]{:S(2)}, u32[]{:S(2)}) collective-permute-start(f32[8,32,128]{2,1,0:T(8,128)S(1)} %get-tuple-element.16.refs_4_), channel_id=1, source_target_pairs={{0,24},{2,26},{4,28},{6,30},{8,16},{10,18},{12,20},{14,22},{16,8},... | collective-permute-start | bytes 393224 | tf_op jit(solution)/shard_map/ppermute | solution.py:244
  29.4 12.1 %all-to-all-start = ((f32[32,1,128]{2,1,0:T(1,128)}), f32[32,1,128]{2,1,0:T(1,128)S(1)}, u32[]{:S(2)}, u32[]{:S(2)}) async-start(f32[32,1,128]{2,1,0:T(1,128)} %broadcast_in_dim.3), calls=%async_computation | async-start | bytes 32768 | tf_op jit(solution)/shard_map/all_to_all | solution.py:331
  34.3 8.4 %collective-permute-start.6 = (f32[272,128]{1,0:T(8,128)S(1)}, f32[272,128]{1,0:T(8,128)S(1)}, u32[]{:S(2)}, u32[]{:S(2)}) collective-permute-start(f32[272,128]{1,0:T(8,128)S(1)} %get-tuple-element.18), channel_id=1, source_target_pairs={{0,8},{2,10},{4,12},{6,14},{8,0},{10,2},{12,4},{14,6},{16,24},{18,... | collective-permute-start | bytes 417800 | tf_op jit(solution)/shard_map/ppermute | solution.py:244
  36.2 13.4 %collective-permute-start.7 = (f32[272,128]{1,0:T(8,128)S(1)}, f32[272,128]{1,0:T(8,128)S(1)}, u32[]{:S(2)}, u32[]{:S(2)}) collective-permute-start(f32[272,128]{1,0:T(8,128)S(1)} %get-tuple-element.19), channel_id=1, source_target_pairs={{0,16},{2,18},{4,20},{6,22},{8,24},{10,26},{12,28},{14,30},{16,0},... | collective-permute-start | bytes 417800 | tf_op jit(solution)/shard_map/ppermute | solution.py:244
  38.6 11.0 %collective-permute-start.8 = (f32[272,128]{1,0:T(8,128)S(1)}, f32[272,128]{1,0:T(8,128)S(1)}, u32[]{:S(2)}, u32[]{:S(2)}) collective-permute-start(f32[272,128]{1,0:T(8,128)S(1)} %get-tuple-element.20), channel_id=1, source_target_pairs={{0,24},{2,26},{4,28},{6,30},{8,16},{10,18},{12,20},{14,22},{16,8},... | collective-permute-start | bytes 417800 | tf_op jit(solution)/shard_map/ppermute | solution.py:244

commit v3 on v1

v3 whole, which is shorter than its diff:
```python
import functools
import math

import jax
import jax.numpy as jnp
from jax import lax
from jax.experimental import pallas as pl
from jax.experimental.pallas import tpu as pltpu
from jax.sharding import PartitionSpec as P

LOW = 4
LANES = 128
BOX_DEV = 4
VMEM_LIMIT = 48 * 1024 * 1024


def complex_rows(real, imag):
    return jnp.concatenate(
        [jnp.concatenate([real, imag], axis=1), jnp.concatenate([imag, -real], axis=1)], axis=0
    )


def fill_kernel(slots, *refs):
    whole_refs, message_refs, current_rows_ref = refs[:8], refs[8 : 8 + LOW], refs[8 + LOW]
    *held_refs, sems, near_sems = refs[9 + LOW :]
    (
        col_device_ref,
        col_offset_ref,
        box_ref,
        rate_ref,
        adjoint_ref,
        currents_ref,
        radiation_ref,
        near_ref,
    ) = held_refs
    blocks, near_count = col_device_ref.shape
    stride = 2 * blocks
    angles = adjoint_ref.shape[0] // stride
    copies = [pltpu.make_async_copy(whole_refs[i], held_refs[i], sems.at[i]) for i in range(7)]
    near_copies = [
        pltpu.make_async_copy(
            whole_refs[7].at[pl.ds(row * near_count, near_count)],
            near_ref.at[pl.ds(row * near_count, near_count)],
            near_sems.at[row],
        )
        for row in range(blocks)
    ]
    for copy in copies[4:5] + near_copies[:1] + copies[:4] + near_copies[1:] + copies[5:]:
        copy.start()
    me = lax.axis_index("basis")
    my_low = lax.rem(me, LOW)
    my_high = lax.div(me, LOW)
    spread = LANES // LOW
    lane8 = lax.broadcasted_iota(jnp.int32, (8, LANES), 1)
    sub8 = lax.broadcasted_iota(jnp.int32, (8, LANES), 0)
    table = jnp.zeros((8, LANES), jnp.float32)
    counts = [jnp.int32(0)] * LOW
    for copy in copies[:5]:
        copy.wait()
    for row in range(blocks):
        real = adjoint_ref[pl.ds(2 * row, angles, stride=stride), :].astype(jnp.bfloat16)
        imag = adjoint_ref[pl.ds(2 * row + 1, angles, stride=stride), :].astype(jnp.bfloat16)
        left = complex_rows(real, imag)
        box = box_ref[row].astype(jnp.float32)
        near_copies[row].wait()
        for k in range(near_count):
            term = jnp.dot(left, near_ref[row * near_count + k], preferred_element_type=jnp.float32)
            device = col_device_ref[row, k]
            low = lax.bitwise_xor(lax.rem(device, LOW), my_low)
            high = lax.bitwise_xor(lax.div(device, LOW), my_high)
            place = high * blocks + col_offset_ref[row, k] + 1
            own_slot = jnp.int32(0)
            for e in range(LOW):
                here = low == e
                slot = jnp.where(here, jnp.minimum(counts[e], slots), slots)
                own_slot = jnp.where(here, counts[e], own_slot)
                counts[e] = counts[e] + here.astype(jnp.int32)
                message_refs[e][slot] = term
            entry = jnp.where(
                sub8 == 0, place.astype(jnp.float32), jnp.where(sub8 == 1, rate_ref[row, k], box)
            )
            table = jnp.where(lane8 == low * spread + own_slot, entry, table)
    for copy in copies[5:]:
        copy.wait()
    for row in range(blocks):
        for part in range(2):
            current_rows_ref[row, pl.ds(part * angles, angles), :] = currents_ref[
                pl.ds(2 * row + part, angles, stride=stride), :
            ]
    count = angles * blocks
    rad_real = radiation_ref[pl.ds(0, count, stride=2), :]
    rad_imag = radiation_ref[pl.ds(1, count, stride=2), :]
    cur_real = currents_ref[pl.ds(0, count, stride=2), :]
    cur_imag = currents_ref[pl.ds(1, count, stride=2), :]
    far_real = jnp.sum((rad_real * cur_real - rad_imag * cur_imag).reshape(angles, blocks, LANES), axis=1)
    far_imag = jnp.sum((rad_real * cur_imag + rad_imag * cur_real).reshape(angles, blocks, LANES), axis=1)
    lane = lax.broadcasted_iota(jnp.int32, (angles, LANES), 1)
    far = jnp.where(lane == 0, jnp.sum(far_real, axis=1, keepdims=True), 0.0) + jnp.where(
        lane == 1, jnp.sum(far_imag, axis=1, keepdims=True), 0.0
    )
    for e in range(LOW):
        message_refs[e][slots, pl.ds(0, angles), :] = far
        message_refs[e][slots, pl.ds(angles, 8), :] = jnp.where(lane8 // spread == e, table, 0.0)


def add_slots(message_refs, first, slots, tables, acc_ref, cur_ref, prod_ref, table_ref, place_ref, sem):
    spread = LANES // LOW
    table_ref[...] = tables.astype(jnp.int32)
    copy = pltpu.make_async_copy(table_ref, place_ref, sem)
    copy.start()
    prod_ref[...] = jnp.zeros(prod_ref.shape, jnp.float32)
    copy.wait()
    for i, message_ref in enumerate(message_refs):
        for s in range(slots):
            place = place_ref[0, (first + i) * spread + s]
            at = jnp.maximum(place - 1, 0)
            term = jnp.where(place > 0, message_ref[s], 0.0)
            acc_ref[at] = acc_ref[at] + term
            both = term * cur_ref[at]
            prod_ref[i * spread + s] = jnp.sum(both.reshape(-1, 8, LANES), axis=0)


def sum_first_kernel(slots, high_count, *refs):
    message_refs, current_refs = refs[: LOW // 2], refs[LOW // 2 : LOW // 2 + high_count]
    acc_ref, cur_ref, extra_ref, by_slot_ref, prod_ref, *tables = refs[LOW // 2 + high_count :]
    blocks, record = current_refs[0].shape[:2]
    extra = message_refs[0][slots]
    for message_ref in message_refs[1:]:
        extra = extra + message_ref[slots]
    for d in range(high_count):
        cur_ref[pl.ds(d * blocks, blocks)] = current_refs[d][...]
    acc_ref[...] = jnp.zeros(acc_ref.shape, jnp.float32)
    own = extra[record // 2 : record // 2 + 8]
    add_slots(message_refs, 0, slots, own, acc_ref, cur_ref, prod_ref, *tables)
    extra_ref[...] = extra
    by_slot_ref[...] = jnp.sum(prod_ref[...], axis=1)


def sum_last_kernel(slots, high_count, blocks, *refs):
    message_refs, refs = refs[: LOW // 2], refs[LOW // 2 :]
    (first_ref, cur_ref, first_extra_ref, first_by_slot_ref), refs = refs[:4], refs[4:]
    out_refs, (grad_ref, acc_ref, prod_ref, *tables) = refs[:high_count], refs[high_count:]
    record = cur_ref.shape[1]
    angles = record // 2
    extra = message_refs[0][slots]
    for message_ref in message_refs[1:]:
        extra = extra + message_ref[slots]
    own = extra[angles : angles + 8]
    extra = extra + first_extra_ref[...]
    acc_ref[...] = first_ref[...]
    add_slots(message_refs, LOW // 2, slots, own, acc_ref, cur_ref, prod_ref, *tables)
    for d in range(high_count):
        for b in range(blocks):
            out_refs[d][pl.ds(b * record, record), :] = acc_ref[d * blocks + b]
        out_refs[d][pl.ds(blocks * record, angles), :] = extra[:angles]
    table = extra[angles : angles + 8]
    by_slot = jnp.concatenate([first_by_slot_ref[...], jnp.sum(prod_ref[...], axis=1)], axis=0)
    by_pair = jnp.transpose(table)
    shares = by_pair[:, 1:2] * jnp.sum(by_slot, axis=1, keepdims=True)
    senders, boxes = grad_ref.shape
    number = lax.broadcasted_iota(jnp.int32, (LANES, boxes), 1).astype(jnp.float32)
    box_sums = jnp.sum(jnp.where(by_pair[:, 2:3] == number, shares, 0.0), axis=0, keepdims=True)
    grad_ref[...] = jnp.broadcast_to(box_sums, (senders, boxes))


def update_kernel(angles, norm_far, high_count, *refs):
    sum_refs = refs[:high_count]
    adjoint_ref, radiation_ref, inverse_ref, out_ref = refs[high_count:]
    blocks = inverse_ref.shape[0]
    stride = 2 * blocks
    record = 2 * angles

    def total(start, rows):
        return functools.reduce(jnp.add, [ref[pl.ds(start, rows), :] for ref in sum_refs])

    far = total(blocks * record, angles) * norm_far
    far_real = jnp.broadcast_to(far[:, 0:1], (angles, LANES))
    far_imag = jnp.broadcast_to(far[:, 1:2], (angles, LANES))
    for block in range(blocks):
        rows_real = pl.ds(2 * block, angles, stride=stride)
        rows_imag = pl.ds(2 * block + 1, angles, stride=stride)
        near = total(block * record, record)
        rad_real, rad_imag = radiation_ref[rows_real, :], radiation_ref[rows_imag, :]
        real = (far_real * rad_real + far_imag * rad_imag - near[:angles]).astype(jnp.bfloat16)
        imag = (far_imag * rad_real - far_real * rad_imag - near[angles:]).astype(jnp.bfloat16)
        step = jnp.dot(complex_rows(real, imag), inverse_ref[block], preferred_element_type=jnp.float32)
        out_ref[rows_real, :] = adjoint_ref[rows_real, :] + step[:angles]
        out_ref[rows_imag, :] = adjoint_ref[rows_imag, :] + step[angles:]


def on_device(
    adjoint,
    currents,
    radiation,
    near_blocks,
    inverse_blocks,
    col_device,
    col_offset,
    box_of_block,
    pair_rate,
):
    angles, blocks, unknowns = adjoint.shape[1], adjoint.shape[2], adjoint.shape[4]
    near_count = near_blocks.shape[1]
    pairs = blocks * near_count
    record = 2 * angles
    basis_count = lax.axis_size("basis")
    high_count = basis_count // LOW
    angles_all = angles * lax.axis_size("angle")
    boxes = BOX_DEV * basis_count
    slots = 2 * pairs // basis_count * high_count
    vmem = pl.BlockSpec(memory_space=pltpu.VMEM)
    params = pltpu.CompilerParams(vmem_limit_bytes=VMEM_LIMIT)

    def moved(value, bits):
        return lax.ppermute(value, "basis", [(i, i ^ bits) for i in range(basis_count)])

    flat = (angles * blocks * 2, unknowns)
    adjoint_rows = adjoint.reshape(flat)
    currents_rows = currents.reshape(flat)
    radiation_rows = radiation.reshape(flat)
    near = near_blocks.reshape(pairs, 2 * unknowns, unknowns)
    inverse = inverse_blocks.reshape(blocks, 2 * unknowns, unknowns)
    f32 = functools.partial(jax.ShapeDtypeStruct, dtype=jnp.float32)
    message = f32((slots + 1, record, unknowns))
    inputs = (
        col_device,
        col_offset,
        box_of_block,
        pair_rate,
        adjoint_rows,
        currents_rows,
        radiation_rows,
        near,
    )
    *messages, own_currents = pl.pallas_call(
        functools.partial(fill_kernel, slots),
        out_shape=[message] * LOW + [f32((blocks, record, unknowns))],
        in_specs=[pl.BlockSpec(memory_space=pltpu.HBM)] * len(inputs),
        out_specs=[vmem] * (LOW + 1),
        scratch_shapes=[pltpu.SMEM(whole.shape, whole.dtype) for whole in inputs[:4]]
        + [pltpu.VMEM(whole.shape, whole.dtype) for whole in inputs[4:]]
        + [pltpu.SemaphoreType.DMA((7,)), pltpu.SemaphoreType.DMA((blocks,))],
        compiler_params=params,
        name="fill",
    )(*[pltpu.with_memory_space_constraint(whole, pltpu.HBM) for whole in inputs])
    arrived = [messages[0]] + [moved(messages[e], e) for e in range(1, LOW)]
    beside = [own_currents] + [moved(own_currents, d * LOW) for d in range(1, high_count)]
    columns = f32((high_count * blocks, record, unknowns))
    half = LANES // 2
    tables = [
        pltpu.VMEM((half, 8, unknowns), jnp.float32),
        pltpu.VMEM((8, LANES), jnp.int32),
        pltpu.SMEM((8, LANES), jnp.int32),
        pltpu.SemaphoreType.DMA,
    ]
    first_sums = pl.pallas_call(
        functools.partial(sum_first_kernel, slots, high_count),
        out_shape=[columns, columns, f32((record, unknowns)), f32((half, unknowns))],
        in_specs=[vmem] * (LOW // 2 + high_count),
        out_specs=[vmem] * 4,
        scratch_shapes=tables,
        compiler_params=params,
        name="sum_first",
    )(*arrived[: LOW // 2], *beside)
    partial = f32((blocks * record + angles, unknowns))
    box_lanes = -(-boxes // LANES) * LANES
    everyone = ("basis", "pol")
    senders = basis_count * lax.axis_size("pol")
    *sums, grad = pl.pallas_call(
        functools.partial(sum_last_kernel, slots, high_count, blocks),
        out_shape=[partial] * high_count + [f32((senders, box_lanes))],
        in_specs=[vmem] * (LOW // 2 + 4),
        out_specs=[vmem] * (high_count + 1),
        scratch_shapes=[pltpu.VMEM(columns.shape, jnp.float32)] + tables,
        compiler_params=params,
        name="sum_last",
    )(*arrived[LOW // 2 :], *first_sums)
    totals = [sums[0]] + [moved(sums[d], d * LOW) for d in range(1, high_count)]
    norm_far = 1.0 / math.sqrt(blocks * basis_count * unknowns)
    updated = pl.pallas_call(
        functools.partial(update_kernel, angles, norm_far, high_count),
        out_shape=f32(flat),
        in_specs=[vmem] * (high_count + 3),
        out_specs=vmem,
        compiler_params=params,
        name="update",
    )(*totals, adjoint_rows, radiation_rows, inverse)
    grad = grad.reshape(senders, 1, box_lanes)
    gathered = lax.all_to_all(grad, everyone, split_axis=0, concat_axis=0)
    gathered, updated = lax.optimization_barrier((gathered, updated))
    total_grad = jnp.sum(gathered[:, 0], axis=0)
    if lax.axis_size("angle") > 1:
        total_grad = lax.psum(total_grad, "angle")
    share = lax.dynamic_slice_in_dim(total_grad, lax.axis_index("basis") * BOX_DEV, BOX_DEV)
    shape_grad = share * (-1.0 / math.sqrt(4 * unknowns * angles_all * near_count))
    return (updated.reshape(adjoint.shape), shape_grad)


def solution(mesh):
    placed = (
        P("pol", "angle", "basis", None, None),
        P("pol", "angle", "basis", None, None),
        P("pol", "angle", "basis", None, None),
        P("basis", None, None, None, None),
        P("basis", None, None, None),
        P("basis", None),
        P("basis", None),
        P("basis"),
        P("basis", None),
    )
    return jax.shard_map(
        on_device,
        mesh=mesh,
        in_specs=placed,
        out_specs=(P("pol", "angle", "basis", None, None), P("basis")),
        check_vma=False,
    )
```

time: 58.4 us -> 45.5 us (0.78)
  local copies, waits for them, and re-layouts: 7.32 us -> 0.01 us
  waiting for transfers between devices: 19.2 us -> 14.8 us
  starting transfers between devices: 25.6 us -> 22.6 us
  Pallas kernels: 4.65 us -> 6.55 us
    ppermute x15 -> x9, starting transfers between devices: 25.6 us -> 17.7 us  [moved(): lax.ppermute(value, 'basis', [(i, i ^ bits) for i in range(basis_count)])]
    unnamed x22 -> x6, local copies, waits for them, and re-layouts: 7.32 us -> 0.01 us
    all_to_all x0 -> x1, starting transfers between devices: none -> 4.93 us  [on_device(): gathered = lax.all_to_all(grad, everyone, split_axis=0, concat_axis=0)]
    ppermute x15 -> x9, waiting for transfers between devices: 18.1 us -> 13.2 us  [moved(): lax.ppermute(value, 'basis', [(i, i ^ bits) for i in range(basis_count)])]
    pallas_call x3 -> x4, Pallas kernels: 4.65 us -> 6.55 us  [the longest x1 2.94 us: on_device(): pl.pallas_call(functools.partial(fill_kernel, slots), out_shape=[message]...]
    all_to_all x0 -> x1, waiting for transfers between devices: none -> 1.57 us  [on_device(): gathered = lax.all_to_all(grad, everyone, split_axis=0, concat_axis=0)]
    ppermute x1 -> x0, waiting for transfers between devices: 1.16 us -> none  [on_device(): lax.ppermute(grad, axis, [(i, i ^ b) for i in range(size)])]
  transfers between devices with their start and end apart: 16 -> 10, of which waited for: 9 -> 5; matrix products, arithmetic and copies ran while one was open for 1% -> 0% of each run, Pallas kernels for 0% -> 4%
where the time goes in v3:
time: 45.5 us; the launch traced here: 45.4 us
  starting transfers between devices  22.6 us (50%)
  waiting for transfers between devices  14.8 us (33%)
  Pallas kernels  6.55 us (14%)
  between operations  0.72 us (2%)
  other arithmetic  0.64 us (1%)
    ppermute x9, starting transfers between devices, moved(): lax.ppermute(value, 'basis', [(i, i ^ bits) for i in range(basis_count)])  17.7 us
    ppermute x9, waiting for transfers between devices, moved(): lax.ppermute(value, 'basis', [(i, i ^ bits) for i in range(basis_count)])  13.2 us
    all_to_all x1, starting transfers between devices, on_device(): gathered = lax.all_to_all(grad, everyone, split_axis=0, concat_axis=0)  4.93 us
    pallas_call x1, Pallas kernels, on_device(): pl.pallas_call(functools.partial(fill_kernel, slots), out_shape=[message]...  2.94 us
    pallas_call x1, Pallas kernels, on_device(): pl.pallas_call(functools.partial(sum_last_kernel, slots, high_count, bloc...  1.68 us
    all_to_all x1, waiting for transfers between devices, on_device(): gathered = lax.all_to_all(grad, everyone, split_axis=0, concat_axis=0)  1.57 us
    pallas_call x1, Pallas kernels, on_device(): pl.pallas_call(functools.partial(sum_first_kernel, slots, high_count), ou...  0.96 us
    pallas_call x1, Pallas kernels, on_device(): pl.pallas_call(functools.partial(update_kernel, angles, norm_far, high_co...  0.96 us
  transfers between devices with their start and end apart: 10, of which 5 were waited for; matrix products, arithmetic and copies ran while one was open for 0% of the time, Pallas kernels for 4%

profile of v3, /device:TPU:0, one launch (start us, length us, event | category | flops | bytes accessed | tf_op | source)
XLA Modules:
  0.0 45.4 jit_solution(7093957458464674803)
XLA Ops:
  0.6 0.0 copy-start
  0.6 0.0 copy-start.1
  0.7 0.0 copy-start.2
  0.7 2.9 %fill.1 = (f32[25,32,128]{2,1,0:T(8,128)S(1)}, f32[25,32,128]{2,1,0:T(8,128)S(1)}, f32[25,32,128]{2,1,0:T(8,128)S(1)}, f32[25,32,128]{2,1,0:T(8,128)S(1)}, f32[8,32,128]{2,1,0:T(8,128)S(1)}) custom-call(s32[8,6]{1,0:T(8,128)} %refs_0_.1, s32[8,6]{1,0:T(8,128)} %refs_1_.1, s32[8]{0:T(128)} %refs_2_.1, f32[8,6]{1,0:T(8,128)} %refs_3_.1, f32[256,128]{1,0:T(8,128)} %bitcast.10, ...), custom_call_target="tpu_custom_call" | custom-call | tf_op jit(solution)/shard_map/fill/pallas_call | solution.py:235
  3.6 3.0 %collective-permute-start.2 = (f32[25,32,128]{2,1,0:T(8,128)S(1)}, f32[25,32,128]{2,1,0:T(8,128)S(1)}, u32[]{:S(2)}, u32[]{:S(2)}) collective-permute-start(f32[25,32,128]{2,1,0:T(8,128)S(1)} %get-tuple-element.21), channel_id=1, source_target_pairs={{0,2},{2,0},{4,6},{6,4},{8,10},{10,8},{12,14},{14,12},{16,18},{18,... | collective-permute-start | bytes 1228808 | tf_op jit(solution)/shard_map/ppermute | solution.py:215
  6.6 1.5 %collective-permute-start = (f32[25,32,128]{2,1,0:T(8,128)S(1)}, f32[25,32,128]{2,1,0:T(8,128)S(1)}, u32[]{:S(2)}, u32[]{:S(2)}) collective-permute-start(f32[25,32,128]{2,1,0:T(8,128)S(1)} %get-tuple-element.18), channel_id=1, source_target_pairs={{0,4},{2,6},{4,0},{6,2},{8,12},{10,14},{12,8},{14,10},{16,20},{18,... | collective-permute-start | bytes 1228808 | tf_op jit(solution)/shard_map/ppermute | solution.py:215
  8.1 0.0 collective-permute-start.1
  8.2 2.0 %collective-permute-start.3 = (f32[8,32,128]{2,1,0:T(8,128)S(1)}, f32[8,32,128]{2,1,0:T(8,128)S(1)}, u32[]{:S(2)}, u32[]{:S(2)}) collective-permute-start(f32[8,32,128]{2,1,0:T(8,128)S(1)} %get-tuple-element.22.refs_2_), channel_id=1, source_target_pairs={{0,8},{2,10},{4,12},{6,14},{8,0},{10,2},{12,4},{14,6},{16,24},{18,... | collective-permute-start | bytes 393224 | tf_op jit(solution)/shard_map/ppermute | solution.py:215
  10.2 2.6 %collective-permute-start.4 = (f32[8,32,128]{2,1,0:T(8,128)S(1)}, f32[8,32,128]{2,1,0:T(8,128)S(1)}, u32[]{:S(2)}, u32[]{:S(2)}) collective-permute-start(f32[8,32,128]{2,1,0:T(8,128)S(1)} %get-tuple-element.22.refs_2_), channel_id=1, source_target_pairs={{0,16},{2,18},{4,20},{6,22},{8,24},{10,26},{12,28},{14,30},{16,0},... | collective-permute-start | bytes 393224 | tf_op jit(solution)/shard_map/ppermute | solution.py:215
  12.8 1.6 %collective-permute-done.3.refs_3_ = f32[8,32,128]{2,1,0:T(8,128)S(1)} collective-permute-done((f32[8,32,128]{2,1,0:T(8,128)S(1)}, f32[8,32,128]{2,1,0:T(8,128)S(1)}, u32[]{:S(2)}, u32[]{:S(2)}) %collective-permute-start.3) | collective-permute-done | bytes 131104 | tf_op jit(solution)/shard_map/ppermute | solution.py:215
  14.4 4.1 %collective-permute-start.5 = (f32[8,32,128]{2,1,0:T(8,128)S(1)}, f32[8,32,128]{2,1,0:T(8,128)S(1)}, u32[]{:S(2)}, u32[]{:S(2)}) collective-permute-start(f32[8,32,128]{2,1,0:T(8,128)S(1)} %get-tuple-element.22.refs_2_), channel_id=1, source_target_pairs={{0,24},{2,26},{4,28},{6,30},{8,16},{10,18},{12,20},{14,22},{16,8},... | collective-permute-start | bytes 393224 | tf_op jit(solution)/shard_map/ppermute | solution.py:215
  18.5 3.4 %collective-permute-done.4.refs_4_ = f32[8,32,128]{2,1,0:T(8,128)S(1)} collective-permute-done((f32[8,32,128]{2,1,0:T(8,128)S(1)}, f32[8,32,128]{2,1,0:T(8,128)S(1)}, u32[]{:S(2)}, u32[]{:S(2)}) %collective-permute-start.4) | collective-permute-done | bytes 131104 | tf_op jit(solution)/shard_map/ppermute | solution.py:215
  21.9 0.0 collective-permute-done.5.refs_5_
  21.9 0.0 collective-permute-done.2.refs_1_
  21.9 1.0 %sum_first.1 = (f32[32,32,128]{2,1,0:T(8,128)S(1)}, f32[32,32,128]{2,1,0:T(8,128)S(1)}, f32[32,128]{1,0:T(8,128)S(1)}, f32[64,128]{1,0:T(8,128)S(1)}) custom-call(f32[25,32,128]{2,1,0:T(8,128)S(1)} %get-tuple-element.20.refs_0_, f32[25,32,128]{2,1,0:T(8,128)S(1)} %collective-permute-done.2.refs_1_, f32[8,32,128]{2,1,0:T(8,128)S(1)} %get-tuple-element.22.refs_2_, ...), custom_call_target="tpu_custom_call" | custom-call | tf_op jit(solution)/shard_map/sum_first/pallas_call | solution.py:256
  22.9 3.4 %collective-permute-done.refs_0_ = f32[25,32,128]{2,1,0:T(8,128)S(1)} collective-permute-done((f32[25,32,128]{2,1,0:T(8,128)S(1)}, f32[25,32,128]{2,1,0:T(8,128)S(1)}, u32[]{:S(2)}, u32[]{:S(2)}) %collective-permute-start) | collective-permute-done | bytes 409632 | tf_op jit(solution)/shard_map/ppermute | solution.py:215
  26.3 0.0 collective-permute-done.1.refs_1_
  26.3 1.7 %sum_last.1 = (f32[272,128]{1,0:T(8,128)S(1)}, f32[272,128]{1,0:T(8,128)S(1)}, f32[272,128]{1,0:T(8,128)S(1)}, f32[272,128]{1,0:T(8,128)S(1)}, f32[32,128]{1,0:T(8,128)}) custom-call(f32[25,32,128]{2,1,0:T(8,128)S(1)} %collective-permute-done.refs_0_, f32[25,32,128]{2,1,0:T(8,128)S(1)} %collective-permute-done.1.refs_1_, ...), custom_call_target="tpu_custom_call" | custom-call | tf_op jit(solution)/shard_map/sum_last/pallas_call | solution.py:269
  28.0 1.6 %collective-permute-start.6 = (f32[272,128]{1,0:T(8,128)S(1)}, f32[272,128]{1,0:T(8,128)S(1)}, u32[]{:S(2)}, u32[]{:S(2)}) collective-permute-start(f32[272,128]{1,0:T(8,128)S(1)} %get-tuple-element.29), channel_id=1, source_target_pairs={{0,8},{2,10},{4,12},{6,14},{8,0},{10,2},{12,4},{14,6},{16,24},{18,... | collective-permute-start | bytes 417800 | tf_op jit(solution)/shard_map/ppermute | solution.py:215
  29.7 2.6 %collective-permute-start.7 = (f32[272,128]{1,0:T(8,128)S(1)}, f32[272,128]{1,0:T(8,128)S(1)}, u32[]{:S(2)}, u32[]{:S(2)}) collective-permute-start(f32[272,128]{1,0:T(8,128)S(1)} %get-tuple-element.30), channel_id=1, source_target_pairs={{0,16},{2,18},{4,20},{6,22},{8,24},{10,26},{12,28},{14,30},{16,0},... | collective-permute-start | bytes 417800 | tf_op jit(solution)/shard_map/ppermute | solution.py:215
  32.2 0.2 collective-permute-start.8
  32.5 4.9 %all-to-all-start = ((f32[32,1,128]{2,1,0:T(1,128)}), f32[32,1,128]{2,1,0:T(1,128)S(1)}, u32[]{:S(2)}, u32[]{:S(2)}) async-start(f32[32,1,128]{2,1,0:T(1,128)} %bitcast.5), calls=%async_computation | async-start | bytes 32768 | tf_op jit(solution)/shard_map/all_to_all | solution.py:289
  37.4 0.0 collective-permute-done.6.refs_1_
  37.4 4.7 %collective-permute-done.7.refs_2_ = f32[272,128]{1,0:T(8,128)S(1)} collective-permute-done((f32[272,128]{1,0:T(8,128)S(1)}, f32[272,128]{1,0:T(8,128)S(1)}, u32[]{:S(2)}, u32[]{:S(2)}) %collective-permute-start.7) | collective-permute-done | bytes 139296 | tf_op jit(solution)/shard_map/ppermute | solution.py:215
  42.2 0.0 collective-permute-done.8.refs_3_
  42.2 0.0 copy-done
  42.2 0.0 copy-done.1
  42.2 0.0 copy-done.2
  42.2 1.0 %update.1 = f32[256,128]{1,0:T(8,128)} custom-call(f32[272,128]{1,0:T(8,128)S(1)} %get-tuple-element.28.refs_0_, f32[272,128]{1,0:T(8,128)S(1)} %collective-permute-done.6.refs_1_, f32[272,128]{1,0:T(8,128)S(1)} %collective-permute-done.7.refs_2_, f32[272,128]{1,0:T(8,128)S(1)} %collective-permute-done.8.refs_3_, f32[256,128]{1,0:T(8,128)S(1)} %bitcast.11, ...), custom_call_target="tpu_custom_call" | custom-call | tf_op jit(solution)/shard_map/update/pallas_call | solution.py:280
  43.1 1.6 %all-to-all-done = f32[32,1,128]{2,1,0:T(1,128)S(1)} async-done(((f32[32,1,128]{2,1,0:T(1,128)}), f32[32,1,128]{2,1,0:T(1,128)S(1)}, u32[]{:S(2)}, u32[]{:S(2)}) %all-to-all-start) | async-done | bytes 16416 | tf_op jit(solution)/shard_map/all_to_all | solution.py:289
  44.7 0.1 reduce_sum.9
  44.8 0.6 %dynamic-slice_multiply_fusion = f32[4]{0:T(128)} fusion(f32[128]{0:T(128)S(1)} %reduce_sum.9, s32[]{:T(128)S(6)} %select_n.3), kind=kLoop, calls=%fused_computation | loop fusion | flops 4 | bytes 36 | tf_op jit(solution)/shard_map/mul | solution.py:295
Async XLA Ops:
  0.6 41.5 %copy-start = (bf16[8,2,128,128]{3,2,1,0:T(8,128)(2,1)S(1)}, bf16[8,2,128,128]{3,2,1,0:T(8,128)(2,1)}, u32[]{:S(2)}) copy-start(bf16[8,2,128,128]{3,2,1,0:T(8,128)(2,1)} %param.13) | copy-start | bytes 1572868
  0.6 41.5 %copy-start.1 = (f32[1,16,8,2,128]{4,3,2,1,0:T(2,128)S(1)}, f32[1,16,8,2,128]{4,3,2,1,0:T(2,128)}, u32[]{:S(2)}) copy-start(f32[1,16,8,2,128]{4,3,2,1,0:T(2,128)} %param.9) | copy-start | bytes 393220
  0.7 41.5 %copy-start.2 = (f32[1,16,8,2,128]{4,3,2,1,0:T(2,128)S(1)}, f32[1,16,8,2,128]{4,3,2,1,0:T(2,128)}, u32[]{:S(2)}) copy-start(f32[1,16,8,2,128]{4,3,2,1,0:T(2,128)} %param.11) | copy-start | bytes 393220
  3.6 18.3 %collective-permute-start.2 = (f32[25,32,128]{2,1,0:T(8,128)S(1)}, f32[25,32,128]{2,1,0:T(8,128)S(1)}, u32[]{:S(2)}, u32[]{:S(2)}) collective-permute-start(f32[25,32,128]{2,1,0:T(8,128)S(1)} %get-tuple-element.21), channel_id=1, source_target_pairs={{0,2},{2,0},{4,6},{6,4},{8,10},{10,8},{12,14},{14,12},{16,18},{18,... | collective-permute-start | bytes 1228808 | tf_op jit(solution)/shard_map/ppermute | solution.py:215
  6.6 19.7 %collective-permute-start = (f32[25,32,128]{2,1,0:T(8,128)S(1)}, f32[25,32,128]{2,1,0:T(8,128)S(1)}, u32[]{:S(2)}, u32[]{:S(2)}) collective-permute-start(f32[25,32,128]{2,1,0:T(8,128)S(1)} %get-tuple-element.18), channel_id=1, source_target_pairs={{0,4},{2,6},{4,0},{6,2},{8,12},{10,14},{12,8},{14,10},{16,20},{18,... | collective-permute-start | bytes 1228808 | tf_op jit(solution)/shard_map/ppermute | solution.py:215
  8.1 18.2 %collective-permute-start.1 = (f32[25,32,128]{2,1,0:T(8,128)S(1)}, f32[25,32,128]{2,1,0:T(8,128)S(1)}, u32[]{:S(2)}, u32[]{:S(2)}) collective-permute-start(f32[25,32,128]{2,1,0:T(8,128)S(1)} %get-tuple-element.19), channel_id=1, source_target_pairs={{0,6},{2,4},{4,2},{6,0},{8,14},{10,12},{12,10},{14,8},{16,22},{18,... | collective-permute-start | bytes 1228808 | tf_op jit(solution)/shard_map/ppermute | solution.py:215
  8.2 6.3 %collective-permute-start.3 = (f32[8,32,128]{2,1,0:T(8,128)S(1)}, f32[8,32,128]{2,1,0:T(8,128)S(1)}, u32[]{:S(2)}, u32[]{:S(2)}) collective-permute-start(f32[8,32,128]{2,1,0:T(8,128)S(1)} %get-tuple-element.22.refs_2_), channel_id=1, source_target_pairs={{0,8},{2,10},{4,12},{6,14},{8,0},{10,2},{12,4},{14,6},{16,24},{18,... | collective-permute-start | bytes 393224 | tf_op jit(solution)/shard_map/ppermute | solution.py:215
  10.2 11.7 %collective-permute-start.4 = (f32[8,32,128]{2,1,0:T(8,128)S(1)}, f32[8,32,128]{2,1,0:T(8,128)S(1)}, u32[]{:S(2)}, u32[]{:S(2)}) collective-permute-start(f32[8,32,128]{2,1,0:T(8,128)S(1)} %get-tuple-element.22.refs_2_), channel_id=1, source_target_pairs={{0,16},{2,18},{4,20},{6,22},{8,24},{10,26},{12,28},{14,30},{16,0},... | collective-permute-start | bytes 393224 | tf_op jit(solution)/shard_map/ppermute | solution.py:215
  14.4 7.5 %collective-permute-start.5 = (f32[8,32,128]{2,1,0:T(8,128)S(1)}, f32[8,32,128]{2,1,0:T(8,128)S(1)}, u32[]{:S(2)}, u32[]{:S(2)}) collective-permute-start(f32[8,32,128]{2,1,0:T(8,128)S(1)} %get-tuple-element.22.refs_2_), channel_id=1, source_target_pairs={{0,24},{2,26},{4,28},{6,30},{8,16},{10,18},{12,20},{14,22},{16,8},... | collective-permute-start | bytes 393224 | tf_op jit(solution)/shard_map/ppermute | solution.py:215
  28.0 9.4 %collective-permute-start.6 = (f32[272,128]{1,0:T(8,128)S(1)}, f32[272,128]{1,0:T(8,128)S(1)}, u32[]{:S(2)}, u32[]{:S(2)}) collective-permute-start(f32[272,128]{1,0:T(8,128)S(1)} %get-tuple-element.29), channel_id=1, source_target_pairs={{0,8},{2,10},{4,12},{6,14},{8,0},{10,2},{12,4},{14,6},{16,24},{18,... | collective-permute-start | bytes 417800 | tf_op jit(solution)/shard_map/ppermute | solution.py:215
  29.7 12.5 %collective-permute-start.7 = (f32[272,128]{1,0:T(8,128)S(1)}, f32[272,128]{1,0:T(8,128)S(1)}, u32[]{:S(2)}, u32[]{:S(2)}) collective-permute-start(f32[272,128]{1,0:T(8,128)S(1)} %get-tuple-element.30), channel_id=1, source_target_pairs={{0,16},{2,18},{4,20},{6,22},{8,24},{10,26},{12,28},{14,30},{16,0},... | collective-permute-start | bytes 417800 | tf_op jit(solution)/shard_map/ppermute | solution.py:215
  32.2 9.9 %collective-permute-start.8 = (f32[272,128]{1,0:T(8,128)S(1)}, f32[272,128]{1,0:T(8,128)S(1)}, u32[]{:S(2)}, u32[]{:S(2)}) collective-permute-start(f32[272,128]{1,0:T(8,128)S(1)} %get-tuple-element.31), channel_id=1, source_target_pairs={{0,24},{2,26},{4,28},{6,30},{8,16},{10,18},{12,20},{14,22},{16,8},... | collective-permute-start | bytes 417800 | tf_op jit(solution)/shard_map/ppermute | solution.py:215
  32.5 12.3 %all-to-all-start = ((f32[32,1,128]{2,1,0:T(1,128)}), f32[32,1,128]{2,1,0:T(1,128)S(1)}, u32[]{:S(2)}, u32[]{:S(2)}) async-start(f32[32,1,128]{2,1,0:T(1,128)} %bitcast.5), calls=%async_computation | async-start | bytes 32768 | tf_op jit(solution)/shard_map/all_to_all | solution.py:289

commit v4 on v3

--- a/solution.py
+++ b/solution.py
@@ -11,6 +11,7 @@
 LOW = 4
 LANES = 128
 BOX_DEV = 4
+FAR_ROW = 3
 VMEM_LIMIT = 48 * 1024 * 1024
 
 
@@ -22,7 +23,7 @@
 
 def fill_kernel(slots, *refs):
     whole_refs, message_refs, current_rows_ref = refs[:8], refs[8 : 8 + LOW], refs[8 + LOW]
-    *held_refs, sems, near_sems = refs[9 + LOW :]
+    *held_refs, buffer_ref, sems, near_sems = refs[9 + LOW :]
     (
         col_device_ref,
         col_offset_ref,
@@ -36,6 +37,7 @@
     blocks, near_count = col_device_ref.shape
     stride = 2 * blocks
     angles = adjoint_ref.shape[0] // stride
+    record = 2 * angles
     copies = [pltpu.make_async_copy(whole_refs[i], held_refs[i], sems.at[i]) for i in range(7)]
     near_copies = [
         pltpu.make_async_copy(
@@ -63,23 +65,26 @@
         left = complex_rows(real, imag)
         box = box_ref[row].astype(jnp.float32)
         near_copies[row].wait()
-        for k in range(near_count):
-            term = jnp.dot(left, near_ref[row * near_count + k], preferred_element_type=jnp.float32)
-            device = col_device_ref[row, k]
-            low = lax.bitwise_xor(lax.rem(device, LOW), my_low)
-            high = lax.bitwise_xor(lax.div(device, LOW), my_high)
-            place = high * blocks + col_offset_ref[row, k] + 1
-            own_slot = jnp.int32(0)
-            for e in range(LOW):
-                here = low == e
-                slot = jnp.where(here, jnp.minimum(counts[e], slots), slots)
-                own_slot = jnp.where(here, counts[e], own_slot)
-                counts[e] = counts[e] + here.astype(jnp.int32)
-                message_refs[e][slot] = term
-            entry = jnp.where(
-                sub8 == 0, place.astype(jnp.float32), jnp.where(sub8 == 1, rate_ref[row, k], box)
-            )
-            table = jnp.where(lane8 == low * spread + own_slot, entry, table)
+        for first in range(0, near_count, 1):
+            some = range(first, min(first + 1, near_count))
+            right = jnp.concatenate([near_ref[row * near_count + k] for k in some], axis=1)
+            terms = jnp.dot(left, right, preferred_element_type=jnp.float32)
+            for k in some:
+                device = col_device_ref[row, k]
+                low = lax.bitwise_xor(lax.rem(device, LOW), my_low)
+                high = lax.bitwise_xor(lax.div(device, LOW), my_high)
+                place = high * blocks + col_offset_ref[row, k] + 1
+                slot = jnp.int32(0)
+                for e in range(LOW):
+                    here = low == e
+                    slot = jnp.where(here, counts[e], slot)
+                    counts[e] = counts[e] + here.astype(jnp.int32)
+                slot = jnp.minimum(slot, slots - 1)
+                buffer_ref[low * slots + slot] = terms[:, (k - first) * LANES : (k - first + 1) * LANES]
+                entry = jnp.where(
+                    sub8 == 0, place.astype(jnp.float32), jnp.where(sub8 == 1, rate_ref[row, k], box)
+                )
+                table = jnp.where(lane8 == low * spread + slot, entry, table)
     for copy in copies[5:]:
         copy.wait()
     for row in range(blocks):
@@ -95,72 +100,71 @@
     far_real = jnp.sum((rad_real * cur_real - rad_imag * cur_imag).reshape(angles, blocks, LANES), axis=1)
     far_imag = jnp.sum((rad_real * cur_imag + rad_imag * cur_real).reshape(angles, blocks, LANES), axis=1)
     lane = lax.broadcasted_iota(jnp.int32, (angles, LANES), 1)
-    far = jnp.where(lane == 0, jnp.sum(far_real, axis=1, keepdims=True), 0.0) + jnp.where(
-        lane == 1, jnp.sum(far_imag, axis=1, keepdims=True), 0.0
-    )
+    angle = lax.broadcasted_iota(jnp.int32, (angles, LANES), 0)
+    far = jnp.where(lane == angle, jnp.sum(far_real, axis=1, keepdims=True), 0.0) + jnp.where(
+        lane == angle + angles, jnp.sum(far_imag, axis=1, keepdims=True), 0.0
+    )
+    far = jnp.broadcast_to(jnp.sum(far, axis=0, keepdims=True), (8, LANES))
     for e in range(LOW):
-        message_refs[e][slots, pl.ds(0, angles), :] = far
-        message_refs[e][slots, pl.ds(angles, 8), :] = jnp.where(lane8 // spread == e, table, 0.0)
-
-
-def add_slots(message_refs, first, slots, tables, acc_ref, cur_ref, prod_ref, table_ref, place_ref, sem):
+        for s in range(slots):
+            message_refs[e][pl.ds(s * record, record), :] = buffer_ref[e * slots + s]
+        mine = jnp.where(lane8 // spread == e, table, 0.0)
+        message_refs[e][pl.ds(slots * record, 8), :] = jnp.where(sub8 == FAR_ROW, far, mine)
+
+
+def add_slots(message_refs, first, slots, boxes, table, scratch_refs):
+    acc_ref, cur_ref, prod_ref, table_ref, place_ref, sem = scratch_refs
     spread = LANES // LOW
-    table_ref[...] = tables.astype(jnp.int32)
+    record = cur_ref.shape[1]
+    table_ref[...] = table.astype(jnp.int32)
     copy = pltpu.make_async_copy(table_ref, place_ref, sem)
     copy.start()
     prod_ref[...] = jnp.zeros(prod_ref.shape, jnp.float32)
+    count = len(message_refs) * spread
+    by_pair = jnp.transpose(table)[first * spread : first * spread + count]
+    number = lax.broadcasted_iota(jnp.int32, (count, boxes), 1).astype(jnp.float32)
+    rates = jnp.where(by_pair[:, 2:3] == number, by_pair[:, 1:2], 0.0)
     copy.wait()
     for i, message_ref in enumerate(message_refs):
         for s in range(slots):
             place = place_ref[0, (first + i) * spread + s]
             at = jnp.maximum(place - 1, 0)
-            term = jnp.where(place > 0, message_ref[s], 0.0)
+            term = jnp.where(place > 0, message_ref[pl.ds(s * record, record), :], 0.0)
             acc_ref[at] = acc_ref[at] + term
             both = term * cur_ref[at]
             prod_ref[i * spread + s] = jnp.sum(both.reshape(-1, 8, LANES), axis=0)
+    by_slot = jnp.sum(jnp.sum(prod_ref[...], axis=1), axis=1, keepdims=True)
+    return jnp.sum((rates * by_slot).reshape(count // 8, 8, boxes), axis=0)
 
 
 def sum_first_kernel(slots, high_count, *refs):
     message_refs, current_refs = refs[: LOW // 2], refs[LOW // 2 : LOW // 2 + high_count]
-    acc_ref, cur_ref, extra_ref, by_slot_ref, prod_ref, *tables = refs[LOW // 2 + high_count :]
+    acc_ref, cur_ref, extra_ref, share_ref, *scratch_refs = refs[LOW // 2 + high_count :]
     blocks, record = current_refs[0].shape[:2]
-    extra = message_refs[0][slots]
-    for message_ref in message_refs[1:]:
-        extra = extra + message_ref[slots]
+    extra = functools.reduce(jnp.add, [ref[pl.ds(slots * record, 8), :] for ref in message_refs])
     for d in range(high_count):
         cur_ref[pl.ds(d * blocks, blocks)] = current_refs[d][...]
     acc_ref[...] = jnp.zeros(acc_ref.shape, jnp.float32)
-    own = extra[record // 2 : record // 2 + 8]
-    add_slots(message_refs, 0, slots, own, acc_ref, cur_ref, prod_ref, *tables)
+    share_ref[...] = add_slots(message_refs, 0, slots, share_ref.shape[1], extra, (acc_ref, cur_ref, *scratch_refs))
     extra_ref[...] = extra
-    by_slot_ref[...] = jnp.sum(prod_ref[...], axis=1)
 
 
 def sum_last_kernel(slots, high_count, blocks, *refs):
     message_refs, refs = refs[: LOW // 2], refs[LOW // 2 :]
-    (first_ref, cur_ref, first_extra_ref, first_by_slot_ref), refs = refs[:4], refs[4:]
-    out_refs, (grad_ref, acc_ref, prod_ref, *tables) = refs[:high_count], refs[high_count:]
+    (first_ref, cur_ref, first_extra_ref, first_share_ref), refs = refs[:4], refs[4:]
+    out_refs, (grad_ref, acc_ref, *scratch_refs) = refs[:high_count], refs[high_count:]
     record = cur_ref.shape[1]
-    angles = record // 2
-    extra = message_refs[0][slots]
-    for message_ref in message_refs[1:]:
-        extra = extra + message_ref[slots]
-    own = extra[angles : angles + 8]
+    extra = functools.reduce(jnp.add, [ref[pl.ds(slots * record, 8), :] for ref in message_refs])
+    acc_ref[...] = first_ref[...]
+    share = add_slots(message_refs, LOW // 2, slots, grad_ref.shape[2], extra, (acc_ref, cur_ref, *scratch_refs))
+    box_sums = jnp.sum(share + first_share_ref[...], axis=0, keepdims=True)
+    grad_ref[...] = jnp.broadcast_to(box_sums[None], grad_ref.shape)
     extra = extra + first_extra_ref[...]
-    acc_ref[...] = first_ref[...]
-    add_slots(message_refs, LOW // 2, slots, own, acc_ref, cur_ref, prod_ref, *tables)
     for d in range(high_count):
         for b in range(blocks):
             out_refs[d][pl.ds(b * record, record), :] = acc_ref[d * blocks + b]
-        out_refs[d][pl.ds(blocks * record, angles), :] = extra[:angles]
-    table = extra[angles : angles + 8]
-    by_slot = jnp.concatenate([first_by_slot_ref[...], jnp.sum(prod_ref[...], axis=1)], axis=0)
-    by_pair = jnp.transpose(table)
-    shares = by_pair[:, 1:2] * jnp.sum(by_slot, axis=1, keepdims=True)
-    senders, boxes = grad_ref.shape
-    number = lax.broadcasted_iota(jnp.int32, (LANES, boxes), 1).astype(jnp.float32)
-    box_sums = jnp.sum(jnp.where(by_pair[:, 2:3] == number, shares, 0.0), axis=0, keepdims=True)
-    grad_ref[...] = jnp.broadcast_to(box_sums, (senders, boxes))
+        for row in range(blocks * record, out_refs[d].shape[0], 8):
+            out_refs[d][pl.ds(row, 8), :] = extra
 
 
 def update_kernel(angles, norm_far, high_count, *refs):
@@ -173,9 +177,13 @@
     def total(start, rows):
         return functools.reduce(jnp.add, [ref[pl.ds(start, rows), :] for ref in sum_refs])
 
-    far = total(blocks * record, angles) * norm_far
-    far_real = jnp.broadcast_to(far[:, 0:1], (angles, LANES))
-    far_imag = jnp.broadcast_to(far[:, 1:2], (angles, LANES))
+    far = total(blocks * record, 8)[FAR_ROW : FAR_ROW + 1] * norm_far
+    lane = lax.broadcasted_iota(jnp.int32, (angles, LANES), 1)
+    angle = lax.broadcasted_iota(jnp.int32, (angles, LANES), 0)
+    far_real = jnp.sum(jnp.where(lane == angle, far, 0.0), axis=1, keepdims=True)
+    far_imag = jnp.sum(jnp.where(lane == angle + angles, far, 0.0), axis=1, keepdims=True)
+    far_real = jnp.broadcast_to(far_real, (angles, LANES))
+    far_imag = jnp.broadcast_to(far_imag, (angles, LANES))
     for block in range(blocks):
         rows_real = pl.ds(2 * block, angles, stride=stride)
         rows_imag = pl.ds(2 * block + 1, angles, stride=stride)
@@ -221,7 +229,7 @@
     near = near_blocks.reshape(pairs, 2 * unknowns, unknowns)
     inverse = inverse_blocks.reshape(blocks, 2 * unknowns, unknowns)
     f32 = functools.partial(jax.ShapeDtypeStruct, dtype=jnp.float32)
-    message = f32((slots + 1, record, unknowns))
+    message = f32((slots * record + 8, unknowns))
     inputs = (
         col_device,
         col_offset,
@@ -239,12 +247,14 @@
         out_specs=[vmem] * (LOW + 1),
         scratch_shapes=[pltpu.SMEM(whole.shape, whole.dtype) for whole in inputs[:4]]
         + [pltpu.VMEM(whole.shape, whole.dtype) for whole in inputs[4:]]
+        + [pltpu.VMEM((LOW * slots, record, unknowns), jnp.float32)]
         + [pltpu.SemaphoreType.DMA((7,)), pltpu.SemaphoreType.DMA((blocks,))],
         compiler_params=params,
         name="fill",
     )(*[pltpu.with_memory_space_constraint(whole, pltpu.HBM) for whole in inputs])
     arrived = [messages[0]] + [moved(messages[e], e) for e in range(1, LOW)]
     beside = [own_currents] + [moved(own_currents, d * LOW) for d in range(1, high_count)]
+    box_lanes = -(-boxes // LANES) * LANES
     columns = f32((high_count * blocks, record, unknowns))
     half = LANES // 2
     tables = [
@@ -255,20 +265,19 @@
     ]
     first_sums = pl.pallas_call(
         functools.partial(sum_first_kernel, slots, high_count),
-        out_shape=[columns, columns, f32((record, unknowns)), f32((half, unknowns))],
+        out_shape=[columns, columns, f32((8, unknowns)), f32((8, box_lanes))],
         in_specs=[vmem] * (LOW // 2 + high_count),
         out_specs=[vmem] * 4,
         scratch_shapes=tables,
         compiler_params=params,
         name="sum_first",
     )(*arrived[: LOW // 2], *beside)
-    partial = f32((blocks * record + angles, unknowns))
-    box_lanes = -(-boxes // LANES) * LANES
+    partials = [f32((blocks * record + 8 * (1 + min(d // 2, 1)), unknowns)) for d in range(high_count)]
     everyone = ("basis", "pol")
     senders = basis_count * lax.axis_size("pol")
     *sums, grad = pl.pallas_call(
         functools.partial(sum_last_kernel, slots, high_count, blocks),
-        out_shape=[partial] * high_count + [f32((senders, box_lanes))],
+        out_shape=partials + [f32((senders, 1, box_lanes))],
         in_specs=[vmem] * (LOW // 2 + 4),
         out_specs=[vmem] * (high_count + 1),
         scratch_shapes=[pltpu.VMEM(columns.shape, jnp.float32)] + tables,
@@ -285,7 +294,6 @@
         compiler_params=params,
         name="update",
     )(*totals, adjoint_rows, radiation_rows, inverse)
-    grad = grad.reshape(senders, 1, box_lanes)
     gathered = lax.all_to_all(grad, everyone, split_axis=0, concat_axis=0)
     gathered, updated = lax.optimization_barrier((gathered, updated))
     total_grad = jnp.sum(gathered[:, 0], axis=0)

time: 45.5 us -> 43.9 us (0.965)
  starting transfers between devices: 22.6 us -> 21.7 us
  waiting for transfers between devices: 14.8 us -> 14.2 us
    ppermute x9, waiting for transfers between devices: 13.2 us -> 12.1 us  [moved(): lax.ppermute(value, 'basis', [(i, i ^ bits) for i in range(basis_count)])]
    all_to_all x1, starting transfers between devices: 4.93 us -> 4.28 us  [on_device(): gathered = lax.all_to_all(grad, everyone, split_axis=0, concat_axis=0)]
    all_to_all x1, waiting for transfers between devices: 1.57 us -> 2.06 us  [on_device(): gathered = lax.all_to_all(grad, everyone, split_axis=0, concat_axis=0)]
where the time goes in v4:
time: 43.9 us; the launch traced here: 43.7 us
  starting transfers between devices  21.7 us (49%)
  waiting for transfers between devices  14.2 us (32%)
  Pallas kernels  6.46 us (15%)
  between operations  0.72 us (2%)
  other arithmetic  0.64 us (1%)
    ppermute x9, starting transfers between devices, moved(): lax.ppermute(value, 'basis', [(i, i ^ bits) for i in range(basis_count)])  17.4 us
    ppermute x9, waiting for transfers between devices, moved(): lax.ppermute(value, 'basis', [(i, i ^ bits) for i in range(basis_count)])  12.1 us
    all_to_all x1, starting transfers between devices, on_device(): gathered = lax.all_to_all(grad, everyone, split_axis=0, concat_axis=0)  4.28 us
    pallas_call x1, Pallas kernels, on_device(): pl.pallas_call(functools.partial(fill_kernel, slots), out_shape=[message]...  2.97 us
    all_to_all x1, waiting for transfers between devices, on_device(): gathered = lax.all_to_all(grad, everyone, split_axis=0, concat_axis=0)  2.06 us
    pallas_call x1, Pallas kernels, on_device(): pl.pallas_call(functools.partial(sum_last_kernel, slots, high_count, bloc...  1.56 us
    pallas_call x1, Pallas kernels, on_device(): pl.pallas_call(functools.partial(update_kernel, angles, norm_far, high_co...  0.97 us
    pallas_call x1, Pallas kernels, on_device(): pl.pallas_call(functools.partial(sum_first_kernel, slots, high_count), ou...  0.96 us
  transfers between devices with their start and end apart: 10, of which 5 were waited for; matrix products, arithmetic and copies ran while one was open for 0% of the time, Pallas kernels for 4%

profile of v4, /device:TPU:0, one launch (start us, length us, event | category | flops | bytes accessed | tf_op | source)
XLA Modules:
  0.0 43.7 jit_solution(13853862328614912983)
XLA Ops:
  0.6 0.0 copy-start
  0.6 0.0 copy-start.1
  0.7 0.0 copy-start.2
  0.7 3.0 %fill.1 = (f32[776,128]{1,0:T(8,128)S(1)}, f32[776,128]{1,0:T(8,128)S(1)}, f32[776,128]{1,0:T(8,128)S(1)}, f32[776,128]{1,0:T(8,128)S(1)}, f32[8,32,128]{2,1,0:T(8,128)S(1)}) custom-call(s32[8,6]{1,0:T(8,128)} %refs_0_.1, s32[8,6]{1,0:T(8,128)} %refs_1_.1, s32[8]{0:T(128)} %refs_2_.1, f32[8,6]{1,0:T(8,128)} %refs_3_.1, f32[256,128]{1,0:T(8,128)} %bitcast.6, ...), custom_call_target="tpu_custom_call" | custom-call | tf_op jit(solution)/shard_map/fill/pallas_call | solution.py:243
  3.6 3.0 %collective-permute-start.2 = (f32[776,128]{1,0:T(8,128)S(1)}, f32[776,128]{1,0:T(8,128)S(1)}, u32[]{:S(2)}, u32[]{:S(2)}) collective-permute-start(f32[776,128]{1,0:T(8,128)S(1)} %get-tuple-element.21), channel_id=1, source_target_pairs={{0,2},{2,0},{4,6},{6,4},{8,10},{10,8},{12,14},{14,12},{16,18},{18,... | collective-permute-start | bytes 1191944 | tf_op jit(solution)/shard_map/ppermute | solution.py:223
  6.6 1.5 %collective-permute-start = (f32[776,128]{1,0:T(8,128)S(1)}, f32[776,128]{1,0:T(8,128)S(1)}, u32[]{:S(2)}, u32[]{:S(2)}) collective-permute-start(f32[776,128]{1,0:T(8,128)S(1)} %get-tuple-element.18), channel_id=1, source_target_pairs={{0,4},{2,6},{4,0},{6,2},{8,12},{10,14},{12,8},{14,10},{16,20},{18,... | collective-permute-start | bytes 1191944 | tf_op jit(solution)/shard_map/ppermute | solution.py:223
  8.2 0.0 collective-permute-start.1
  8.2 2.0 %collective-permute-start.3 = (f32[8,32,128]{2,1,0:T(8,128)S(1)}, f32[8,32,128]{2,1,0:T(8,128)S(1)}, u32[]{:S(2)}, u32[]{:S(2)}) collective-permute-start(f32[8,32,128]{2,1,0:T(8,128)S(1)} %get-tuple-element.22.refs_2_), channel_id=1, source_target_pairs={{0,8},{2,10},{4,12},{6,14},{8,0},{10,2},{12,4},{14,6},{16,24},{18,... | collective-permute-start | bytes 393224 | tf_op jit(solution)/shard_map/ppermute | solution.py:223
  10.2 2.6 %collective-permute-start.4 = (f32[8,32,128]{2,1,0:T(8,128)S(1)}, f32[8,32,128]{2,1,0:T(8,128)S(1)}, u32[]{:S(2)}, u32[]{:S(2)}) collective-permute-start(f32[8,32,128]{2,1,0:T(8,128)S(1)} %get-tuple-element.22.refs_2_), channel_id=1, source_target_pairs={{0,16},{2,18},{4,20},{6,22},{8,24},{10,26},{12,28},{14,30},{16,0},... | collective-permute-start | bytes 393224 | tf_op jit(solution)/shard_map/ppermute | solution.py:223
  12.8 1.6 %collective-permute-done.3.refs_3_ = f32[8,32,128]{2,1,0:T(8,128)S(1)} collective-permute-done((f32[8,32,128]{2,1,0:T(8,128)S(1)}, f32[8,32,128]{2,1,0:T(8,128)S(1)}, u32[]{:S(2)}, u32[]{:S(2)}) %collective-permute-start.3) | collective-permute-done | bytes 131104 | tf_op jit(solution)/shard_map/ppermute | solution.py:223
  14.5 4.0 %collective-permute-start.5 = (f32[8,32,128]{2,1,0:T(8,128)S(1)}, f32[8,32,128]{2,1,0:T(8,128)S(1)}, u32[]{:S(2)}, u32[]{:S(2)}) collective-permute-start(f32[8,32,128]{2,1,0:T(8,128)S(1)} %get-tuple-element.22.refs_2_), channel_id=1, source_target_pairs={{0,24},{2,26},{4,28},{6,30},{8,16},{10,18},{12,20},{14,22},{16,8},... | collective-permute-start | bytes 393224 | tf_op jit(solution)/shard_map/ppermute | solution.py:223
  18.5 3.5 %collective-permute-done.4.refs_4_ = f32[8,32,128]{2,1,0:T(8,128)S(1)} collective-permute-done((f32[8,32,128]{2,1,0:T(8,128)S(1)}, f32[8,32,128]{2,1,0:T(8,128)S(1)}, u32[]{:S(2)}, u32[]{:S(2)}) %collective-permute-start.4) | collective-permute-done | bytes 131104 | tf_op jit(solution)/shard_map/ppermute | solution.py:223
  22.0 0.0 collective-permute-done.5.refs_5_
  22.0 0.0 collective-permute-done.2.refs_1_
  22.0 1.0 %sum_first.1 = (f32[32,32,128]{2,1,0:T(8,128)S(1)}, f32[32,32,128]{2,1,0:T(8,128)S(1)}, f32[8,128]{1,0:T(8,128)S(1)}, f32[8,128]{1,0:T(8,128)S(1)}) custom-call(f32[776,128]{1,0:T(8,128)S(1)} %get-tuple-element.20.refs_0_, f32[776,128]{1,0:T(8,128)S(1)} %collective-permute-done.2.refs_1_, f32[8,32,128]{2,1,0:T(8,128)S(1)} %get-tuple-element.22.refs_2_, ...), custom_call_target="tpu_custom_call" | custom-call | tf_op jit(solution)/shard_map/sum_first/pallas_call | solution.py:266
  23.0 2.9 %collective-permute-done.refs_0_ = f32[776,128]{1,0:T(8,128)S(1)} collective-permute-done((f32[776,128]{1,0:T(8,128)S(1)}, f32[776,128]{1,0:T(8,128)S(1)}, u32[]{:S(2)}, u32[]{:S(2)}) %collective-permute-start) | collective-permute-done | bytes 397344 | tf_op jit(solution)/shard_map/ppermute | solution.py:223
  25.8 0.0 collective-permute-done.1.refs_1_
  25.8 1.6 %sum_last.1 = (f32[264,128]{1,0:T(8,128)S(1)}, f32[264,128]{1,0:T(8,128)S(1)}, f32[272,128]{1,0:T(8,128)S(1)}, f32[272,128]{1,0:T(8,128)S(1)}, f32[32,1,128]{2,1,0:T(1,128)}) custom-call(f32[776,128]{1,0:T(8,128)S(1)} %collective-permute-done.refs_0_, f32[776,128]{1,0:T(8,128)S(1)} %collective-permute-done.1.refs_1_, ...), custom_call_target="tpu_custom_call" | custom-call | tf_op jit(solution)/shard_map/sum_last/pallas_call | solution.py:278
  27.4 2.7 %collective-permute-start.7 = (f32[272,128]{1,0:T(8,128)S(1)}, f32[272,128]{1,0:T(8,128)S(1)}, u32[]{:S(2)}, u32[]{:S(2)}) collective-permute-start(f32[272,128]{1,0:T(8,128)S(1)} %get-tuple-element.30), channel_id=1, source_target_pairs={{0,16},{2,18},{4,20},{6,22},{8,24},{10,26},{12,28},{14,30},{16,0},... | collective-permute-start | bytes 417800 | tf_op jit(solution)/shard_map/ppermute | solution.py:223
  30.0 1.3 %collective-permute-start.8 = (f32[272,128]{1,0:T(8,128)S(1)}, f32[272,128]{1,0:T(8,128)S(1)}, u32[]{:S(2)}, u32[]{:S(2)}) collective-permute-start(f32[272,128]{1,0:T(8,128)S(1)} %get-tuple-element.31), channel_id=1, source_target_pairs={{0,24},{2,26},{4,28},{6,30},{8,16},{10,18},{12,20},{14,22},{16,8},... | collective-permute-start | bytes 417800 | tf_op jit(solution)/shard_map/ppermute | solution.py:223
  31.4 0.2 collective-permute-start.6
  31.6 4.3 %all-to-all-start = ((f32[32,1,128]{2,1,0:T(1,128)}), f32[32,1,128]{2,1,0:T(1,128)S(1)}, u32[]{:S(2)}, u32[]{:S(2)}) async-start(f32[32,1,128]{2,1,0:T(1,128)} %get-tuple-element.27), calls=%async_computation | async-start | bytes 32768 | tf_op jit(solution)/shard_map/all_to_all | solution.py:297
  35.9 4.1 %collective-permute-done.6.refs_1_ = f32[264,128]{1,0:T(8,128)S(1)} collective-permute-done((f32[264,128]{1,0:T(8,128)S(1)}, f32[264,128]{1,0:T(8,128)S(1)}, u32[]{:S(2)}, u32[]{:S(2)}) %collective-permute-start.6) | collective-permute-done | bytes 135200 | tf_op jit(solution)/shard_map/ppermute | solution.py:223
  40.0 0.0 collective-permute-done.7.refs_2_
  40.0 0.0 collective-permute-done.8.refs_3_
  40.0 0.0 copy-done
  40.0 0.0 copy-done.1
  40.0 0.0 copy-done.2
  40.0 1.0 %update.1 = f32[256,128]{1,0:T(8,128)} custom-call(f32[264,128]{1,0:T(8,128)S(1)} %get-tuple-element.28.refs_0_, f32[264,128]{1,0:T(8,128)S(1)} %collective-permute-done.6.refs_1_, f32[272,128]{1,0:T(8,128)S(1)} %collective-permute-done.7.refs_2_, f32[272,128]{1,0:T(8,128)S(1)} %collective-permute-done.8.refs_3_, f32[256,128]{1,0:T(8,128)S(1)} %bitcast.7, ...), custom_call_target="tpu_custom_call" | custom-call | tf_op jit(solution)/shard_map/update/pallas_call | solution.py:289
  41.0 2.1 %all-to-all-done = f32[32,1,128]{2,1,0:T(1,128)S(1)} async-done(((f32[32,1,128]{2,1,0:T(1,128)}), f32[32,1,128]{2,1,0:T(1,128)S(1)}, u32[]{:S(2)}, u32[]{:S(2)}) %all-to-all-start) | async-done | bytes 16416 | tf_op jit(solution)/shard_map/all_to_all | solution.py:297
  43.1 0.1 reduce_sum.9
  43.1 0.6 %dynamic-slice_multiply_fusion = f32[4]{0:T(128)} fusion(f32[128]{0:T(128)S(1)} %reduce_sum.9, s32[]{:T(128)S(6)} %select_n.3), kind=kLoop, calls=%fused_computation | loop fusion | flops 4 | bytes 36 | tf_op jit(solution)/shard_map/mul | solution.py:303
Async XLA Ops:
  0.6 39.4 %copy-start = (f32[1,16,8,2,128]{4,3,2,1,0:T(2,128)S(1)}, f32[1,16,8,2,128]{4,3,2,1,0:T(2,128)}, u32[]{:S(2)}) copy-start(f32[1,16,8,2,128]{4,3,2,1,0:T(2,128)} %param.9) | copy-start | bytes 393220
  0.6 39.4 %copy-start.1 = (f32[1,16,8,2,128]{4,3,2,1,0:T(2,128)S(1)}, f32[1,16,8,2,128]{4,3,2,1,0:T(2,128)}, u32[]{:S(2)}) copy-start(f32[1,16,8,2,128]{4,3,2,1,0:T(2,128)} %param.11) | copy-start | bytes 393220
  0.7 39.4 %copy-start.2 = (bf16[8,2,128,128]{3,2,1,0:T(8,128)(2,1)S(1)}, bf16[8,2,128,128]{3,2,1,0:T(8,128)(2,1)}, u32[]{:S(2)}) copy-start(bf16[8,2,128,128]{3,2,1,0:T(8,128)(2,1)} %param.13) | copy-start | bytes 1572868
  3.6 18.3 %collective-permute-start.2 = (f32[776,128]{1,0:T(8,128)S(1)}, f32[776,128]{1,0:T(8,128)S(1)}, u32[]{:S(2)}, u32[]{:S(2)}) collective-permute-start(f32[776,128]{1,0:T(8,128)S(1)} %get-tuple-element.21), channel_id=1, source_target_pairs={{0,2},{2,0},{4,6},{6,4},{8,10},{10,8},{12,14},{14,12},{16,18},{18,... | collective-permute-start | bytes 1191944 | tf_op jit(solution)/shard_map/ppermute | solution.py:223
  6.6 19.2 %collective-permute-start = (f32[776,128]{1,0:T(8,128)S(1)}, f32[776,128]{1,0:T(8,128)S(1)}, u32[]{:S(2)}, u32[]{:S(2)}) collective-permute-start(f32[776,128]{1,0:T(8,128)S(1)} %get-tuple-element.18), channel_id=1, source_target_pairs={{0,4},{2,6},{4,0},{6,2},{8,12},{10,14},{12,8},{14,10},{16,20},{18,... | collective-permute-start | bytes 1191944 | tf_op jit(solution)/shard_map/ppermute | solution.py:223
  8.2 17.7 %collective-permute-start.1 = (f32[776,128]{1,0:T(8,128)S(1)}, f32[776,128]{1,0:T(8,128)S(1)}, u32[]{:S(2)}, u32[]{:S(2)}) collective-permute-start(f32[776,128]{1,0:T(8,128)S(1)} %get-tuple-element.19), channel_id=1, source_target_pairs={{0,6},{2,4},{4,2},{6,0},{8,14},{10,12},{12,10},{14,8},{16,22},{18,... | collective-permute-start | bytes 1191944 | tf_op jit(solution)/shard_map/ppermute | solution.py:223
  8.2 6.3 %collective-permute-start.3 = (f32[8,32,128]{2,1,0:T(8,128)S(1)}, f32[8,32,128]{2,1,0:T(8,128)S(1)}, u32[]{:S(2)}, u32[]{:S(2)}) collective-permute-start(f32[8,32,128]{2,1,0:T(8,128)S(1)} %get-tuple-element.22.refs_2_), channel_id=1, source_target_pairs={{0,8},{2,10},{4,12},{6,14},{8,0},{10,2},{12,4},{14,6},{16,24},{18,... | collective-permute-start | bytes 393224 | tf_op jit(solution)/shard_map/ppermute | solution.py:223
  10.2 11.8 %collective-permute-start.4 = (f32[8,32,128]{2,1,0:T(8,128)S(1)}, f32[8,32,128]{2,1,0:T(8,128)S(1)}, u32[]{:S(2)}, u32[]{:S(2)}) collective-permute-start(f32[8,32,128]{2,1,0:T(8,128)S(1)} %get-tuple-element.22.refs_2_), channel_id=1, source_target_pairs={{0,16},{2,18},{4,20},{6,22},{8,24},{10,26},{12,28},{14,30},{16,0},... | collective-permute-start | bytes 393224 | tf_op jit(solution)/shard_map/ppermute | solution.py:223
  14.5 7.5 %collective-permute-start.5 = (f32[8,32,128]{2,1,0:T(8,128)S(1)}, f32[8,32,128]{2,1,0:T(8,128)S(1)}, u32[]{:S(2)}, u32[]{:S(2)}) collective-permute-start(f32[8,32,128]{2,1,0:T(8,128)S(1)} %get-tuple-element.22.refs_2_), channel_id=1, source_target_pairs={{0,24},{2,26},{4,28},{6,30},{8,16},{10,18},{12,20},{14,22},{16,8},... | collective-permute-start | bytes 393224 | tf_op jit(solution)/shard_map/ppermute | solution.py:223
  27.4 12.6 %collective-permute-start.7 = (f32[272,128]{1,0:T(8,128)S(1)}, f32[272,128]{1,0:T(8,128)S(1)}, u32[]{:S(2)}, u32[]{:S(2)}) collective-permute-start(f32[272,128]{1,0:T(8,128)S(1)} %get-tuple-element.30), channel_id=1, source_target_pairs={{0,16},{2,18},{4,20},{6,22},{8,24},{10,26},{12,28},{14,30},{16,0},... | collective-permute-start | bytes 417800 | tf_op jit(solution)/shard_map/ppermute | solution.py:223
  30.0 10.0 %collective-permute-start.8 = (f32[272,128]{1,0:T(8,128)S(1)}, f32[272,128]{1,0:T(8,128)S(1)}, u32[]{:S(2)}, u32[]{:S(2)}) collective-permute-start(f32[272,128]{1,0:T(8,128)S(1)} %get-tuple-element.31), channel_id=1, source_target_pairs={{0,24},{2,26},{4,28},{6,30},{8,16},{10,18},{12,20},{14,22},{16,8},... | collective-permute-start | bytes 417800 | tf_op jit(solution)/shard_map/ppermute | solution.py:223
  31.4 8.6 %collective-permute-start.6 = (f32[264,128]{1,0:T(8,128)S(1)}, f32[264,128]{1,0:T(8,128)S(1)}, u32[]{:S(2)}, u32[]{:S(2)}) collective-permute-start(f32[264,128]{1,0:T(8,128)S(1)} %get-tuple-element.29), channel_id=1, source_target_pairs={{0,8},{2,10},{4,12},{6,14},{8,0},{10,2},{12,4},{14,6},{16,24},{18,... | collective-permute-start | bytes 405512 | tf_op jit(solution)/shard_map/ppermute | solution.py:223
  31.6 11.4 %all-to-all-start = ((f32[32,1,128]{2,1,0:T(1,128)}), f32[32,1,128]{2,1,0:T(1,128)S(1)}, u32[]{:S(2)}, u32[]{:S(2)}) async-start(f32[32,1,128]{2,1,0:T(1,128)} %get-tuple-element.27), calls=%async_computation | async-start | bytes 32768 | tf_op jit(solution)/shard_map/all_to_all | solution.py:297

commit v5 on v4

--- a/solution.py
+++ b/solution.py
@@ -41,11 +41,11 @@
     copies = [pltpu.make_async_copy(whole_refs[i], held_refs[i], sems.at[i]) for i in range(7)]
     near_copies = [
         pltpu.make_async_copy(
-            whole_refs[7].at[pl.ds(row * near_count, near_count)],
-            near_ref.at[pl.ds(row * near_count, near_count)],
+            whole_refs[7].at[pl.ds(row * near_count * 2, near_count * 2)],
+            near_ref.at[pl.ds(row * near_count * 2, near_count * 2)],
             near_sems.at[row],
         )
-        for row in range(blocks)
+        for row in range(blocks // 2)
     ]
     for copy in copies[4:5] + near_copies[:1] + copies[:4] + near_copies[1:] + copies[5:]:
         copy.start()
@@ -57,6 +57,7 @@
     sub8 = lax.broadcasted_iota(jnp.int32, (8, LANES), 0)
     table = jnp.zeros((8, LANES), jnp.float32)
     counts = [jnp.int32(0)] * LOW
+    buffer_ref[...] = jnp.zeros(buffer_ref.shape, jnp.float32)
     for copy in copies[:5]:
         copy.wait()
     for row in range(blocks):
@@ -64,7 +65,8 @@
         imag = adjoint_ref[pl.ds(2 * row + 1, angles, stride=stride), :].astype(jnp.bfloat16)
         left = complex_rows(real, imag)
         box = box_ref[row].astype(jnp.float32)
-        near_copies[row].wait()
+        if row % 2 == 0:
+            near_copies[row // 2].wait()
         for first in range(0, near_count, 1):
             some = range(first, min(first + 1, near_count))
             right = jnp.concatenate([near_ref[row * near_count + k] for k in some], axis=1)
@@ -73,7 +75,7 @@
                 device = col_device_ref[row, k]
                 low = lax.bitwise_xor(lax.rem(device, LOW), my_low)
                 high = lax.bitwise_xor(lax.div(device, LOW), my_high)
-                place = high * blocks + col_offset_ref[row, k] + 1
+                place = high * blocks + col_offset_ref[row, k]
                 slot = jnp.int32(0)
                 for e in range(LOW):
                     here = low == e
@@ -127,9 +129,8 @@
     copy.wait()
     for i, message_ref in enumerate(message_refs):
         for s in range(slots):
-            place = place_ref[0, (first + i) * spread + s]
-            at = jnp.maximum(place - 1, 0)
-            term = jnp.where(place > 0, message_ref[pl.ds(s * record, record), :], 0.0)
+            at = place_ref[0, (first + i) * spread + s]
+            term = message_ref[pl.ds(s * record, record), :]
             acc_ref[at] = acc_ref[at] + term
             both = term * cur_ref[at]
             prod_ref[i * spread + s] = jnp.sum(both.reshape(-1, 8, LANES), axis=0)

time: 43.9 us -> 43.5 us (level)
  no operation moved by 1% of the time
where the time goes in v5:
time: 43.5 us; the launch traced here: 43.3 us
  starting transfers between devices  21.7 us (50%)
  waiting for transfers between devices  14.1 us (32%)
  Pallas kernels  6.13 us (14%)
  between operations  0.72 us (2%)
  other arithmetic  0.64 us (1%)
    ppermute x9, starting transfers between devices, moved(): lax.ppermute(value, 'basis', [(i, i ^ bits) for i in range(basis_count)])  17.5 us
    ppermute x9, waiting for transfers between devices, moved(): lax.ppermute(value, 'basis', [(i, i ^ bits) for i in range(basis_count)])  12.1 us
    all_to_all x1, starting transfers between devices, on_device(): gathered = lax.all_to_all(grad, everyone, split_axis=0, concat_axis=0)  4.24 us
    pallas_call x1, Pallas kernels, on_device(): pl.pallas_call(functools.partial(fill_kernel, slots), out_shape=[message]...  2.67 us
    all_to_all x1, waiting for transfers between devices, on_device(): gathered = lax.all_to_all(grad, everyone, split_axis=0, concat_axis=0)  2.03 us
    pallas_call x1, Pallas kernels, on_device(): pl.pallas_call(functools.partial(sum_last_kernel, slots, high_count, bloc...  1.51 us
    pallas_call x1, Pallas kernels, on_device(): pl.pallas_call(functools.partial(sum_first_kernel, slots, high_count), ou...  0.98 us
    pallas_call x1, Pallas kernels, on_device(): pl.pallas_call(functools.partial(update_kernel, angles, norm_far, high_co...  0.97 us
  transfers between devices with their start and end apart: 10, of which 5 were waited for; matrix products, arithmetic and copies ran while one was open for 0% of the time, Pallas kernels for 4%

profile of v5, /device:TPU:0, one launch (start us, length us, event | category | flops | bytes accessed | tf_op | source)
XLA Modules:
  0.0 43.3 jit_solution(13654916592918696215)
XLA Ops:
  0.6 0.0 copy-start
  0.6 0.0 copy-start.1
  0.7 0.0 copy-start.2
  0.7 2.7 %fill.1 = (f32[776,128]{1,0:T(8,128)S(1)}, f32[776,128]{1,0:T(8,128)S(1)}, f32[776,128]{1,0:T(8,128)S(1)}, f32[776,128]{1,0:T(8,128)S(1)}, f32[8,32,128]{2,1,0:T(8,128)S(1)}) custom-call(s32[8,6]{1,0:T(8,128)} %refs_0_.1, s32[8,6]{1,0:T(8,128)} %refs_1_.1, s32[8]{0:T(128)} %refs_2_.1, f32[8,6]{1,0:T(8,128)} %refs_3_.1, f32[256,128]{1,0:T(8,128)} %bitcast.6, ...), custom_call_target="tpu_custom_call" | custom-call | tf_op jit(solution)/shard_map/fill/pallas_call | solution.py:244
  3.3 3.0 %collective-permute-start.2 = (f32[776,128]{1,0:T(8,128)S(1)}, f32[776,128]{1,0:T(8,128)S(1)}, u32[]{:S(2)}, u32[]{:S(2)}) collective-permute-start(f32[776,128]{1,0:T(8,128)S(1)} %get-tuple-element.21), channel_id=1, source_target_pairs={{0,2},{2,0},{4,6},{6,4},{8,10},{10,8},{12,14},{14,12},{16,18},{18,... | collective-permute-start | bytes 1191944 | tf_op jit(solution)/shard_map/ppermute | solution.py:224
  6.3 1.5 %collective-permute-start = (f32[776,128]{1,0:T(8,128)S(1)}, f32[776,128]{1,0:T(8,128)S(1)}, u32[]{:S(2)}, u32[]{:S(2)}) collective-permute-start(f32[776,128]{1,0:T(8,128)S(1)} %get-tuple-element.18), channel_id=1, source_target_pairs={{0,4},{2,6},{4,0},{6,2},{8,12},{10,14},{12,8},{14,10},{16,20},{18,... | collective-permute-start | bytes 1191944 | tf_op jit(solution)/shard_map/ppermute | solution.py:224
  7.9 0.0 collective-permute-start.1
  7.9 2.0 %collective-permute-start.3 = (f32[8,32,128]{2,1,0:T(8,128)S(1)}, f32[8,32,128]{2,1,0:T(8,128)S(1)}, u32[]{:S(2)}, u32[]{:S(2)}) collective-permute-start(f32[8,32,128]{2,1,0:T(8,128)S(1)} %get-tuple-element.22.refs_2_), channel_id=1, source_target_pairs={{0,8},{2,10},{4,12},{6,14},{8,0},{10,2},{12,4},{14,6},{16,24},{18,... | collective-permute-start | bytes 393224 | tf_op jit(solution)/shard_map/ppermute | solution.py:224
  9.9 2.6 %collective-permute-start.4 = (f32[8,32,128]{2,1,0:T(8,128)S(1)}, f32[8,32,128]{2,1,0:T(8,128)S(1)}, u32[]{:S(2)}, u32[]{:S(2)}) collective-permute-start(f32[8,32,128]{2,1,0:T(8,128)S(1)} %get-tuple-element.22.refs_2_), channel_id=1, source_target_pairs={{0,16},{2,18},{4,20},{6,22},{8,24},{10,26},{12,28},{14,30},{16,0},... | collective-permute-start | bytes 393224 | tf_op jit(solution)/shard_map/ppermute | solution.py:224
  12.5 1.6 %collective-permute-done.3.refs_3_ = f32[8,32,128]{2,1,0:T(8,128)S(1)} collective-permute-done((f32[8,32,128]{2,1,0:T(8,128)S(1)}, f32[8,32,128]{2,1,0:T(8,128)S(1)}, u32[]{:S(2)}, u32[]{:S(2)}) %collective-permute-start.3) | collective-permute-done | bytes 131104 | tf_op jit(solution)/shard_map/ppermute | solution.py:224
  14.2 4.1 %collective-permute-start.5 = (f32[8,32,128]{2,1,0:T(8,128)S(1)}, f32[8,32,128]{2,1,0:T(8,128)S(1)}, u32[]{:S(2)}, u32[]{:S(2)}) collective-permute-start(f32[8,32,128]{2,1,0:T(8,128)S(1)} %get-tuple-element.22.refs_2_), channel_id=1, source_target_pairs={{0,24},{2,26},{4,28},{6,30},{8,16},{10,18},{12,20},{14,22},{16,8},... | collective-permute-start | bytes 393224 | tf_op jit(solution)/shard_map/ppermute | solution.py:224
  18.2 3.4 %collective-permute-done.4.refs_4_ = f32[8,32,128]{2,1,0:T(8,128)S(1)} collective-permute-done((f32[8,32,128]{2,1,0:T(8,128)S(1)}, f32[8,32,128]{2,1,0:T(8,128)S(1)}, u32[]{:S(2)}, u32[]{:S(2)}) %collective-permute-start.4) | collective-permute-done | bytes 131104 | tf_op jit(solution)/shard_map/ppermute | solution.py:224
  21.7 0.0 collective-permute-done.5.refs_5_
  21.7 0.0 collective-permute-done.2.refs_1_
  21.7 1.0 %sum_first.1 = (f32[32,32,128]{2,1,0:T(8,128)S(1)}, f32[32,32,128]{2,1,0:T(8,128)S(1)}, f32[8,128]{1,0:T(8,128)S(1)}, f32[8,128]{1,0:T(8,128)S(1)}) custom-call(f32[776,128]{1,0:T(8,128)S(1)} %get-tuple-element.20.refs_0_, f32[776,128]{1,0:T(8,128)S(1)} %collective-permute-done.2.refs_1_, f32[8,32,128]{2,1,0:T(8,128)S(1)} %get-tuple-element.22.refs_2_, ...), custom_call_target="tpu_custom_call" | custom-call | tf_op jit(solution)/shard_map/sum_first/pallas_call | solution.py:267
  22.6 2.9 %collective-permute-done.refs_0_ = f32[776,128]{1,0:T(8,128)S(1)} collective-permute-done((f32[776,128]{1,0:T(8,128)S(1)}, f32[776,128]{1,0:T(8,128)S(1)}, u32[]{:S(2)}, u32[]{:S(2)}) %collective-permute-start) | collective-permute-done | bytes 397344 | tf_op jit(solution)/shard_map/ppermute | solution.py:224
  25.5 0.0 collective-permute-done.1.refs_1_
  25.5 1.5 %sum_last.1 = (f32[264,128]{1,0:T(8,128)S(1)}, f32[264,128]{1,0:T(8,128)S(1)}, f32[272,128]{1,0:T(8,128)S(1)}, f32[272,128]{1,0:T(8,128)S(1)}, f32[32,1,128]{2,1,0:T(1,128)}) custom-call(f32[776,128]{1,0:T(8,128)S(1)} %collective-permute-done.refs_0_, f32[776,128]{1,0:T(8,128)S(1)} %collective-permute-done.1.refs_1_, ...), custom_call_target="tpu_custom_call" | custom-call | tf_op jit(solution)/shard_map/sum_last/pallas_call | solution.py:279
  27.0 2.7 %collective-permute-start.7 = (f32[272,128]{1,0:T(8,128)S(1)}, f32[272,128]{1,0:T(8,128)S(1)}, u32[]{:S(2)}, u32[]{:S(2)}) collective-permute-start(f32[272,128]{1,0:T(8,128)S(1)} %get-tuple-element.30), channel_id=1, source_target_pairs={{0,16},{2,18},{4,20},{6,22},{8,24},{10,26},{12,28},{14,30},{16,0},... | collective-permute-start | bytes 417800 | tf_op jit(solution)/shard_map/ppermute | solution.py:224
  29.7 1.4 %collective-permute-start.8 = (f32[272,128]{1,0:T(8,128)S(1)}, f32[272,128]{1,0:T(8,128)S(1)}, u32[]{:S(2)}, u32[]{:S(2)}) collective-permute-start(f32[272,128]{1,0:T(8,128)S(1)} %get-tuple-element.31), channel_id=1, source_target_pairs={{0,24},{2,26},{4,28},{6,30},{8,16},{10,18},{12,20},{14,22},{16,8},... | collective-permute-start | bytes 417800 | tf_op jit(solution)/shard_map/ppermute | solution.py:224
  31.0 0.2 collective-permute-start.6
  31.3 4.2 %all-to-all-start = ((f32[32,1,128]{2,1,0:T(1,128)}), f32[32,1,128]{2,1,0:T(1,128)S(1)}, u32[]{:S(2)}, u32[]{:S(2)}) async-start(f32[32,1,128]{2,1,0:T(1,128)} %get-tuple-element.27), calls=%async_computation | async-start | bytes 32768 | tf_op jit(solution)/shard_map/all_to_all | solution.py:298
  35.5 4.1 %collective-permute-done.6.refs_1_ = f32[264,128]{1,0:T(8,128)S(1)} collective-permute-done((f32[264,128]{1,0:T(8,128)S(1)}, f32[264,128]{1,0:T(8,128)S(1)}, u32[]{:S(2)}, u32[]{:S(2)}) %collective-permute-start.6) | collective-permute-done | bytes 135200 | tf_op jit(solution)/shard_map/ppermute | solution.py:224
  39.6 0.0 collective-permute-done.7.refs_2_
  39.6 0.0 collective-permute-done.8.refs_3_
  39.6 0.0 copy-done
  39.7 0.0 copy-done.1
  39.7 0.0 copy-done.2
  39.7 1.0 %update.1 = f32[256,128]{1,0:T(8,128)} custom-call(f32[264,128]{1,0:T(8,128)S(1)} %get-tuple-element.28.refs_0_, f32[264,128]{1,0:T(8,128)S(1)} %collective-permute-done.6.refs_1_, f32[272,128]{1,0:T(8,128)S(1)} %collective-permute-done.7.refs_2_, f32[272,128]{1,0:T(8,128)S(1)} %collective-permute-done.8.refs_3_, f32[256,128]{1,0:T(8,128)S(1)} %bitcast.7, ...), custom_call_target="tpu_custom_call" | custom-call | tf_op jit(solution)/shard_map/update/pallas_call | solution.py:290
  40.6 2.0 %all-to-all-done = f32[32,1,128]{2,1,0:T(1,128)S(1)} async-done(((f32[32,1,128]{2,1,0:T(1,128)}), f32[32,1,128]{2,1,0:T(1,128)S(1)}, u32[]{:S(2)}, u32[]{:S(2)}) %all-to-all-start) | async-done | bytes 16416 | tf_op jit(solution)/shard_map/all_to_all | solution.py:298
  42.7 0.1 reduce_sum.9
  42.7 0.6 %dynamic-slice_multiply_fusion = f32[4]{0:T(128)} fusion(f32[128]{0:T(128)S(1)} %reduce_sum.9, s32[]{:T(128)S(6)} %select_n.3), kind=kLoop, calls=%fused_computation | loop fusion | flops 4 | bytes 36 | tf_op jit(solution)/shard_map/mul | solution.py:304
Async XLA Ops:
  0.6 39.0 %copy-start = (f32[1,16,8,2,128]{4,3,2,1,0:T(2,128)S(1)}, f32[1,16,8,2,128]{4,3,2,1,0:T(2,128)}, u32[]{:S(2)}) copy-start(f32[1,16,8,2,128]{4,3,2,1,0:T(2,128)} %param.9) | copy-start | bytes 393220
  0.6 39.0 %copy-start.1 = (f32[1,16,8,2,128]{4,3,2,1,0:T(2,128)S(1)}, f32[1,16,8,2,128]{4,3,2,1,0:T(2,128)}, u32[]{:S(2)}) copy-start(f32[1,16,8,2,128]{4,3,2,1,0:T(2,128)} %param.11) | copy-start | bytes 393220
  0.7 39.0 %copy-start.2 = (bf16[8,2,128,128]{3,2,1,0:T(8,128)(2,1)S(1)}, bf16[8,2,128,128]{3,2,1,0:T(8,128)(2,1)}, u32[]{:S(2)}) copy-start(bf16[8,2,128,128]{3,2,1,0:T(8,128)(2,1)} %param.13) | copy-start | bytes 1572868
  3.3 18.3 %collective-permute-start.2 = (f32[776,128]{1,0:T(8,128)S(1)}, f32[776,128]{1,0:T(8,128)S(1)}, u32[]{:S(2)}, u32[]{:S(2)}) collective-permute-start(f32[776,128]{1,0:T(8,128)S(1)} %get-tuple-element.21), channel_id=1, source_target_pairs={{0,2},{2,0},{4,6},{6,4},{8,10},{10,8},{12,14},{14,12},{16,18},{18,... | collective-permute-start | bytes 1191944 | tf_op jit(solution)/shard_map/ppermute | solution.py:224
  6.3 19.2 %collective-permute-start = (f32[776,128]{1,0:T(8,128)S(1)}, f32[776,128]{1,0:T(8,128)S(1)}, u32[]{:S(2)}, u32[]{:S(2)}) collective-permute-start(f32[776,128]{1,0:T(8,128)S(1)} %get-tuple-element.18), channel_id=1, source_target_pairs={{0,4},{2,6},{4,0},{6,2},{8,12},{10,14},{12,8},{14,10},{16,20},{18,... | collective-permute-start | bytes 1191944 | tf_op jit(solution)/shard_map/ppermute | solution.py:224
  7.9 17.7 %collective-permute-start.1 = (f32[776,128]{1,0:T(8,128)S(1)}, f32[776,128]{1,0:T(8,128)S(1)}, u32[]{:S(2)}, u32[]{:S(2)}) collective-permute-start(f32[776,128]{1,0:T(8,128)S(1)} %get-tuple-element.19), channel_id=1, source_target_pairs={{0,6},{2,4},{4,2},{6,0},{8,14},{10,12},{12,10},{14,8},{16,22},{18,... | collective-permute-start | bytes 1191944 | tf_op jit(solution)/shard_map/ppermute | solution.py:224
  7.9 6.3 %collective-permute-start.3 = (f32[8,32,128]{2,1,0:T(8,128)S(1)}, f32[8,32,128]{2,1,0:T(8,128)S(1)}, u32[]{:S(2)}, u32[]{:S(2)}) collective-permute-start(f32[8,32,128]{2,1,0:T(8,128)S(1)} %get-tuple-element.22.refs_2_), channel_id=1, source_target_pairs={{0,8},{2,10},{4,12},{6,14},{8,0},{10,2},{12,4},{14,6},{16,24},{18,... | collective-permute-start | bytes 393224 | tf_op jit(solution)/shard_map/ppermute | solution.py:224
  9.9 11.7 %collective-permute-start.4 = (f32[8,32,128]{2,1,0:T(8,128)S(1)}, f32[8,32,128]{2,1,0:T(8,128)S(1)}, u32[]{:S(2)}, u32[]{:S(2)}) collective-permute-start(f32[8,32,128]{2,1,0:T(8,128)S(1)} %get-tuple-element.22.refs_2_), channel_id=1, source_target_pairs={{0,16},{2,18},{4,20},{6,22},{8,24},{10,26},{12,28},{14,30},{16,0},... | collective-permute-start | bytes 393224 | tf_op jit(solution)/shard_map/ppermute | solution.py:224
  14.2 7.5 %collective-permute-start.5 = (f32[8,32,128]{2,1,0:T(8,128)S(1)}, f32[8,32,128]{2,1,0:T(8,128)S(1)}, u32[]{:S(2)}, u32[]{:S(2)}) collective-permute-start(f32[8,32,128]{2,1,0:T(8,128)S(1)} %get-tuple-element.22.refs_2_), channel_id=1, source_target_pairs={{0,24},{2,26},{4,28},{6,30},{8,16},{10,18},{12,20},{14,22},{16,8},... | collective-permute-start | bytes 393224 | tf_op jit(solution)/shard_map/ppermute | solution.py:224
  27.0 12.6 %collective-permute-start.7 = (f32[272,128]{1,0:T(8,128)S(1)}, f32[272,128]{1,0:T(8,128)S(1)}, u32[]{:S(2)}, u32[]{:S(2)}) collective-permute-start(f32[272,128]{1,0:T(8,128)S(1)} %get-tuple-element.30), channel_id=1, source_target_pairs={{0,16},{2,18},{4,20},{6,22},{8,24},{10,26},{12,28},{14,30},{16,0},... | collective-permute-start | bytes 417800 | tf_op jit(solution)/shard_map/ppermute | solution.py:224
  29.7 10.0 %collective-permute-start.8 = (f32[272,128]{1,0:T(8,128)S(1)}, f32[272,128]{1,0:T(8,128)S(1)}, u32[]{:S(2)}, u32[]{:S(2)}) collective-permute-start(f32[272,128]{1,0:T(8,128)S(1)} %get-tuple-element.31), channel_id=1, source_target_pairs={{0,24},{2,26},{4,28},{6,30},{8,16},{10,18},{12,20},{14,22},{16,8},... | collective-permute-start | bytes 417800 | tf_op jit(solution)/shard_map/ppermute | solution.py:224
  31.0 8.6 %collective-permute-start.6 = (f32[264,128]{1,0:T(8,128)S(1)}, f32[264,128]{1,0:T(8,128)S(1)}, u32[]{:S(2)}, u32[]{:S(2)}) collective-permute-start(f32[264,128]{1,0:T(8,128)S(1)} %get-tuple-element.29), channel_id=1, source_target_pairs={{0,8},{2,10},{4,12},{6,14},{8,0},{10,2},{12,4},{14,6},{16,24},{18,... | collective-permute-start | bytes 405512 | tf_op jit(solution)/shard_map/ppermute | solution.py:224
  31.3 11.4 %all-to-all-start = ((f32[32,1,128]{2,1,0:T(1,128)}), f32[32,1,128]{2,1,0:T(1,128)S(1)}, u32[]{:S(2)}, u32[]{:S(2)}) async-start(f32[32,1,128]{2,1,0:T(1,128)} %get-tuple-element.27), calls=%async_computation | async-start | bytes 32768 | tf_op jit(solution)/shard_map/all_to_all | solution.py:298

commit v6 on v5

--- a/solution.py
+++ b/solution.py
@@ -114,13 +114,16 @@
         message_refs[e][pl.ds(slots * record, 8), :] = jnp.where(sub8 == FAR_ROW, far, mine)
 
 
-def add_slots(message_refs, first, slots, boxes, table, scratch_refs):
-    acc_ref, cur_ref, prod_ref, table_ref, place_ref, sem = scratch_refs
-    spread = LANES // LOW
-    record = cur_ref.shape[1]
+def start_places(table, table_ref, place_ref, sem):
     table_ref[...] = table.astype(jnp.int32)
     copy = pltpu.make_async_copy(table_ref, place_ref, sem)
     copy.start()
+    return copy
+
+
+def box_shares(message_refs, first, slots, boxes, table, cur_ref, prod_ref, place_ref, copy):
+    spread = LANES // LOW
+    record = cur_ref.shape[1]
     prod_ref[...] = jnp.zeros(prod_ref.shape, jnp.float32)
     count = len(message_refs) * spread
     by_pair = jnp.transpose(table)[first * spread : first * spread + count]
@@ -130,42 +133,61 @@
     for i, message_ref in enumerate(message_refs):
         for s in range(slots):
             at = place_ref[0, (first + i) * spread + s]
-            term = message_ref[pl.ds(s * record, record), :]
-            acc_ref[at] = acc_ref[at] + term
-            both = term * cur_ref[at]
+            both = message_ref[pl.ds(s * record, record), :] * cur_ref[at]
             prod_ref[i * spread + s] = jnp.sum(both.reshape(-1, 8, LANES), axis=0)
     by_slot = jnp.sum(jnp.sum(prod_ref[...], axis=1), axis=1, keepdims=True)
     return jnp.sum((rates * by_slot).reshape(count // 8, 8, boxes), axis=0)
 
 
+def add_slots(message_refs, first, slots, record, acc_ref, place_ref):
+    for i, message_ref in enumerate(message_refs):
+        for s in range(slots):
+            at = place_ref[0, (first + i) * (LANES // LOW) + s]
+            acc_ref[at] = acc_ref[at] + message_ref[pl.ds(s * record, record), :]
+
+
 def sum_first_kernel(slots, high_count, *refs):
     message_refs, current_refs = refs[: LOW // 2], refs[LOW // 2 : LOW // 2 + high_count]
-    acc_ref, cur_ref, extra_ref, share_ref, *scratch_refs = refs[LOW // 2 + high_count :]
+    acc_ref, cur_ref, extra_ref, share_ref, prod_ref, table_ref, place_ref, sem = refs[
+        LOW // 2 + high_count :
+    ]
     blocks, record = current_refs[0].shape[:2]
     extra = functools.reduce(jnp.add, [ref[pl.ds(slots * record, 8), :] for ref in message_refs])
+    copy = start_places(extra, table_ref, place_ref, sem)
     for d in range(high_count):
         cur_ref[pl.ds(d * blocks, blocks)] = current_refs[d][...]
     acc_ref[...] = jnp.zeros(acc_ref.shape, jnp.float32)
-    share_ref[...] = add_slots(message_refs, 0, slots, share_ref.shape[1], extra, (acc_ref, cur_ref, *scratch_refs))
+    share_ref[...] = box_shares(
+        message_refs, 0, slots, share_ref.shape[1], extra, cur_ref, prod_ref, place_ref, copy
+    )
+    add_slots(message_refs, 0, slots, record, acc_ref, place_ref)
     extra_ref[...] = extra
 
 
 def sum_last_kernel(slots, high_count, blocks, *refs):
     message_refs, refs = refs[: LOW // 2], refs[LOW // 2 :]
     (first_ref, cur_ref, first_extra_ref, first_share_ref), refs = refs[:4], refs[4:]
-    out_refs, (grad_ref, acc_ref, *scratch_refs) = refs[:high_count], refs[high_count:]
+    out_refs, (whole_grad_ref, acc_ref, *refs) = refs[:high_count], refs[high_count:]
+    prod_ref, table_ref, place_ref, sem, grad_ref, grad_sem = refs
     record = cur_ref.shape[1]
     extra = functools.reduce(jnp.add, [ref[pl.ds(slots * record, 8), :] for ref in message_refs])
+    copy = start_places(extra, table_ref, place_ref, sem)
     acc_ref[...] = first_ref[...]
-    share = add_slots(message_refs, LOW // 2, slots, grad_ref.shape[2], extra, (acc_ref, cur_ref, *scratch_refs))
+    share = box_shares(
+        message_refs, LOW // 2, slots, grad_ref.shape[2], extra, cur_ref, prod_ref, place_ref, copy
+    )
     box_sums = jnp.sum(share + first_share_ref[...], axis=0, keepdims=True)
     grad_ref[...] = jnp.broadcast_to(box_sums[None], grad_ref.shape)
+    copy = pltpu.make_async_copy(grad_ref, whole_grad_ref, grad_sem)
+    copy.start()
+    add_slots(message_refs, LOW // 2, slots, record, acc_ref, place_ref)
     extra = extra + first_extra_ref[...]
     for d in range(high_count):
         for b in range(blocks):
             out_refs[d][pl.ds(b * record, record), :] = acc_ref[d * blocks + b]
         for row in range(blocks * record, out_refs[d].shape[0], 8):
             out_refs[d][pl.ds(row, 8), :] = extra
+    copy.wait()
 
 
 def update_kernel(angles, norm_far, high_count, *refs):
@@ -280,8 +302,10 @@
         functools.partial(sum_last_kernel, slots, high_count, blocks),
         out_shape=partials + [f32((senders, 1, box_lanes))],
         in_specs=[vmem] * (LOW // 2 + 4),
-        out_specs=[vmem] * (high_count + 1),
-        scratch_shapes=[pltpu.VMEM(columns.shape, jnp.float32)] + tables,
+        out_specs=[vmem] * high_count + [pl.BlockSpec(memory_space=pltpu.HBM)],
+        scratch_shapes=[pltpu.VMEM(columns.shape, jnp.float32)]
+        + tables
+        + [pltpu.VMEM((senders, 1, box_lanes), jnp.float32), pltpu.SemaphoreType.DMA],
         compiler_params=params,
         name="sum_last",
     )(*arrived[LOW // 2 :], *first_sums)

time: 43.5 us -> 43.4 us (level)
  transfers between devices with their start and end apart: 10 -> 10, of which waited for: 5 -> 5; matrix products, arithmetic and copies ran while one was open for 0% -> 0% of each run, Pallas kernels for 4% -> 5%
where the time goes in v6:
time: 43.4 us; the launch traced here: 43.2 us
  starting transfers between devices  21.7 us (50%)
  waiting for transfers between devices  14.1 us (32%)
  Pallas kernels  6.07 us (14%)
  between operations  0.72 us (2%)
  other arithmetic  0.64 us (1%)
    ppermute x9, starting transfers between devices, moved(): lax.ppermute(value, 'basis', [(i, i ^ bits) for i in range(basis_count)])  17.5 us
    ppermute x9, waiting for transfers between devices, moved(): lax.ppermute(value, 'basis', [(i, i ^ bits) for i in range(basis_count)])  12 us
    all_to_all x1, starting transfers between devices, on_device(): gathered = lax.all_to_all(grad, everyone, split_axis=0, concat_axis=0)  4.24 us
    pallas_call x1, Pallas kernels, on_device(): pl.pallas_call(functools.partial(fill_kernel, slots), out_shape=[message]...  2.67 us
    all_to_all x1, waiting for transfers between devices, on_device(): gathered = lax.all_to_all(grad, everyone, split_axis=0, concat_axis=0)  2.03 us
    pallas_call x1, Pallas kernels, on_device(): pl.pallas_call(functools.partial(sum_last_kernel, slots, high_count, bloc...  1.43 us
    pallas_call x1, Pallas kernels, on_device(): pl.pallas_call(functools.partial(sum_first_kernel, slots, high_count), ou...  1 us
    pallas_call x1, Pallas kernels, on_device(): pl.pallas_call(functools.partial(update_kernel, angles, norm_far, high_co...  0.97 us
  transfers between devices with their start and end apart: 10, of which 5 were waited for; matrix products, arithmetic and copies ran while one was open for 0% of the time, Pallas kernels for 5%

profile of v6, /device:TPU:0, one launch (start us, length us, event | category | flops | bytes accessed | tf_op | source)
XLA Modules:
  0.0 43.2 jit_solution(14864224801554028907)
XLA Ops:
  0.6 0.0 copy-start
  0.6 0.0 copy-start.1
  0.7 0.0 copy-start.2
  0.7 2.7 %fill.1 = (f32[776,128]{1,0:T(8,128)S(1)}, f32[776,128]{1,0:T(8,128)S(1)}, f32[776,128]{1,0:T(8,128)S(1)}, f32[776,128]{1,0:T(8,128)S(1)}, f32[8,32,128]{2,1,0:T(8,128)S(1)}) custom-call(s32[8,6]{1,0:T(8,128)} %refs_0_.1, s32[8,6]{1,0:T(8,128)} %refs_1_.1, s32[8]{0:T(128)} %refs_2_.1, f32[8,6]{1,0:T(8,128)} %refs_3_.1, f32[256,128]{1,0:T(8,128)} %bitcast.6, ...), custom_call_target="tpu_custom_call" | custom-call | tf_op jit(solution)/shard_map/fill/pallas_call | solution.py:266
  3.3 3.0 %collective-permute-start.2 = (f32[776,128]{1,0:T(8,128)S(1)}, f32[776,128]{1,0:T(8,128)S(1)}, u32[]{:S(2)}, u32[]{:S(2)}) collective-permute-start(f32[776,128]{1,0:T(8,128)S(1)} %get-tuple-element.21), channel_id=1, source_target_pairs={{0,2},{2,0},{4,6},{6,4},{8,10},{10,8},{12,14},{14,12},{16,18},{18,... | collective-permute-start | bytes 1191944 | tf_op jit(solution)/shard_map/ppermute | solution.py:246
  6.3 1.5 %collective-permute-start = (f32[776,128]{1,0:T(8,128)S(1)}, f32[776,128]{1,0:T(8,128)S(1)}, u32[]{:S(2)}, u32[]{:S(2)}) collective-permute-start(f32[776,128]{1,0:T(8,128)S(1)} %get-tuple-element.18), channel_id=1, source_target_pairs={{0,4},{2,6},{4,0},{6,2},{8,12},{10,14},{12,8},{14,10},{16,20},{18,... | collective-permute-start | bytes 1191944 | tf_op jit(solution)/shard_map/ppermute | solution.py:246
  7.9 0.0 collective-permute-start.1
  7.9 2.0 %collective-permute-start.3 = (f32[8,32,128]{2,1,0:T(8,128)S(1)}, f32[8,32,128]{2,1,0:T(8,128)S(1)}, u32[]{:S(2)}, u32[]{:S(2)}) collective-permute-start(f32[8,32,128]{2,1,0:T(8,128)S(1)} %get-tuple-element.22.refs_2_), channel_id=1, source_target_pairs={{0,8},{2,10},{4,12},{6,14},{8,0},{10,2},{12,4},{14,6},{16,24},{18,... | collective-permute-start | bytes 393224 | tf_op jit(solution)/shard_map/ppermute | solution.py:246
  9.9 2.6 %collective-permute-start.4 = (f32[8,32,128]{2,1,0:T(8,128)S(1)}, f32[8,32,128]{2,1,0:T(8,128)S(1)}, u32[]{:S(2)}, u32[]{:S(2)}) collective-permute-start(f32[8,32,128]{2,1,0:T(8,128)S(1)} %get-tuple-element.22.refs_2_), channel_id=1, source_target_pairs={{0,16},{2,18},{4,20},{6,22},{8,24},{10,26},{12,28},{14,30},{16,0},... | collective-permute-start | bytes 393224 | tf_op jit(solution)/shard_map/ppermute | solution.py:246
  12.5 1.6 %collective-permute-done.3.refs_3_ = f32[8,32,128]{2,1,0:T(8,128)S(1)} collective-permute-done((f32[8,32,128]{2,1,0:T(8,128)S(1)}, f32[8,32,128]{2,1,0:T(8,128)S(1)}, u32[]{:S(2)}, u32[]{:S(2)}) %collective-permute-start.3) | collective-permute-done | bytes 131104 | tf_op jit(solution)/shard_map/ppermute | solution.py:246
  14.2 4.1 %collective-permute-start.5 = (f32[8,32,128]{2,1,0:T(8,128)S(1)}, f32[8,32,128]{2,1,0:T(8,128)S(1)}, u32[]{:S(2)}, u32[]{:S(2)}) collective-permute-start(f32[8,32,128]{2,1,0:T(8,128)S(1)} %get-tuple-element.22.refs_2_), channel_id=1, source_target_pairs={{0,24},{2,26},{4,28},{6,30},{8,16},{10,18},{12,20},{14,22},{16,8},... | collective-permute-start | bytes 393224 | tf_op jit(solution)/shard_map/ppermute | solution.py:246
  18.2 3.4 %collective-permute-done.4.refs_4_ = f32[8,32,128]{2,1,0:T(8,128)S(1)} collective-permute-done((f32[8,32,128]{2,1,0:T(8,128)S(1)}, f32[8,32,128]{2,1,0:T(8,128)S(1)}, u32[]{:S(2)}, u32[]{:S(2)}) %collective-permute-start.4) | collective-permute-done | bytes 131104 | tf_op jit(solution)/shard_map/ppermute | solution.py:246
  21.7 0.0 collective-permute-done.5.refs_5_
  21.7 0.0 collective-permute-done.2.refs_1_
  21.7 1.0 %sum_first.1 = (f32[32,32,128]{2,1,0:T(8,128)S(1)}, f32[32,32,128]{2,1,0:T(8,128)S(1)}, f32[8,128]{1,0:T(8,128)S(1)}, f32[8,128]{1,0:T(8,128)S(1)}) custom-call(f32[776,128]{1,0:T(8,128)S(1)} %get-tuple-element.20.refs_0_, f32[776,128]{1,0:T(8,128)S(1)} %collective-permute-done.2.refs_1_, f32[8,32,128]{2,1,0:T(8,128)S(1)} %get-tuple-element.22.refs_2_, ...), custom_call_target="tpu_custom_call" | custom-call | tf_op jit(solution)/shard_map/sum_first/pallas_call | solution.py:289
  22.7 2.8 %collective-permute-done.refs_0_ = f32[776,128]{1,0:T(8,128)S(1)} collective-permute-done((f32[776,128]{1,0:T(8,128)S(1)}, f32[776,128]{1,0:T(8,128)S(1)}, u32[]{:S(2)}, u32[]{:S(2)}) %collective-permute-start) | collective-permute-done | bytes 397344 | tf_op jit(solution)/shard_map/ppermute | solution.py:246
  25.5 0.0 collective-permute-done.1.refs_1_
  25.5 1.4 %sum_last.1 = (f32[264,128]{1,0:T(8,128)S(1)}, f32[264,128]{1,0:T(8,128)S(1)}, f32[272,128]{1,0:T(8,128)S(1)}, f32[272,128]{1,0:T(8,128)S(1)}, f32[32,1,128]{2,1,0:T(1,128)}) custom-call(f32[776,128]{1,0:T(8,128)S(1)} %collective-permute-done.refs_0_, f32[776,128]{1,0:T(8,128)S(1)} %collective-permute-done.1.refs_1_, ...), custom_call_target="tpu_custom_call" | custom-call | tf_op jit(solution)/shard_map/sum_last/pallas_call | solution.py:301
  27.0 2.7 %collective-permute-start.7 = (f32[272,128]{1,0:T(8,128)S(1)}, f32[272,128]{1,0:T(8,128)S(1)}, u32[]{:S(2)}, u32[]{:S(2)}) collective-permute-start(f32[272,128]{1,0:T(8,128)S(1)} %get-tuple-element.30), channel_id=1, source_target_pairs={{0,16},{2,18},{4,20},{6,22},{8,24},{10,26},{12,28},{14,30},{16,0},... | collective-permute-start | bytes 417800 | tf_op jit(solution)/shard_map/ppermute | solution.py:246
  29.6 1.3 %collective-permute-start.8 = (f32[272,128]{1,0:T(8,128)S(1)}, f32[272,128]{1,0:T(8,128)S(1)}, u32[]{:S(2)}, u32[]{:S(2)}) collective-permute-start(f32[272,128]{1,0:T(8,128)S(1)} %get-tuple-element.31), channel_id=1, source_target_pairs={{0,24},{2,26},{4,28},{6,30},{8,16},{10,18},{12,20},{14,22},{16,8},... | collective-permute-start | bytes 417800 | tf_op jit(solution)/shard_map/ppermute | solution.py:246
  31.0 0.2 collective-permute-start.6
  31.2 4.2 %all-to-all-start = ((f32[32,1,128]{2,1,0:T(1,128)}), f32[32,1,128]{2,1,0:T(1,128)S(1)}, u32[]{:S(2)}, u32[]{:S(2)}) async-start(f32[32,1,128]{2,1,0:T(1,128)} %get-tuple-element.27), calls=%async_computation | async-start | bytes 32768 | tf_op jit(solution)/shard_map/all_to_all | solution.py:322
  35.4 4.1 %collective-permute-done.6.refs_1_ = f32[264,128]{1,0:T(8,128)S(1)} collective-permute-done((f32[264,128]{1,0:T(8,128)S(1)}, f32[264,128]{1,0:T(8,128)S(1)}, u32[]{:S(2)}, u32[]{:S(2)}) %collective-permute-start.6) | collective-permute-done | bytes 135200 | tf_op jit(solution)/shard_map/ppermute | solution.py:246
  39.5 0.0 collective-permute-done.7.refs_2_
  39.6 0.0 collective-permute-done.8.refs_3_
  39.6 0.0 copy-done
  39.6 0.0 copy-done.1
  39.6 0.0 copy-done.2
  39.6 1.0 %update.1 = f32[256,128]{1,0:T(8,128)} custom-call(f32[264,128]{1,0:T(8,128)S(1)} %get-tuple-element.28.refs_0_, f32[264,128]{1,0:T(8,128)S(1)} %collective-permute-done.6.refs_1_, f32[272,128]{1,0:T(8,128)S(1)} %collective-permute-done.7.refs_2_, f32[272,128]{1,0:T(8,128)S(1)} %collective-permute-done.8.refs_3_, f32[256,128]{1,0:T(8,128)S(1)} %bitcast.7, ...), custom_call_target="tpu_custom_call" | custom-call | tf_op jit(solution)/shard_map/update/pallas_call | solution.py:314
  40.6 2.0 %all-to-all-done = f32[32,1,128]{2,1,0:T(1,128)S(1)} async-done(((f32[32,1,128]{2,1,0:T(1,128)}), f32[32,1,128]{2,1,0:T(1,128)S(1)}, u32[]{:S(2)}, u32[]{:S(2)}) %all-to-all-start) | async-done | bytes 16416 | tf_op jit(solution)/shard_map/all_to_all | solution.py:322
  42.6 0.1 reduce_sum.9
  42.6 0.6 %dynamic-slice_multiply_fusion = f32[4]{0:T(128)} fusion(f32[128]{0:T(128)S(1)} %reduce_sum.9, s32[]{:T(128)S(6)} %select_n.3), kind=kLoop, calls=%fused_computation | loop fusion | flops 4 | bytes 36 | tf_op jit(solution)/shard_map/mul | solution.py:328
Async XLA Ops:
  0.6 38.9 %copy-start = (f32[1,16,8,2,128]{4,3,2,1,0:T(2,128)S(1)}, f32[1,16,8,2,128]{4,3,2,1,0:T(2,128)}, u32[]{:S(2)}) copy-start(f32[1,16,8,2,128]{4,3,2,1,0:T(2,128)} %param.9) | copy-start | bytes 393220
  0.6 38.9 %copy-start.1 = (f32[1,16,8,2,128]{4,3,2,1,0:T(2,128)S(1)}, f32[1,16,8,2,128]{4,3,2,1,0:T(2,128)}, u32[]{:S(2)}) copy-start(f32[1,16,8,2,128]{4,3,2,1,0:T(2,128)} %param.11) | copy-start | bytes 393220
  0.7 38.9 %copy-start.2 = (bf16[8,2,128,128]{3,2,1,0:T(8,128)(2,1)S(1)}, bf16[8,2,128,128]{3,2,1,0:T(8,128)(2,1)}, u32[]{:S(2)}) copy-start(bf16[8,2,128,128]{3,2,1,0:T(8,128)(2,1)} %param.13) | copy-start | bytes 1572868
  3.3 18.3 %collective-permute-start.2 = (f32[776,128]{1,0:T(8,128)S(1)}, f32[776,128]{1,0:T(8,128)S(1)}, u32[]{:S(2)}, u32[]{:S(2)}) collective-permute-start(f32[776,128]{1,0:T(8,128)S(1)} %get-tuple-element.21), channel_id=1, source_target_pairs={{0,2},{2,0},{4,6},{6,4},{8,10},{10,8},{12,14},{14,12},{16,18},{18,... | collective-permute-start | bytes 1191944 | tf_op jit(solution)/shard_map/ppermute | solution.py:246
  6.3 19.2 %collective-permute-start = (f32[776,128]{1,0:T(8,128)S(1)}, f32[776,128]{1,0:T(8,128)S(1)}, u32[]{:S(2)}, u32[]{:S(2)}) collective-permute-start(f32[776,128]{1,0:T(8,128)S(1)} %get-tuple-element.18), channel_id=1, source_target_pairs={{0,4},{2,6},{4,0},{6,2},{8,12},{10,14},{12,8},{14,10},{16,20},{18,... | collective-permute-start | bytes 1191944 | tf_op jit(solution)/shard_map/ppermute | solution.py:246
  7.9 17.7 %collective-permute-start.1 = (f32[776,128]{1,0:T(8,128)S(1)}, f32[776,128]{1,0:T(8,128)S(1)}, u32[]{:S(2)}, u32[]{:S(2)}) collective-permute-start(f32[776,128]{1,0:T(8,128)S(1)} %get-tuple-element.19), channel_id=1, source_target_pairs={{0,6},{2,4},{4,2},{6,0},{8,14},{10,12},{12,10},{14,8},{16,22},{18,... | collective-permute-start | bytes 1191944 | tf_op jit(solution)/shard_map/ppermute | solution.py:246
  7.9 6.3 %collective-permute-start.3 = (f32[8,32,128]{2,1,0:T(8,128)S(1)}, f32[8,32,128]{2,1,0:T(8,128)S(1)}, u32[]{:S(2)}, u32[]{:S(2)}) collective-permute-start(f32[8,32,128]{2,1,0:T(8,128)S(1)} %get-tuple-element.22.refs_2_), channel_id=1, source_target_pairs={{0,8},{2,10},{4,12},{6,14},{8,0},{10,2},{12,4},{14,6},{16,24},{18,... | collective-permute-start | bytes 393224 | tf_op jit(solution)/shard_map/ppermute | solution.py:246
  9.9 11.7 %collective-permute-start.4 = (f32[8,32,128]{2,1,0:T(8,128)S(1)}, f32[8,32,128]{2,1,0:T(8,128)S(1)}, u32[]{:S(2)}, u32[]{:S(2)}) collective-permute-start(f32[8,32,128]{2,1,0:T(8,128)S(1)} %get-tuple-element.22.refs_2_), channel_id=1, source_target_pairs={{0,16},{2,18},{4,20},{6,22},{8,24},{10,26},{12,28},{14,30},{16,0},... | collective-permute-start | bytes 393224 | tf_op jit(solution)/shard_map/ppermute | solution.py:246
  14.2 7.5 %collective-permute-start.5 = (f32[8,32,128]{2,1,0:T(8,128)S(1)}, f32[8,32,128]{2,1,0:T(8,128)S(1)}, u32[]{:S(2)}, u32[]{:S(2)}) collective-permute-start(f32[8,32,128]{2,1,0:T(8,128)S(1)} %get-tuple-element.22.refs_2_), channel_id=1, source_target_pairs={{0,24},{2,26},{4,28},{6,30},{8,16},{10,18},{12,20},{14,22},{16,8},... | collective-permute-start | bytes 393224 | tf_op jit(solution)/shard_map/ppermute | solution.py:246
  27.0 12.6 %collective-permute-start.7 = (f32[272,128]{1,0:T(8,128)S(1)}, f32[272,128]{1,0:T(8,128)S(1)}, u32[]{:S(2)}, u32[]{:S(2)}) collective-permute-start(f32[272,128]{1,0:T(8,128)S(1)} %get-tuple-element.30), channel_id=1, source_target_pairs={{0,16},{2,18},{4,20},{6,22},{8,24},{10,26},{12,28},{14,30},{16,0},... | collective-permute-start | bytes 417800 | tf_op jit(solution)/shard_map/ppermute | solution.py:246
  29.6 9.9 %collective-permute-start.8 = (f32[272,128]{1,0:T(8,128)S(1)}, f32[272,128]{1,0:T(8,128)S(1)}, u32[]{:S(2)}, u32[]{:S(2)}) collective-permute-start(f32[272,128]{1,0:T(8,128)S(1)} %get-tuple-element.31), channel_id=1, source_target_pairs={{0,24},{2,26},{4,28},{6,30},{8,16},{10,18},{12,20},{14,22},{16,8},... | collective-permute-start | bytes 417800 | tf_op jit(solution)/shard_map/ppermute | solution.py:246
  31.0 8.6 %collective-permute-start.6 = (f32[264,128]{1,0:T(8,128)S(1)}, f32[264,128]{1,0:T(8,128)S(1)}, u32[]{:S(2)}, u32[]{:S(2)}) collective-permute-start(f32[264,128]{1,0:T(8,128)S(1)} %get-tuple-element.29), channel_id=1, source_target_pairs={{0,8},{2,10},{4,12},{6,14},{8,0},{10,2},{12,4},{14,6},{16,24},{18,... | collective-permute-start | bytes 405512 | tf_op jit(solution)/shard_map/ppermute | solution.py:246
  31.2 11.4 %all-to-all-start = ((f32[32,1,128]{2,1,0:T(1,128)}), f32[32,1,128]{2,1,0:T(1,128)S(1)}, u32[]{:S(2)}, u32[]{:S(2)}) async-start(f32[32,1,128]{2,1,0:T(1,128)} %get-tuple-element.27), calls=%async_computation | async-start | bytes 32768 | tf_op jit(solution)/shard_map/all_to_all | solution.py:322

commit v7 on v6

--- a/solution.py
+++ b/solution.py
@@ -164,7 +164,7 @@
     extra_ref[...] = extra
 
 
-def sum_last_kernel(slots, high_count, blocks, *refs):
+def sum_last_kernel(slots, high_count, blocks, norm_shape, *refs):
     message_refs, refs = refs[: LOW // 2], refs[LOW // 2 :]
     (first_ref, cur_ref, first_extra_ref, first_share_ref), refs = refs[:4], refs[4:]
     out_refs, (whole_grad_ref, acc_ref, *refs) = refs[:high_count], refs[high_count:]
@@ -176,7 +176,7 @@
     share = box_shares(
         message_refs, LOW // 2, slots, grad_ref.shape[2], extra, cur_ref, prod_ref, place_ref, copy
     )
-    box_sums = jnp.sum(share + first_share_ref[...], axis=0, keepdims=True)
+    box_sums = jnp.sum(share + first_share_ref[...], axis=0, keepdims=True) * norm_shape
     grad_ref[...] = jnp.broadcast_to(box_sums[None], grad_ref.shape)
     copy = pltpu.make_async_copy(grad_ref, whole_grad_ref, grad_sem)
     copy.start()
@@ -298,8 +298,9 @@
     partials = [f32((blocks * record + 8 * (1 + min(d // 2, 1)), unknowns)) for d in range(high_count)]
     everyone = ("basis", "pol")
     senders = basis_count * lax.axis_size("pol")
+    norm_shape = -1.0 / math.sqrt(4 * unknowns * angles_all * near_count)
     *sums, grad = pl.pallas_call(
-        functools.partial(sum_last_kernel, slots, high_count, blocks),
+        functools.partial(sum_last_kernel, slots, high_count, blocks, norm_shape),
         out_shape=partials + [f32((senders, 1, box_lanes))],
         in_specs=[vmem] * (LOW // 2 + 4),
         out_specs=[vmem] * high_count + [pl.BlockSpec(memory_space=pltpu.HBM)],
@@ -321,12 +322,11 @@
     )(*totals, adjoint_rows, radiation_rows, inverse)
     gathered = lax.all_to_all(grad, everyone, split_axis=0, concat_axis=0)
     gathered, updated = lax.optimization_barrier((gathered, updated))
-    total_grad = jnp.sum(gathered[:, 0], axis=0)
+    mine = lax.dynamic_slice_in_dim(gathered, lax.axis_index("basis") * BOX_DEV, BOX_DEV, axis=2)
+    share = jnp.sum(mine[:, 0], axis=0)
     if lax.axis_size("angle") > 1:
-        total_grad = lax.psum(total_grad, "angle")
-    share = lax.dynamic_slice_in_dim(total_grad, lax.axis_index("basis") * BOX_DEV, BOX_DEV)
-    shape_grad = share * (-1.0 / math.sqrt(4 * unknowns * angles_all * near_count))
-    return (updated.reshape(adjoint.shape), shape_grad)
+        share = lax.psum(share, "angle")
+    return (updated.reshape(adjoint.shape), share)
 
 
 def solution(mesh):

time: 43.4 us -> 43.4 us (level)
    mul x1 -> x0, other arithmetic: 0.59 us -> none  [on_device(): share * (-1.0 / math.sqrt(4 * unknowns * angles_all * near_count))]
    reduce_sum x1, other arithmetic: 0.05 us -> 0.63 us  [on_device(): share = jnp.sum(mine[:, 0], axis=0)]
where the time goes in v7:
time: 43.4 us; the launch traced here: 43.2 us
  starting transfers between devices  21.7 us (50%)
  waiting for transfers between devices  14.1 us (32%)
  Pallas kernels  6.07 us (14%)
  between operations  0.72 us (2%)
  other arithmetic  0.63 us (1%)
    ppermute x9, starting transfers between devices, moved(): lax.ppermute(value, 'basis', [(i, i ^ bits) for i in range(basis_count)])  17.5 us
    ppermute x9, waiting for transfers between devices, moved(): lax.ppermute(value, 'basis', [(i, i ^ bits) for i in range(basis_count)])  12 us
    all_to_all x1, starting transfers between devices, on_device(): gathered = lax.all_to_all(grad, everyone, split_axis=0, concat_axis=0)  4.23 us
    pallas_call x1, Pallas kernels, on_device(): pl.pallas_call(functools.partial(fill_kernel, slots), out_shape=[message]...  2.67 us
    all_to_all x1, waiting for transfers between devices, on_device(): gathered = lax.all_to_all(grad, everyone, split_axis=0, concat_axis=0)  2.03 us
    pallas_call x1, Pallas kernels, on_device(): pl.pallas_call(functools.partial(sum_last_kernel, slots, high_count, bloc...  1.43 us
    pallas_call x1, Pallas kernels, on_device(): pl.pallas_call(functools.partial(sum_first_kernel, slots, high_count), ou...  1.01 us
    pallas_call x1, Pallas kernels, on_device(): pl.pallas_call(functools.partial(update_kernel, angles, norm_far, high_co...  0.97 us
  transfers between devices with their start and end apart: 10, of which 5 were waited for; matrix products, arithmetic and copies ran while one was open for 0% of the time, Pallas kernels for 5%

profile of v7, /device:TPU:0, one launch (start us, length us, event | category | flops | bytes accessed | tf_op | source)
XLA Modules:
  0.0 43.2 jit_solution(16197824155542296625)
XLA Ops:
  0.6 0.0 copy-start
  0.6 0.0 copy-start.1
  0.7 0.0 copy-start.2
  0.7 2.7 %fill.1 = (f32[776,128]{1,0:T(8,128)S(1)}, f32[776,128]{1,0:T(8,128)S(1)}, f32[776,128]{1,0:T(8,128)S(1)}, f32[776,128]{1,0:T(8,128)S(1)}, f32[8,32,128]{2,1,0:T(8,128)S(1)}) custom-call(s32[8,6]{1,0:T(8,128)} %refs_0_.1, s32[8,6]{1,0:T(8,128)} %refs_1_.1, s32[8]{0:T(128)} %refs_2_.1, f32[8,6]{1,0:T(8,128)} %refs_3_.1, f32[256,128]{1,0:T(8,128)} %bitcast.6, ...), custom_call_target="tpu_custom_call" | custom-call | tf_op jit(solution)/shard_map/fill/pallas_call | solution.py:266
  3.3 3.0 %collective-permute-start.2 = (f32[776,128]{1,0:T(8,128)S(1)}, f32[776,128]{1,0:T(8,128)S(1)}, u32[]{:S(2)}, u32[]{:S(2)}) collective-permute-start(f32[776,128]{1,0:T(8,128)S(1)} %get-tuple-element.21), channel_id=1, source_target_pairs={{0,2},{2,0},{4,6},{6,4},{8,10},{10,8},{12,14},{14,12},{16,18},{18,... | collective-permute-start | bytes 1191944 | tf_op jit(solution)/shard_map/ppermute | solution.py:246
  6.3 1.5 %collective-permute-start = (f32[776,128]{1,0:T(8,128)S(1)}, f32[776,128]{1,0:T(8,128)S(1)}, u32[]{:S(2)}, u32[]{:S(2)}) collective-permute-start(f32[776,128]{1,0:T(8,128)S(1)} %get-tuple-element.18), channel_id=1, source_target_pairs={{0,4},{2,6},{4,0},{6,2},{8,12},{10,14},{12,8},{14,10},{16,20},{18,... | collective-permute-start | bytes 1191944 | tf_op jit(solution)/shard_map/ppermute | solution.py:246
  7.9 0.0 collective-permute-start.1
  7.9 2.0 %collective-permute-start.3 = (f32[8,32,128]{2,1,0:T(8,128)S(1)}, f32[8,32,128]{2,1,0:T(8,128)S(1)}, u32[]{:S(2)}, u32[]{:S(2)}) collective-permute-start(f32[8,32,128]{2,1,0:T(8,128)S(1)} %get-tuple-element.22.refs_2_), channel_id=1, source_target_pairs={{0,8},{2,10},{4,12},{6,14},{8,0},{10,2},{12,4},{14,6},{16,24},{18,... | collective-permute-start | bytes 393224 | tf_op jit(solution)/shard_map/ppermute | solution.py:246
  9.9 2.6 %collective-permute-start.4 = (f32[8,32,128]{2,1,0:T(8,128)S(1)}, f32[8,32,128]{2,1,0:T(8,128)S(1)}, u32[]{:S(2)}, u32[]{:S(2)}) collective-permute-start(f32[8,32,128]{2,1,0:T(8,128)S(1)} %get-tuple-element.22.refs_2_), channel_id=1, source_target_pairs={{0,16},{2,18},{4,20},{6,22},{8,24},{10,26},{12,28},{14,30},{16,0},... | collective-permute-start | bytes 393224 | tf_op jit(solution)/shard_map/ppermute | solution.py:246
  12.5 1.6 %collective-permute-done.3.refs_3_ = f32[8,32,128]{2,1,0:T(8,128)S(1)} collective-permute-done((f32[8,32,128]{2,1,0:T(8,128)S(1)}, f32[8,32,128]{2,1,0:T(8,128)S(1)}, u32[]{:S(2)}, u32[]{:S(2)}) %collective-permute-start.3) | collective-permute-done | bytes 131104 | tf_op jit(solution)/shard_map/ppermute | solution.py:246
  14.2 4.1 %collective-permute-start.5 = (f32[8,32,128]{2,1,0:T(8,128)S(1)}, f32[8,32,128]{2,1,0:T(8,128)S(1)}, u32[]{:S(2)}, u32[]{:S(2)}) collective-permute-start(f32[8,32,128]{2,1,0:T(8,128)S(1)} %get-tuple-element.22.refs_2_), channel_id=1, source_target_pairs={{0,24},{2,26},{4,28},{6,30},{8,16},{10,18},{12,20},{14,22},{16,8},... | collective-permute-start | bytes 393224 | tf_op jit(solution)/shard_map/ppermute | solution.py:246
  18.2 3.4 %collective-permute-done.4.refs_4_ = f32[8,32,128]{2,1,0:T(8,128)S(1)} collective-permute-done((f32[8,32,128]{2,1,0:T(8,128)S(1)}, f32[8,32,128]{2,1,0:T(8,128)S(1)}, u32[]{:S(2)}, u32[]{:S(2)}) %collective-permute-start.4) | collective-permute-done | bytes 131104 | tf_op jit(solution)/shard_map/ppermute | solution.py:246
  21.7 0.0 collective-permute-done.5.refs_5_
  21.7 0.0 collective-permute-done.2.refs_1_
  21.7 1.0 %sum_first.1 = (f32[32,32,128]{2,1,0:T(8,128)S(1)}, f32[32,32,128]{2,1,0:T(8,128)S(1)}, f32[8,128]{1,0:T(8,128)S(1)}, f32[8,128]{1,0:T(8,128)S(1)}) custom-call(f32[776,128]{1,0:T(8,128)S(1)} %get-tuple-element.20.refs_0_, f32[776,128]{1,0:T(8,128)S(1)} %collective-permute-done.2.refs_1_, f32[8,32,128]{2,1,0:T(8,128)S(1)} %get-tuple-element.22.refs_2_, ...), custom_call_target="tpu_custom_call" | custom-call | tf_op jit(solution)/shard_map/sum_first/pallas_call | solution.py:289
  22.7 2.8 %collective-permute-done.refs_0_ = f32[776,128]{1,0:T(8,128)S(1)} collective-permute-done((f32[776,128]{1,0:T(8,128)S(1)}, f32[776,128]{1,0:T(8,128)S(1)}, u32[]{:S(2)}, u32[]{:S(2)}) %collective-permute-start) | collective-permute-done | bytes 397344 | tf_op jit(solution)/shard_map/ppermute | solution.py:246
  25.5 0.0 collective-permute-done.1.refs_1_
  25.5 1.4 %sum_last.1 = (f32[264,128]{1,0:T(8,128)S(1)}, f32[264,128]{1,0:T(8,128)S(1)}, f32[272,128]{1,0:T(8,128)S(1)}, f32[272,128]{1,0:T(8,128)S(1)}, f32[32,1,128]{2,1,0:T(1,128)}) custom-call(f32[776,128]{1,0:T(8,128)S(1)} %collective-permute-done.refs_0_, f32[776,128]{1,0:T(8,128)S(1)} %collective-permute-done.1.refs_1_, ...), custom_call_target="tpu_custom_call" | custom-call | tf_op jit(solution)/shard_map/sum_last/pallas_call | solution.py:302
  27.0 2.7 %collective-permute-start.7 = (f32[272,128]{1,0:T(8,128)S(1)}, f32[272,128]{1,0:T(8,128)S(1)}, u32[]{:S(2)}, u32[]{:S(2)}) collective-permute-start(f32[272,128]{1,0:T(8,128)S(1)} %get-tuple-element.30), channel_id=1, source_target_pairs={{0,16},{2,18},{4,20},{6,22},{8,24},{10,26},{12,28},{14,30},{16,0},... | collective-permute-start | bytes 417800 | tf_op jit(solution)/shard_map/ppermute | solution.py:246
  29.6 1.3 %collective-permute-start.8 = (f32[272,128]{1,0:T(8,128)S(1)}, f32[272,128]{1,0:T(8,128)S(1)}, u32[]{:S(2)}, u32[]{:S(2)}) collective-permute-start(f32[272,128]{1,0:T(8,128)S(1)} %get-tuple-element.31), channel_id=1, source_target_pairs={{0,24},{2,26},{4,28},{6,30},{8,16},{10,18},{12,20},{14,22},{16,8},... | collective-permute-start | bytes 417800 | tf_op jit(solution)/shard_map/ppermute | solution.py:246
  31.0 0.2 collective-permute-start.6
  31.2 4.2 %all-to-all-start = ((f32[32,1,128]{2,1,0:T(1,128)}), f32[32,1,128]{2,1,0:T(1,128)S(1)}, u32[]{:S(2)}, u32[]{:S(2)}) async-start(f32[32,1,128]{2,1,0:T(1,128)} %get-tuple-element.27), calls=%async_computation | async-start | bytes 32768 | tf_op jit(solution)/shard_map/all_to_all | solution.py:323
  35.4 4.1 %collective-permute-done.6.refs_1_ = f32[264,128]{1,0:T(8,128)S(1)} collective-permute-done((f32[264,128]{1,0:T(8,128)S(1)}, f32[264,128]{1,0:T(8,128)S(1)}, u32[]{:S(2)}, u32[]{:S(2)}) %collective-permute-start.6) | collective-permute-done | bytes 135200 | tf_op jit(solution)/shard_map/ppermute | solution.py:246
  39.5 0.0 collective-permute-done.7.refs_2_
  39.6 0.0 collective-permute-done.8.refs_3_
  39.6 0.0 copy-done
  39.6 0.0 copy-done.1
  39.6 0.0 copy-done.2
  39.6 1.0 %update.1 = f32[256,128]{1,0:T(8,128)} custom-call(f32[264,128]{1,0:T(8,128)S(1)} %get-tuple-element.28.refs_0_, f32[264,128]{1,0:T(8,128)S(1)} %collective-permute-done.6.refs_1_, f32[272,128]{1,0:T(8,128)S(1)} %collective-permute-done.7.refs_2_, f32[272,128]{1,0:T(8,128)S(1)} %collective-permute-done.8.refs_3_, f32[256,128]{1,0:T(8,128)S(1)} %bitcast.7, ...), custom_call_target="tpu_custom_call" | custom-call | tf_op jit(solution)/shard_map/update/pallas_call | solution.py:315
  40.6 2.0 %all-to-all-done = f32[32,1,128]{2,1,0:T(1,128)S(1)} async-done(((f32[32,1,128]{2,1,0:T(1,128)}), f32[32,1,128]{2,1,0:T(1,128)S(1)}, u32[]{:S(2)}, u32[]{:S(2)}) %all-to-all-start) | async-done | bytes 16416 | tf_op jit(solution)/shard_map/all_to_all | solution.py:323
  42.6 0.6 %dynamic-slice_reduce_fusion = f32[4]{0:T(128)} fusion(f32[32,1,128]{2,1,0:T(1,128)S(1)} %all-to-all-done, s32[]{:T(128)S(6)} %select_n.3), kind=kLoop, calls=%fused_computation | loop fusion | flops 124 | bytes 532 | tf_op jit(solution)/shard_map/reduce_sum | solution.py:326
Async XLA Ops:
  0.6 38.9 %copy-start = (f32[1,16,8,2,128]{4,3,2,1,0:T(2,128)S(1)}, f32[1,16,8,2,128]{4,3,2,1,0:T(2,128)}, u32[]{:S(2)}) copy-start(f32[1,16,8,2,128]{4,3,2,1,0:T(2,128)} %param.9) | copy-start | bytes 393220
  0.6 38.9 %copy-start.1 = (f32[1,16,8,2,128]{4,3,2,1,0:T(2,128)S(1)}, f32[1,16,8,2,128]{4,3,2,1,0:T(2,128)}, u32[]{:S(2)}) copy-start(f32[1,16,8,2,128]{4,3,2,1,0:T(2,128)} %param.11) | copy-start | bytes 393220
  0.7 38.9 %copy-start.2 = (bf16[8,2,128,128]{3,2,1,0:T(8,128)(2,1)S(1)}, bf16[8,2,128,128]{3,2,1,0:T(8,128)(2,1)}, u32[]{:S(2)}) copy-start(bf16[8,2,128,128]{3,2,1,0:T(8,128)(2,1)} %param.13) | copy-start | bytes 1572868
  3.3 18.3 %collective-permute-start.2 = (f32[776,128]{1,0:T(8,128)S(1)}, f32[776,128]{1,0:T(8,128)S(1)}, u32[]{:S(2)}, u32[]{:S(2)}) collective-permute-start(f32[776,128]{1,0:T(8,128)S(1)} %get-tuple-element.21), channel_id=1, source_target_pairs={{0,2},{2,0},{4,6},{6,4},{8,10},{10,8},{12,14},{14,12},{16,18},{18,... | collective-permute-start | bytes 1191944 | tf_op jit(solution)/shard_map/ppermute | solution.py:246
  6.3 19.2 %collective-permute-start = (f32[776,128]{1,0:T(8,128)S(1)}, f32[776,128]{1,0:T(8,128)S(1)}, u32[]{:S(2)}, u32[]{:S(2)}) collective-permute-start(f32[776,128]{1,0:T(8,128)S(1)} %get-tuple-element.18), channel_id=1, source_target_pairs={{0,4},{2,6},{4,0},{6,2},{8,12},{10,14},{12,8},{14,10},{16,20},{18,... | collective-permute-start | bytes 1191944 | tf_op jit(solution)/shard_map/ppermute | solution.py:246
  7.9 17.7 %collective-permute-start.1 = (f32[776,128]{1,0:T(8,128)S(1)}, f32[776,128]{1,0:T(8,128)S(1)}, u32[]{:S(2)}, u32[]{:S(2)}) collective-permute-start(f32[776,128]{1,0:T(8,128)S(1)} %get-tuple-element.19), channel_id=1, source_target_pairs={{0,6},{2,4},{4,2},{6,0},{8,14},{10,12},{12,10},{14,8},{16,22},{18,... | collective-permute-start | bytes 1191944 | tf_op jit(solution)/shard_map/ppermute | solution.py:246
  7.9 6.3 %collective-permute-start.3 = (f32[8,32,128]{2,1,0:T(8,128)S(1)}, f32[8,32,128]{2,1,0:T(8,128)S(1)}, u32[]{:S(2)}, u32[]{:S(2)}) collective-permute-start(f32[8,32,128]{2,1,0:T(8,128)S(1)} %get-tuple-element.22.refs_2_), channel_id=1, source_target_pairs={{0,8},{2,10},{4,12},{6,14},{8,0},{10,2},{12,4},{14,6},{16,24},{18,... | collective-permute-start | bytes 393224 | tf_op jit(solution)/shard_map/ppermute | solution.py:246
  9.9 11.7 %collective-permute-start.4 = (f32[8,32,128]{2,1,0:T(8,128)S(1)}, f32[8,32,128]{2,1,0:T(8,128)S(1)}, u32[]{:S(2)}, u32[]{:S(2)}) collective-permute-start(f32[8,32,128]{2,1,0:T(8,128)S(1)} %get-tuple-element.22.refs_2_), channel_id=1, source_target_pairs={{0,16},{2,18},{4,20},{6,22},{8,24},{10,26},{12,28},{14,30},{16,0},... | collective-permute-start | bytes 393224 | tf_op jit(solution)/shard_map/ppermute | solution.py:246
  14.2 7.5 %collective-permute-start.5 = (f32[8,32,128]{2,1,0:T(8,128)S(1)}, f32[8,32,128]{2,1,0:T(8,128)S(1)}, u32[]{:S(2)}, u32[]{:S(2)}) collective-permute-start(f32[8,32,128]{2,1,0:T(8,128)S(1)} %get-tuple-element.22.refs_2_), channel_id=1, source_target_pairs={{0,24},{2,26},{4,28},{6,30},{8,16},{10,18},{12,20},{14,22},{16,8},... | collective-permute-start | bytes 393224 | tf_op jit(solution)/shard_map/ppermute | solution.py:246
  27.0 12.6 %collective-permute-start.7 = (f32[272,128]{1,0:T(8,128)S(1)}, f32[272,128]{1,0:T(8,128)S(1)}, u32[]{:S(2)}, u32[]{:S(2)}) collective-permute-start(f32[272,128]{1,0:T(8,128)S(1)} %get-tuple-element.30), channel_id=1, source_target_pairs={{0,16},{2,18},{4,20},{6,22},{8,24},{10,26},{12,28},{14,30},{16,0},... | collective-permute-start | bytes 417800 | tf_op jit(solution)/shard_map/ppermute | solution.py:246
  29.6 9.9 %collective-permute-start.8 = (f32[272,128]{1,0:T(8,128)S(1)}, f32[272,128]{1,0:T(8,128)S(1)}, u32[]{:S(2)}, u32[]{:S(2)}) collective-permute-start(f32[272,128]{1,0:T(8,128)S(1)} %get-tuple-element.31), channel_id=1, source_target_pairs={{0,24},{2,26},{4,28},{6,30},{8,16},{10,18},{12,20},{14,22},{16,8},... | collective-permute-start | bytes 417800 | tf_op jit(solution)/shard_map/ppermute | solution.py:246
  31.0 8.6 %collective-permute-start.6 = (f32[264,128]{1,0:T(8,128)S(1)}, f32[264,128]{1,0:T(8,128)S(1)}, u32[]{:S(2)}, u32[]{:S(2)}) collective-permute-start(f32[264,128]{1,0:T(8,128)S(1)} %get-tuple-element.29), channel_id=1, source_target_pairs={{0,8},{2,10},{4,12},{6,14},{8,0},{10,2},{12,4},{14,6},{16,24},{18,... | collective-permute-start | bytes 405512 | tf_op jit(solution)/shard_map/ppermute | solution.py:246
  31.2 11.4 %all-to-all-start = ((f32[32,1,128]{2,1,0:T(1,128)}), f32[32,1,128]{2,1,0:T(1,128)S(1)}, u32[]{:S(2)}, u32[]{:S(2)}) async-start(f32[32,1,128]{2,1,0:T(1,128)} %get-tuple-element.27), calls=%async_computation | async-start | bytes 32768 | tf_op jit(solution)/shard_map/all_to_all | solution.py:323
